TPU v7x, 32 devices: a whole 2x2x4 slice. The times are simulated.
32 devices in a mesh: dp: 8 (over y, x, core), seq: 4 (over z).
Axes of the slice: x: 2, y: 2, z: 4, core: 2. Of those that a mesh axis runs over, the one named last changes fastest.
Arguments:
- tokens_in: bfloat16 [8, 2048, 1024], P('dp', 'seq'), may hold values from -6 to 6
- user_ids: int32 [8, 2048], P('dp'), may hold values from 0 to 3, never falling along the last dimension, each value on 1 to 1024 neighbouring positions
- w_in: bfloat16 [1024, 2048], replicated, may hold values from -0.1875 to 0.1875
- w_out: bfloat16 [512, 1024], replicated, may hold values from -0.25 to 0.25
- cotangent: bfloat16 [8, 2048, 1024], P('dp', 'seq'), may hold values from -6 to 6
Outputs:
- output: bfloat16 [8, 2048, 1024], P('dp', 'seq')
- grad_tokens: bfloat16 [8, 2048, 1024], P('dp', 'seq')
- grad_w_in: float32 [1024, 2048], P(('dp', 'seq'))
- grad_w_out: float32 [512, 1024], P(None, ('dp', 'seq'))
Inputs may be any that keep to these rules, and one draw needn't show every extreme that they name: `user_ids`: in each stream the user number never falls; each user holds 1 to 1024 consecutive events and some user holds exactly 1024.
All inputs are finite; a program needn't handle non-finite values.
Results may differ from a plain program's by a relative error of at most 0.015.
Values may be sent and summed in bfloat16 or wider, within the bound.
No kernel may reach another device: no remote copies, remote signals or barrier semaphores. Data moves between devices by JAX's collectives and lax.ppermute only.
A program may use at most 128 MiB of HBM per device.

v0:
```python
import functools
import math

import jax
import jax.numpy as jnp
from jax import lax
from jax.experimental import pallas as pl
from jax.experimental.pallas import tpu as pltpu
from jax.sharding import PartitionSpec as P

HEADS = 4
HD = 128
HALF_SCALE = 0.5 / math.sqrt(HD)
SCALE = 1.0 / math.sqrt(HD)
EPSILON = 1e-05
GRANT = 18 << 20
BF16 = jnp.bfloat16
F32 = jnp.float32
VMEM = pl.BlockSpec(memory_space=pltpu.VMEM)
SMEM = pl.BlockSpec(memory_space=pltpu.SMEM)


def shift(value, by):
    devices = lax.axis_size("seq")
    pairs = [(i, i + by) for i in range(devices) if 0 <= i + by < devices]
    return lax.ppermute(value, "seq", pairs)


def call(kernel, outs, args, specs=None, scratch=(), flops=0, nbytes=0, name=None, after=(), weight=8):
    first, last = len(args), len(args) + len(after)

    def body(*refs):
        kernel(*refs[:first], *refs[last:])

    return pl.pallas_call(
        body,
        grid=(1,),
        out_shape=outs,
        in_specs=(specs or [VMEM] * first) + [pl.BlockSpec(memory_space=pl.ANY)] * len(after),
        out_specs=jax.tree.map(lambda _: VMEM, outs),
        scratch_shapes=scratch,
        compiler_params=pltpu.CompilerParams(vmem_limit_bytes=GRANT),
        cost_estimate=pl.CostEstimate(
            flops=weight * flops, bytes_accessed=nbytes, transcendentals=0
        ),
        name=name,
    )(*args, *after)


def columns(rows, width, block):
    return pl.BlockSpec((rows, width), lambda i: (0, block))


def like(rows, width, kind):
    return jax.ShapeDtypeStruct((rows, width), kind)


def dot(a, b):
    return jnp.dot(a, b, preferred_element_type=F32)


def dot_nt(a, b):
    return lax.dot_general(a, b, (((1,), (1,)), ((), ())), preferred_element_type=F32)


def dot_tn(a, b):
    return lax.dot_general(a, b, (((0,), (0,)), ((), ())), preferred_element_type=F32)


def centred(values):
    center = values - jnp.mean(values, axis=-1, keepdims=True)
    inverse = lax.rsqrt(jnp.mean(center * center, axis=-1, keepdims=True) + EPSILON)
    return center * inverse, inverse


def back(scaled, inverse, upstream):
    return inverse * (
        upstream
        - jnp.mean(upstream, axis=-1, keepdims=True)
        - scaled * jnp.mean(upstream * scaled, axis=-1, keepdims=True)
    )


def silu_and_slope(half):
    bend = 1.0 + jnp.tanh(half)
    value = half * bend
    return value, 0.5 * (bend + value * (2.0 - bend))


def project_kernel(raw, blocks, x_ref, *refs):
    w_refs, refs = refs[:blocks], refs[blocks:]
    if raw == "send":
        refs, (normed_send, act_send) = refs[:-2], refs[-2:]
    if raw:
        normed_ref, refs = refs[0], refs[1:]
        normed_ref[...] = centred(x_ref[...].astype(F32))[0].astype(BF16)
    else:
        normed_ref = x_ref
    slope_ref, act_refs = refs[0], refs[1:]
    width = slope_ref.shape[1] // blocks
    for b in range(blocks):
        value, slope = silu_and_slope(0.5 * dot(normed_ref[...], w_refs[b][...]))
        act_refs[b][...] = value.astype(BF16)
        slope_ref[:, b * width : (b + 1) * width] = slope.astype(BF16)
    if raw == "send":
        normed_send[...] = normed_ref[...]
        act_send[...] = act_refs[0][...]


def project(x, w_in, blocks, raw, after=()):
    n, d = x.shape
    width = w_in.shape[1] // 4
    outs = [like(n, d, BF16)] if raw else []
    outs += [like(n, width * len(blocks), BF16)] + [like(n, width, BF16)] * len(blocks)
    outs += [like(n, d, BF16), like(n, width, BF16)] if raw == "send" else []
    return call(
        functools.partial(project_kernel, raw, len(blocks)),
        outs,
        [x] + [w_in] * len(blocks),
        [VMEM] + [columns(d, width, b) for b in blocks],
        flops=2 * n * d * width * len(blocks),
        nbytes=2 * n * d + 2 * d * width * len(blocks),
        name="project",
        after=after,
    )


def pair_loop(kind, chunks, later, earlier, place_ref, ids_ref, n, n_seq, body):
    step = n // 2
    if kind == "own":
        for c in reversed(chunks):
            rows = c * step
            body(slice(rows, rows + step), slice(0, rows + step), rows, c == chunks[-1])
        return
    q_block, k_block = place_ref[1] + later, place_ref[1] - earlier
    valid = (q_block < n_seq) & (k_block >= 0)
    q_start, k_start = jnp.minimum(q_block, n_seq - 1) * n, jnp.maximum(k_block, 0) * n
    crosses = valid & (ids_ref[0, q_start + chunks[0] * step] == ids_ref[0, k_start + n - 1])
    if kind == "near":
        rows = slice(chunks[0] * step, (chunks[-1] + 1) * step)
        pl.when(crosses)(lambda: body(rows, slice(0, n), None, False))
        return

    @pl.loop(0, 2 * len(chunks))
    def _(i):
        row = pl.multiple_of((chunks[0] + i // 2) * step, step)
        key = pl.multiple_of((i % 2) * step, step)
        shared = ids_ref[0, q_start + row] == ids_ref[0, k_start + key + step - 1]
        pl.when(valid & shared)(
            lambda: body(pl.ds(row, step), pl.ds(key, step), None, False)
        )


def extent(part):
    if isinstance(part, slice):
        return part.start, part.stop - part.start
    return part.start, part.size


def ids_of(ref, block, rows, n, n_seq, axis):
    first, size = extent(rows)
    start = pl.multiple_of(jnp.clip(block, 0, n_seq - 1) * n, n) + first
    start = pl.multiple_of(start, size) if not isinstance(first, int) else start
    return ref[pl.ds(start, size), :] if axis == 0 else ref[:, pl.ds(start, size)]


def forward_kernel(
    n_seq, kind, chunks, later, earlier, more, place_ref, ids_ref, row_ref, col_ref, q_ref, k_ref, v_ref, *refs
):
    refs = list(refs)
    add_ref = refs.pop(0) if more else None
    out_ref = refs.pop(0)
    if kind != "far":
        refs.pop(0)[...] = k_ref[...].T
    sum_ref = refs.pop(0) if refs else out_ref
    n = q_ref.shape[0]
    base = chunks[0] * (n // 2)
    me = place_ref[1]
    if more or kind != "own":
        sum_ref[...] = add_ref[...] if more else jnp.zeros_like(sum_ref)

    def part(rows, keys, offset, first):
        first_row, size = extent(rows)
        out = slice(first_row - base, first_row - base + size) if kind != "far" else slice(0, size)
        mask = ids_of(col_ref, me + later, rows, n, n_seq, 0) == ids_of(row_ref, me - earlier, keys, n, n_seq, 1)
        if offset is not None:
            mask &= lax.broadcasted_iota(jnp.int32, mask.shape, 1) <= offset + lax.broadcasted_iota(
                jnp.int32, mask.shape, 0
            )
        for h in range(HEADS):
            cols = slice(h * HD, (h + 1) * HD)
            half = dot_nt(q_ref[rows, cols], k_ref[keys, cols]) * HALF_SCALE
            weights = jnp.where(mask, half * (1.0 + jnp.tanh(half)), 0.0).astype(BF16)
            term = dot(weights, v_ref[keys, cols])
            sum_ref[out, cols] = term if kind == "own" and not more else sum_ref[out, cols] + term

    pair_loop(kind, chunks, later, earlier, place_ref, ids_ref, n, n_seq, part)
    if sum_ref is not out_ref:
        out_ref[...] = sum_ref[...].astype(out_ref.dtype)


def forward(users, kind, q, k, v, later=0, earlier=0, add=None, dtype=F32, chunks=(0, 1), after=()):
    n, width = q.shape
    args = [*users, q, k, v] + ([] if add is None else [add])
    return call(
        functools.partial(
            forward_kernel, lax.axis_size("seq"), kind, chunks, later, earlier, add is not None
        ),
        [like(n // 2 * len(chunks), width, dtype)] + ([] if kind == "far" else [like(width, n, BF16)]),
        args,
        [SMEM] * 2 + [VMEM] * (len(args) - 2),
        scratch=[] if dtype == F32 else [pltpu.VMEM((n // 2 * len(chunks), width), F32)],
        flops=2 * n * n * width * len(chunks),
        nbytes=10 * n * width,
        name="forward",
        after=after,
    )


def backward_kernel(
    n_seq, kind, chunks, later, earlier, halves, given, place_ref, ids_ref, row_ref, col_ref, q_ref, k_ref, kt_ref, v_ref, *refs
):
    refs = list(refs)
    g_refs = [refs.pop(0) for _ in range(max(halves, 1))]
    add_q_ref, add_k_ref, slope_q_ref, slope_k_ref = [refs.pop(0) if x else None for x in given]
    gq_ref, gk_ref = refs.pop(0), refs.pop(0)
    sum_q_ref = gq_ref if slope_q_ref is None else refs.pop(0)
    sum_k_ref = gk_ref if slope_k_ref is None else refs.pop(0)
    n, width = q_ref.shape
    g_ref = g_refs[0]
    if halves == 2:
        g_ref = refs.pop(0)
        g_ref[: n // 2, :] = g_refs[0][...]
        g_ref[n // 2 :, :] = g_refs[1][...]
    me = place_ref[1]
    added = 0 if add_q_ref is None else add_q_ref.shape[0]
    if added:
        sum_q_ref[:added, :] = add_q_ref[...]
    if added < sum_q_ref.shape[0]:
        sum_q_ref[added:, :] = jnp.zeros_like(sum_q_ref[added:, :])
    if kind != "own":
        sum_k_ref[...] = jnp.zeros_like(sum_k_ref) if add_k_ref is None else add_k_ref[...]

    def part(rows, keys, offset, first):
        mask = ids_of(col_ref, me - earlier, keys, n, n_seq, 0) == ids_of(row_ref, me + later, rows, n, n_seq, 1)
        if offset is not None:
            mask &= lax.broadcasted_iota(jnp.int32, mask.shape, 0) <= offset + lax.broadcasted_iota(
                jnp.int32, mask.shape, 1
            )
        for h in range(HEADS):
            cols = slice(h * HD, (h + 1) * HD)
            k_cols = slice(width + h * HD, width + (h + 1) * HD)
            g = g_ref[rows, cols]
            half = dot_nt(k_ref[keys, cols], q_ref[rows, cols]) * HALF_SCALE
            bend = jnp.where(mask, 1.0 + jnp.tanh(half), 0.0)
            value = half * bend
            weights = value.astype(BF16)
            grads = (dot_nt(v_ref[keys, cols], g) * (bend + value * (2.0 - bend))).astype(BF16)
            part_v = dot(weights, g)
            part_k = dot(grads, q_ref[rows, cols]) * HALF_SCALE
            part_q = dot(kt_ref[cols, keys], grads).T * HALF_SCALE
            sum_k_ref[keys, cols] = part_v if first else sum_k_ref[keys, cols] + part_v
            sum_k_ref[keys, k_cols] = part_k if first else sum_k_ref[keys, k_cols] + part_k
            sum_q_ref[rows, cols] += part_q

    pair_loop(kind, chunks, later, earlier, place_ref, ids_ref, n, n_seq, part)
    if slope_q_ref is not None:
        gq_ref[...] = (sum_q_ref[...] * slope_q_ref[...].astype(F32)).astype(BF16)
    if slope_k_ref is not None:
        gk_ref[...] = (sum_k_ref[...] * slope_k_ref[...].astype(F32)).astype(BF16)


def backward(
    users, kind, q, keys, v, grads, later=0, earlier=0, add_q=None, add_k=None, slope_q=None, slope_k=None,
    chunks=(0, 1), after=()
):
    n, width = q.shape
    halves = len(grads) if isinstance(grads, list) else 0
    optional = [add_q, add_k, slope_q, slope_k]
    given = [x is not None for x in optional]
    args = [*users, q, *keys, v, *(grads if halves else [grads])] + [x for x in optional if x is not None]
    q_rows = n if 1 in chunks else n // 2
    scratch = [] if slope_q is None else [pltpu.VMEM((q_rows, width), F32)]
    scratch += [] if slope_k is None else [pltpu.VMEM((n, 2 * width), F32)]
    scratch += [pltpu.VMEM((n, width), BF16)] if halves == 2 else []
    return call(
        functools.partial(
            backward_kernel, lax.axis_size("seq"), kind, chunks, later, earlier, halves, given
        ),
        [
            like(q_rows, width, F32 if slope_q is None else BF16),
            like(n, 2 * width, F32 if slope_k is None else BF16),
        ],
        args,
        [SMEM] * 2 + [VMEM] * (len(args) - 2),
        scratch=scratch,
        flops=5 * n * n * width * len(chunks),
        nbytes=20 * n * width,
        name="backward",
        after=after,
    )


def gate_kernel(start, far, *refs):
    refs = list(refs)
    far_refs = [refs.pop(0) for _ in range(far)]
    own_ref, gg_ref, u_ref, slope_ref = refs[:4]
    outs = refs[-3:] if start == 0 else refs[-4:-1]
    n = far_refs[0].shape[0] if far_refs else own_ref.shape[0]
    rows = slice(start, start + n)
    attended = own_ref[rows, :]
    for far_ref in far_refs:
        attended = attended + far_ref[...].astype(F32)
    normed, inverse = centred(attended)
    gate = u_ref[rows, :].astype(F32)
    grad = gg_ref[rows, :]
    width = u_ref.shape[1]
    grad_attended = back(normed, inverse, grad * gate).astype(BF16)
    results = [
        grad_attended,
        (normed * gate).astype(BF16),
        (grad * normed * slope_ref[rows, :width].astype(F32)).astype(BF16),
    ]
    for out, result in zip(outs, results):
        out[rows, :] = result
    if start:
        refs[-1][...] = grad_attended
        for out, before in zip(outs, refs[4:7]):
            out[:start, :] = before[...]


def product_kernel(x_ref, w_ref, out_ref):
    out_ref[...] = dot_nt(x_ref[...], w_ref[...]).astype(out_ref.dtype)


def output_kernel(gated_ref, w_ref, tokens_ref, out_ref):
    out_ref[...] = (dot(gated_ref[...], w_ref[...]) + tokens_ref[...].astype(F32)).astype(BF16)


def far_kernel(x_ref, wv_ref, wk_ref, out_ref):
    width = wv_ref.shape[1]
    out_ref[...] = (
        dot_nt(x_ref[:, :width], wv_ref[...]) + dot_nt(x_ref[:, width:], wk_ref[...])
    ).astype(out_ref.dtype)


def near_kernel(gu_ref, gvk_ref, gq_ref, wu_ref, wv_ref, wq_ref, wk_ref, *refs):
    width = wv_ref.shape[1]
    grad_q = gq_ref[...].astype(F32)
    for far_ref in refs[:-1]:
        grad_q = grad_q + far_ref[...].astype(F32)
    refs[-1][...] = (
        dot_nt(gu_ref[...], wu_ref[...])
        + dot_nt(gvk_ref[:, :width], wv_ref[...])
        + dot_nt(grad_q.astype(BF16), wq_ref[...])
        + dot_nt(gvk_ref[:, width:], wk_ref[...])
    )


def tokens_kernel(tokens_ref, cotangent_ref, near_ref, *refs):
    grad = near_ref[...]
    for far_ref in refs[:-1]:
        grad = grad + far_ref[...].astype(F32)
    scaled, inverse = centred(tokens_ref[...].astype(F32))
    refs[-1][...] = (back(scaled, inverse, grad) + cotangent_ref[...].astype(F32)).astype(BF16)


def orders(dp):
    bits = dp.bit_length() - 1
    return [0] + list(range(1, bits)), [0] + list(range(bits - 1, 0, -1))


def block_of(me, slot, dp):
    bits = dp.bit_length() - 1
    clear, set_ = [
        sum(((slot >> (bits - 1 - p)) & 1) << order[p] for p in range(bits)) for order in orders(dp)
    ]
    return me ^ jnp.where((me & 1) == (slot >> (bits - 1)), clear, set_)


def weight_kernel(dp, half, parts, place_ref, *refs):
    out_ref = refs[-1]
    n_slots, rows = out_ref.shape[0], out_ref.shape[1]
    blocks = [block_of(place_ref[0], s, dp) for s in range(half * n_slots, (half + 1) * n_slots)]
    taken, at = 0, 0
    for count, width in parts:
        total = None
        for _ in range(count):
            x_ref, g_ref = refs[taken], refs[taken + 1]
            taken += 2
            x = jnp.concatenate(
                [x_ref[:, pl.ds(pl.multiple_of(b * rows, rows), rows)] for b in blocks], axis=1
            )
            term = dot_tn(x, g_ref[...])
            total = term if total is None else total + term
        out_ref[:, :, at : at + width] = total.astype(BF16).reshape(n_slots, rows, width)
        at += width


def weight_half(place, parts, half, after=(), weight=8):
    dp = lax.axis_size("dp")
    d = parts[0][0][0].shape[1]
    rows = d // dp
    widths = [pairs[0][1].shape[1] for pairs in parts]
    if rows % 128:
        total = jnp.concatenate(
            [sum(dot_tn(x, g) for x, g in pairs).astype(BF16) for pairs in parts], axis=1
        )
        return jnp.stack(
            [
                lax.dynamic_slice_in_dim(total, block_of(place[0], s, dp) * rows, rows)
                for s in range(half * dp // 2, (half + 1) * dp // 2)
            ]
        )
    args = [a for pairs in parts for pair in pairs for a in pair]
    n = args[0].shape[0]
    return call(
        functools.partial(weight_kernel, dp, half, [(len(p), w) for p, w in zip(parts, widths)]),
        jax.ShapeDtypeStruct((dp // 2, rows, sum(widths)), BF16),
        [place] + args,
        [SMEM] + [VMEM] * len(args),
        flops=sum(n * d * w * len(p) for p, w in zip(parts, widths)),
        nbytes=d * sum(widths),
        name="weights",
        after=after,
        weight=weight,
    )


def halve_kernel(mine_ref, other_ref, send_ref, keep_ref):
    half = send_ref.shape[0]
    total = mine_ref[...].astype(F32) + other_ref[...].astype(F32)
    send_ref[...] = total[half:].astype(BF16)
    keep_ref[...] = total[:half].astype(BF16)


def halve(mine, other, after=()):
    half = jax.ShapeDtypeStruct((mine.shape[0] // 2, *mine.shape[1:]), BF16)
    return call(halve_kernel, [half, half], [mine, other], name="halve", after=after)


def swap_dp(value, phase):
    dp = lax.axis_size("dp")
    pairs = [(i, i ^ (1 << orders(dp)[i & 1][phase])) for i in range(dp)]
    return lax.ppermute(value, "dp", pairs)


def over_seq(mine, other):
    n_seq, me = lax.axis_size("seq"), lax.axis_index("seq")
    rows, width = mine.shape[1] // n_seq, mine.shape[2]

    def chunk(index):
        start = (0, index * rows, 0)
        a = lax.dynamic_slice(mine, start, (1, rows, width))[0].astype(F32)
        return a + lax.dynamic_slice(other, start, (1, rows, width))[0].astype(F32)

    far = [
        lax.ppermute(chunk(me ^ r).astype(BF16), "seq", [(i, i ^ r) for i in range(n_seq)])
        for r in range(1, n_seq)
    ]
    return [chunk(me), *far]


def total_kernel(*refs):
    in_ref, out_ref = refs[-2:]
    count = (len(refs) - 2) // 2
    early, late = [
        sum([ref[...].astype(F32) for ref in part[1:]], part[0][...])
        for part in (refs[:count], refs[count : 2 * count])
    ]
    width = in_ref.shape[1] // 4
    in_ref[:, :width] = early[:, width:]
    in_ref[:, width : 2 * width] = late[:, :width]
    in_ref[:, 2 * width : 3 * width] = late[:, 2 * width :]
    in_ref[:, 3 * width :] = late[:, width : 2 * width]
    out_ref[...] = early[:, :width]


def local(tokens_in, user_ids, w_in, w_out, cotangent):
    tokens, id_table, upstream = tokens_in[0], user_ids[0], cotangent[0]
    n, d = tokens.shape
    width = w_out.shape[0]
    n_seq = lax.axis_size("seq")
    span = n_seq // 2
    up = (span + 1) // 2
    down = span - up
    place = jnp.stack([lax.axis_index("dp"), lax.axis_index("seq")]).astype(jnp.int32)
    ids = id_table.reshape(1, -1)
    users = [place, ids, ids, id_table.reshape(-1, 1)]

    far_tokens = [shift(tokens, by) for by in range(1, up + 1)]
    normed, slope_q, query, *sent = project(tokens, w_in, [2], "send" if down else True)
    if down:
        next_normed, next_query = [shift(x, -up) for x in sent]
    slope_u, gate, *_ = project(normed, w_in, [0], False)
    slope_vk, values, keys = project(normed, w_in, [1, 3], False, after=[gate])
    grad_gated = call(
        product_kernel, like(n, width, F32), [upstream, w_out], flops=2 * n * d * width,
        name="gated", after=[keys],
    )
    attended, keys_t = forward(users, "own", query, keys, values, after=[grad_gated])

    pieces = []
    for by in range(1, up + 1):
        pieces.append(project(far_tokens[by - 1], w_in, [1, 3], True, after=[attended]))
    far_attended = []
    order = [attended]
    if down:
        for half in (0, 1):
            partial = None
            for by in range(1, down + 1):
                _, _, far_values, far_keys = pieces[by - 1]
                [partial] = forward(
                    users, "far", next_query, far_keys, far_values, up, by, partial,
                    BF16 if by == down else F32, (half,), order,
                )
            order = [partial]
            far_attended.append(shift(partial, up))
    for by, (far_normed, slope, far_values, far_keys) in enumerate(pieces, 1):
        attended, far_t = forward(
            users, "near", query, far_keys, far_values, 0, by, attended, after=order
        )
        pieces[by - 1] = (far_normed, slope, far_values, (far_keys, far_t))

    gate_args = [attended, grad_gated, gate, slope_u]
    far_sums = [None] * up
    if down:
        first = call(
            functools.partial(gate_kernel, 0, 1),
            [like(n // 2, width, BF16)] * 3,
            [far_attended[0], *gate_args],
            flops=500 * n * width,
            name="gate",
        )
        next_grad = [shift(first[0], -up)]
        grad_q = None
        for by, (_, _, far_values, far_keys) in enumerate(pieces, 1):
            grad_q, far_sums[by - 1] = backward(
                users, "near", query, far_keys, far_values, [first[0]], 0, by, add_q=grad_q, chunks=(0,)
            )
        grad_attended, gated, grad_u, second = call(
            functools.partial(gate_kernel, n // 2, 1),
            [like(n, width, BF16)] * 3 + [like(n // 2, width, BF16)],
            [far_attended[1], *gate_args, *first],
            flops=500 * n * width,
            name="gate",
            after=[grad_q],
        )
        next_grad.append(shift(second, -up))
        rest = (1,)
    else:
        grad_attended, gated, grad_u = call(
            functools.partial(gate_kernel, 0, 0), [like(n, width, BF16)] * 3, gate_args, name="gate"
        )
        grad_q, rest = None, (0, 1)
    early = [[(upstream, gated)], [(normed, grad_u)]]
    early_send = weight_half(place, early, 1)
    early_other = swap_dp(early_send, 0)
    grad_q, grad_vk = backward(
        users, "own", query, (keys, keys_t), values, grad_attended, add_q=grad_q, slope_k=slope_vk,
        after=[early_send] + ([next_normed] if down else []),
    )
    early_mine = weight_half(place, early, 0, after=[grad_vk])
    early_send, early_mine = halve(early_mine, early_other)
    early_other = swap_dp(early_send, 1)
    for by, (_, slope, far_values, far_keys) in enumerate(pieces, 1):
        grad_q, far_sums[by - 1] = backward(
            users, "near", query, far_keys, far_values, grad_attended, 0, by, add_q=grad_q,
            add_k=far_sums[by - 1], slope_q=slope_q if by == up else None,
            slope_k=None if by <= down else slope, chunks=rest, after=[early_send],
        )
    if down:
        next_slope, _ = project(next_normed, w_in, [2], False, after=[grad_q])
    next_q = None
    for by in range(1, down + 1):
        _, slope, far_values, far_keys = pieces[by - 1]
        next_q, far_sums[by - 1] = backward(
            users, "far", next_query, far_keys, far_values, next_grad, up, by,
            add_q=next_q, add_k=far_sums[by - 1],
            slope_q=next_slope if by == down else None, slope_k=slope,
        )
    vk_pairs = [(normed, grad_vk)] + [(p[0], g) for p, g in zip(pieces, far_sums)]
    q_pairs = [(normed, grad_q)] + ([(next_normed, next_q)] if down else [])
    late = [vk_pairs, q_pairs]
    phases = range(2, lax.axis_size("dp").bit_length() - 1)
    order = [next_q] if down else [grad_q]
    for phase in phases:
        early_send, early_mine = halve(early_mine, early_other, after=order)
        early_other = swap_dp(early_send, phase)
        order = [early_send]
    late_send = weight_half(place, late, 1, after=order, weight=1)
    late_other = swap_dp(late_send, 0)
    late_mine = weight_half(place, late, 0, after=[late_send], weight=1)
    late_send, late_mine = halve(late_mine, late_other)
    late_other = swap_dp(late_send, 1)
    far_parts = []
    for by, grad in enumerate(far_sums, 1):
        part = call(
            far_kernel,
            like(n, d, BF16),
            [grad, w_in, w_in],
            [VMEM, columns(d, width, 1), columns(d, width, 3)],
            flops=4 * n * d * width,
            name="far", weight=1,
            after=[late_send],
        )
        far_parts.append(part)
    order = far_parts
    far_parts = [shift(part, -by) for by, part in enumerate(far_parts, 1)]
    next_q = [shift(next_q, up)] if down else []
    output = call(
        output_kernel, like(n, d, BF16), [gated, w_out, tokens], flops=2 * n * d * width,
        name="output", weight=0, after=[*order, early_other, *next_q],
    )
    early_sum = over_seq(early_mine, early_other)
    order = [output]
    for phase in phases:
        late_send, late_mine = halve(late_mine, late_other, after=order)
        late_other = swap_dp(late_send, phase)
        order = [late_send]
    late_sum = over_seq(late_mine, late_other)
    near = call(
        near_kernel,
        like(n, d, F32),
        [grad_u, grad_vk, grad_q] + [w_in] * 4 + next_q,
        [VMEM] * 3 + [columns(d, width, b) for b in range(4)] + [VMEM] * len(next_q),
        flops=8 * n * d * width,
        name="near", weight=0,
        after=[*order, late_other],
    )
    grad_tokens = call(
        tokens_kernel, like(n, d, BF16), [tokens, upstream, near, *far_parts], name="tokens", weight=0,
        after=[late_other],
    )
    rows = early_sum[0].shape[0]
    total_in, out_w = call(
        total_kernel,
        [like(rows, 4 * width, F32), like(rows, width, F32)],
        [*early_sum, *late_sum],
        name="total",
        after=[grad_tokens],
    )
    return (output[None], grad_tokens[None], total_in, out_w.T)


def solution(mesh):
    in_specs = (P("dp", "seq", None), P("dp", None), P(), P(), P("dp", "seq", None))
    out_specs = (
        P("dp", "seq", None),
        P("dp", "seq", None),
        P(("dp", "seq"), None),
        P(None, ("dp", "seq")),
    )
    return jax.shard_map(local, mesh=mesh, in_specs=in_specs, out_specs=out_specs, check_vma=False)
```

profile of v0, /device:TPU:0, one launch (start us, length us, event | category | flops | bytes accessed | tf_op | source)
XLA Modules:
  0.0 127.3 jit_solution(2460159923649060023)
XLA Ops:
  0.6 5.9 %collective-permute-start.1 = (bf16[512,1024]{1,0:T(8,128)(2,1)}, bf16[512,1024]{1,0:T(8,128)(2,1)}, u32[]{:S(2)}, u32[]{:S(2)}) collective-permute-start(bf16[512,1024]{1,0:T(8,128)(2,1)} %bitcast.25), channel_id=1, source_target_pairs={{0,1},{1,2},{2,3},{4,5},{5,6},{6,7},{8,9},{9,10},{10,11},{12,13},{... | collective-permute-start | bytes 3145736 | tf_op jit(solution)/shard_map/ppermute | solution.py:26
  6.6 2.2 %copy-done = bf16[1024,2048]{1,0:T(8,128)(2,1)S(1)} copy-done((bf16[1024,2048]{1,0:T(8,128)(2,1)S(1)}, bf16[1024,2048]{1,0:T(8,128)(2,1)}, u32[]{:S(2)}) %copy-start) | copy-done | bytes 4194328
  8.8 1.2 copy-done.5
  10.0 2.2 %project.5 = (bf16[512,1024]{1,0:T(8,128)(2,1)S(1)}, bf16[512,512]{1,0:T(8,128)(2,1)S(1)}, bf16[512,512]{1,0:T(8,128)(2,1)S(1)}, bf16[512,1024]{1,0:T(8,128)(2,1)}, bf16[512,512]{1,0:T(8,128)(2,1)}) custom-call(bf16[512,1024]{1,0:T(8,128)(2,1)S(1)} %bitcast.26, bf16[1024,2048]{1,0:T(8,128)(2,1)S(1)} %copy-done), custom_call_target="tpu_custom_call" | custom-call | flops 4294967296 | bytes 2097152 | tf_op jit(solution)/shard_map/project/pallas_call | solution.py:35
  12.2 1.3 %collective-permute-start = (bf16[512,512]{1,0:T(8,128)(2,1)}, bf16[512,512]{1,0:T(8,128)(2,1)}, u32[]{:S(2)}, u32[]{:S(2)}) collective-permute-start(bf16[512,512]{1,0:T(8,128)(2,1)} %get-tuple-element.48), channel_id=1, source_target_pairs={{1,0},{2,1},{3,2},{5,4},{6,5},{7,6},{9,8},{10,9},{11,10},{13,12},{... | collective-permute-start | bytes 1572872 | tf_op jit(solution)/shard_map/ppermute | solution.py:26
  13.5 1.3 %collective-permute-start.6 = (bf16[512,1024]{1,0:T(8,128)(2,1)}, bf16[512,1024]{1,0:T(8,128)(2,1)S(1)}, u32[]{:S(2)}, u32[]{:S(2)}) collective-permute-start(bf16[512,1024]{1,0:T(8,128)(2,1)} %get-tuple-element.70), channel_id=1, source_target_pairs={{1,0},{2,1},{3,2},{5,4},{6,5},{7,6},{9,8},{10,9},{11,10},{13,12},{... | collective-permute-start | bytes 3145736 | tf_op jit(solution)/shard_map/ppermute | solution.py:26
  16.6 1.7 %project.7 = (bf16[512,1024]{1,0:T(8,128)(2,1)S(1)}, bf16[512,512]{1,0:T(8,128)(2,1)S(1)}, bf16[512,512]{1,0:T(8,128)(2,1)S(1)}) custom-call(bf16[512,1024]{1,0:T(8,128)(2,1)S(1)} %get-tuple-element.50.refs_0_.refs_3_.refs_1_.refs_5_, bf16[1024,2048]{1,0:T(8,128)(2,1)S(1)} %copy-done.1, bf16[1024,2048]{1,0:T(8,128)(2,1)S(1)} %copy-done.1, ...), custom_call_target="tpu_custom_call" | custom-call | flops 8589934592 | bytes 3145728 | tf_op jit(solution)/shard_map/project/pallas_call | solution.py:35
  21.0 1.3 %copy.11.refs_3_ = s32[2048,1]{1,0:T(8,128)} copy(s32[2048,1]{0,1:T(1,128)S(1)} %bitcast.34) | data formatting | bytes 16384 | tf_op jit(solution)/shard_map/reshape;squeeze | solution.py:489
  22.4 1.2 copy-done.14
  26.2 2.2 %forward.4 = (f32[512,512]{1,0:T(8,128)S(1)}, bf16[512,512]{1,0:T(8,128)(2,1)S(1)}) custom-call(s32[2]{0:T(128)S(1)} %pad_add_fusion.refs_0_, s32[1,2048]{1,0:T(1,128)S(1)} %copy-done.25, s32[1,2048]{1,0:T(1,128)S(1)} %copy-done.25, s32[2048,1]{1,0:T(8,128)S(1)} %copy-done.13, bf16[512,512]{1,0:T(8,128)(2,1)S(1)} %copy-done.29, ...), custom_call_target="tpu_custom_call" | custom-call | flops 4294967296 | bytes 2621440 | tf_op jit(solution)/shard_map/forward/pallas_call | solution.py:35
  28.4 3.3 %project.8 = (bf16[512,1024]{1,0:T(8,128)(2,1)S(1)}, bf16[512,1024]{1,0:T(8,128)(2,1)S(1)}, bf16[512,512]{1,0:T(8,128)(2,1)S(1)}, bf16[512,512]{1,0:T(8,128)(2,1)S(1)}) custom-call(bf16[512,1024]{1,0:T(8,128)(2,1)} %collective-permute-done.1.refs_0_, bf16[1024,2048]{1,0:T(8,128)(2,1)S(1)} %copy-done.2, bf16[1024,2048]{1,0:T(8,128)(2,1)S(1)} %copy-done.2, ...), custom_call_target="tpu_custom_call" | custom-call | flops 8589934592 | bytes 3145728 | tf_op jit(solution)/shard_map/project/pallas_call | solution.py:35
  31.8 1.2 forward.5.refs_7_
  32.9 6.5 %collective-permute-start.3 = (bf16[256,512]{1,0:T(8,128)(2,1)S(1)}, bf16[256,512]{1,0:T(8,128)(2,1)S(1)}, u32[]{:S(2)}, u32[]{:S(2)}) collective-permute-start(bf16[256,512]{1,0:T(8,128)(2,1)S(1)} %forward.5.refs_7_), channel_id=1, source_target_pairs={{0,1},{1,2},{2,3},{4,5},{5,6},{6,7},{8,9},{9,10},{10,11},{12,13},{... | collective-permute-start | bytes 786440 | tf_op jit(solution)/shard_map/ppermute | solution.py:26
  39.5 1.2 forward.6.refs_8_
  40.6 2.7 %collective-permute-start.2 = (bf16[256,512]{1,0:T(8,128)(2,1)S(1)}, bf16[256,512]{1,0:T(8,128)(2,1)S(1)}, u32[]{:S(2)}, u32[]{:S(2)}) collective-permute-start(bf16[256,512]{1,0:T(8,128)(2,1)S(1)} %forward.6.refs_8_), channel_id=1, source_target_pairs={{0,1},{1,2},{2,3},{4,5},{5,6},{6,7},{8,9},{9,10},{10,11},{12,13},{... | collective-permute-start | bytes 786440 | tf_op jit(solution)/shard_map/ppermute | solution.py:26
  44.2 1.9 %collective-permute-done.3.refs_0_ = bf16[256,512]{1,0:T(8,128)(2,1)S(1)} collective-permute-done((bf16[256,512]{1,0:T(8,128)(2,1)S(1)}, bf16[256,512]{1,0:T(8,128)(2,1)S(1)}, u32[]{:S(2)}, u32[]{:S(2)}) %collective-permute-start.3) | collective-permute-done | bytes 262176 | tf_op jit(solution)/shard_map/ppermute | solution.py:26
  46.6 1.3 %collective-permute-start.4 = (bf16[256,512]{1,0:T(8,128)(2,1)S(1)}, bf16[256,512]{1,0:T(8,128)(2,1)S(1)}, u32[]{:S(2)}, u32[]{:S(2)}) collective-permute-start(bf16[256,512]{1,0:T(8,128)(2,1)S(1)} %get-tuple-element.59.refs_8_.refs_5_), channel_id=1, source_target_pairs={{1,0},{2,1},{3,2},{5,4},{6,5},{7,6},{9,8},{10,9},{11,10},{13,12},{... | collective-permute-start | bytes 786440 | tf_op jit(solution)/shard_map/ppermute | solution.py:26
  50.6 1.3 %weights.4.refs_11_ = bf16[4,128,1024]{2,1,0:T(8,128)(2,1)S(1)} custom-call(s32[2]{0:T(128)S(1)} %pad_add_fusion.refs_0_, bf16[512,1024]{1,0:T(8,128)(2,1)S(1)} %bitcast.31, bf16[512,512]{1,0:T(8,128)(2,1)S(1)} %get-tuple-element.64.refs_2_.refs_0_, bf16[512,1024]{1,0:T(8,128)(2,1)S(1)} %get-tuple-element.50.refs_0_.refs_3_.refs_1_.refs_5_, ...), custom_call_target="tpu_custom_call" | custom-call | flops 4294967296 | bytes 1048576 | tf_op jit(solution)/shard_map/weights/pallas_call | solution.py:35
  52.0 1.3 %collective-permute-start.5 = (bf16[256,512]{1,0:T(8,128)(2,1)S(1)}, bf16[256,512]{1,0:T(8,128)(2,1)S(1)}, u32[]{:S(2)}, u32[]{:S(2)}) collective-permute-start(bf16[256,512]{1,0:T(8,128)(2,1)S(1)} %get-tuple-element.65), channel_id=1, source_target_pairs={{1,0},{2,1},{3,2},{5,4},{6,5},{7,6},{9,8},{10,9},{11,10},{13,12},{... | collective-permute-start | bytes 786440 | tf_op jit(solution)/shard_map/ppermute | solution.py:26
  53.3 3.3 %backward.5 = (f32[512,512]{1,0:T(8,128)S(1)}, bf16[512,1024]{1,0:T(8,128)(2,1)S(1)}) custom-call(s32[2]{0:T(128)S(1)} %pad_add_fusion.refs_0_, s32[1,2048]{1,0:T(1,128)S(1)} %copy-done.25, s32[1,2048]{1,0:T(1,128)S(1)} %copy-done.25, s32[2048,1]{1,0:T(8,128)S(1)} %copy-done.13, bf16[512,512]{1,0:T(8,128)(2,1)S(1)} %copy-done.29, ...), custom_call_target="tpu_custom_call" | custom-call | flops 10737418240 | bytes 5242880 | tf_op jit(solution)/shard_map/backward/pallas_call | solution.py:35
  56.6 1.3 %weights.5.refs_0_ = bf16[4,128,1024]{2,1,0:T(8,128)(2,1)S(1)} custom-call(s32[2]{0:T(128)S(1)} %pad_add_fusion.refs_0_, bf16[512,1024]{1,0:T(8,128)(2,1)S(1)} %bitcast.32, bf16[512,512]{1,0:T(8,128)(2,1)S(1)} %get-tuple-element.64.refs_2_.refs_0_, bf16[512,1024]{1,0:T(8,128)(2,1)S(1)} %get-tuple-element.50.refs_0_.refs_3_.refs_1_.refs_5_, ...), custom_call_target="tpu_custom_call" | custom-call | flops 4294967296 | bytes 1048576 | tf_op jit(solution)/shard_map/weights/pallas_call | solution.py:35
  58.2 1.6 %collective-permute-start.8 = (bf16[2,128,1024]{2,1,0:T(8,128)(2,1)S(1)}, bf16[2,128,1024]{2,1,0:T(8,128)(2,1)S(1)}, u32[]{:S(2)}, u32[]{:S(2)}) collective-permute-start(bf16[2,128,1024]{2,1,0:T(8,128)(2,1)S(1)} %get-tuple-element.75.refs_12_), channel_id=1, source_target_pairs={{0,8},{4,20},{8,0},{12,28},{16,24},{20,4},{24,16},{28,12},{1,9},{5... | collective-permute-start | bytes 1572872 | tf_op jit(solution)/shard_map/ppermute | solution.py:445
  59.8 1.2 backward.6
  61.0 1.7 %project.9 = (bf16[512,512]{1,0:T(8,128)(2,1)S(1)}, bf16[512,512]{1,0:T(8,128)(2,1)}) custom-call(bf16[512,1024]{1,0:T(8,128)(2,1)S(1)} %copy-done.9, bf16[1024,2048]{1,0:T(8,128)(2,1)S(1)} %copy-done.2, bf16[512,512]{1,0:T(8,128)(2,1)S(1)} %get-tuple-element.77.refs_2_.refs_6_), custom_call_target="tpu_custom_call" | custom-call | flops 4294967296 | bytes 2097152 | tf_op jit(solution)/shard_map/project/pallas_call | solution.py:35
  62.7 1.8 %collective-permute-done.5.refs_9_ = bf16[256,512]{1,0:T(8,128)(2,1)S(1)} collective-permute-done((bf16[256,512]{1,0:T(8,128)(2,1)S(1)}, bf16[256,512]{1,0:T(8,128)(2,1)S(1)}, u32[]{:S(2)}, u32[]{:S(2)}) %collective-permute-start.5) | collective-permute-done | bytes 262176 | tf_op jit(solution)/shard_map/ppermute | solution.py:26
  64.6 1.7 %backward.7 = (bf16[512,512]{1,0:T(8,128)(2,1)S(1)}, bf16[512,1024]{1,0:T(8,128)(2,1)S(1)}) custom-call(s32[2]{0:T(128)S(1)} %pad_add_fusion.refs_0_, s32[1,2048]{1,0:T(1,128)S(1)} %copy-done.25, s32[1,2048]{1,0:T(1,128)S(1)} %copy-done.25, s32[2048,1]{1,0:T(8,128)S(1)} %copy-done.13, bf16[512,512]{1,0:T(8,128)(2,1)} %collective-permute-done.refs_4_, ...), custom_call_target="tpu_custom_call" | custom-call | flops 10737418240 | bytes 5242880 | tf_op jit(solution)/shard_map/backward/pallas_call | solution.py:35
  66.2 1.2 collective-permute-done.8.refs_1_
  67.6 2.4 %weights.6.refs_9_ = bf16[4,128,1536]{2,1,0:T(8,128)(2,1)S(1)} custom-call(s32[2]{0:T(128)S(1)} %pad_add_fusion.refs_0_, bf16[512,1024]{1,0:T(8,128)(2,1)S(1)} %get-tuple-element.50.refs_0_.refs_3_.refs_1_.refs_5_, bf16[512,1024]{1,0:T(8,128)(2,1)S(1)} %get-tuple-element.74.refs_5_.refs_2_.refs_1_, bf16[512,1024]{1,0:T(8,128)(2,1)S(1)} %get-tuple-element.81.refs_3_, ...), custom_call_target="tpu_custom_call" | custom-call | flops 1610612736 | bytes 1572864 | tf_op jit(solution)/shard_map/weights/pallas_call | solution.py:35
  70.1 2.4 %weights.7.refs_0_ = bf16[4,128,1536]{2,1,0:T(8,128)(2,1)S(1)} custom-call(s32[2]{0:T(128)S(1)} %pad_add_fusion.refs_0_, bf16[512,1024]{1,0:T(8,128)(2,1)S(1)} %get-tuple-element.50.refs_0_.refs_3_.refs_1_.refs_5_, bf16[512,1024]{1,0:T(8,128)(2,1)S(1)} %get-tuple-element.74.refs_5_.refs_2_.refs_1_, bf16[512,1024]{1,0:T(8,128)(2,1)S(1)} %get-tuple-element.81.refs_3_, ...), custom_call_target="tpu_custom_call" | custom-call | flops 1610612736 | bytes 1572864 | tf_op jit(solution)/shard_map/weights/pallas_call | solution.py:35
  73.9 1.6 %collective-permute-start.12 = (bf16[2,128,1536]{2,1,0:T(8,128)(2,1)S(1)}, bf16[2,128,1536]{2,1,0:T(8,128)(2,1)S(1)}, u32[]{:S(2)}, u32[]{:S(2)}) collective-permute-start(bf16[2,128,1536]{2,1,0:T(8,128)(2,1)S(1)} %get-tuple-element.85.refs_3_), channel_id=1, source_target_pairs={{0,8},{4,20},{8,0},{12,28},{16,24},{20,4},{24,16},{28,12},{1,9},{5... | collective-permute-start | bytes 2359304 | tf_op jit(solution)/shard_map/ppermute | solution.py:445
  75.4 6.0 %collective-permute-start.11 = (bf16[512,512]{1,0:T(8,128)(2,1)S(1)}, bf16[512,512]{1,0:T(8,128)(2,1)S(1)}, u32[]{:S(2)}, u32[]{:S(2)}) collective-permute-start(bf16[512,512]{1,0:T(8,128)(2,1)S(1)} %get-tuple-element.82.refs_2_.refs_8_), channel_id=1, source_target_pairs={{0,1},{1,2},{2,3},{4,5},{5,6},{6,7},{8,9},{9,10},{10,11},{12,13},{... | collective-permute-start | bytes 1572872 | tf_op jit(solution)/shard_map/ppermute | solution.py:26
  81.4 2.3 %far.1.refs_3_ = bf16[512,1024]{1,0:T(8,128)(2,1)} custom-call(bf16[512,1024]{1,0:T(8,128)(2,1)S(1)} %get-tuple-element.80.refs_4_.refs_0_, bf16[1024,2048]{1,0:T(8,128)(2,1)S(1)} %copy-done.2, bf16[1024,2048]{1,0:T(8,128)(2,1)S(1)} %copy-done.2, bf16[2,128,1536]{2,1,0:T(8,128)(2,1)S(1)} %get-tuple-element.85.refs_3_), custom_call_target="tpu_custom_call" | custom-call | flops 1073741824 | tf_op jit(solution)/shard_map/far/pallas_call | solution.py:35
  83.7 1.5 %collective-permute-start.14 = (bf16[512,1024]{1,0:T(8,128)(2,1)}, bf16[512,1024]{1,0:T(8,128)(2,1)}, u32[]{:S(2)}, u32[]{:S(2)}) collective-permute-start(bf16[512,1024]{1,0:T(8,128)(2,1)} %far.1.refs_3_), channel_id=1, source_target_pairs={{1,0},{2,1},{3,2},{5,4},{6,5},{7,6},{9,8},{10,9},{11,10},{13,12},{... | collective-permute-start | bytes 3145736 | tf_op jit(solution)/shard_map/ppermute | solution.py:26
  86.3 6.2 %collective-permute-done.11.refs_5_.refs_7_ = bf16[512,512]{1,0:T(8,128)(2,1)S(1)} collective-permute-done((bf16[512,512]{1,0:T(8,128)(2,1)S(1)}, bf16[512,512]{1,0:T(8,128)(2,1)S(1)}, u32[]{:S(2)}, u32[]{:S(2)}) %collective-permute-start.11) | collective-permute-done | bytes 524320 | tf_op jit(solution)/shard_map/ppermute | solution.py:26
  92.5 1.7 %output.1.refs_2_ = bf16[512,1024]{1,0:T(8,128)(2,1)} custom-call(bf16[512,512]{1,0:T(8,128)(2,1)S(1)} %get-tuple-element.64.refs_2_.refs_0_, bf16[512,1024]{1,0:T(8,128)(2,1)S(1)} %copy-done.15, bf16[512,1024]{1,0:T(8,128)(2,1)S(1)} %bitcast.27, bf16[512,1024]{1,0:T(8,128)(2,1)} %far.1.refs_3_, bf16[1,128,1024]{2,1,0:T(8,128)(2,1)S(1)} %collective-permute-done.10.refs_4_, ...), custom_call_target="tpu_custom_call" | custom-call | tf_op jit(solution)/shard_map/output/pallas_call | solution.py:35
  94.2 1.2 copy-done.7
  97.1 1.6 %collective-permute-start.13 = (bf16[1,128,1536]{2,1,0:T(8,128)(2,1)}, bf16[1,128,1536]{2,1,0:T(8,128)(2,1)S(1)}, u32[]{:S(2)}, u32[]{:S(2)}) collective-permute-start(bf16[1,128,1536]{2,1,0:T(8,128)(2,1)} %get-tuple-element.87.refs_8_), channel_id=1, source_target_pairs={{0,16},{4,12},{8,24},{12,4},{16,0},{20,28},{24,8},{28,20},{1,17},{... | collective-permute-start | bytes 1179656 | tf_op jit(solution)/shard_map/ppermute | solution.py:445
  98.7 1.2 fusion.5
  99.8 2.6 %collective-permute-start.15 = (bf16[32,1024]{1,0:T(8,128)(2,1)S(1)}, bf16[32,1024]{1,0:T(8,128)(2,1)S(1)}, u32[]{:S(2)}, u32[]{:S(2)}) collective-permute-start(bf16[32,1024]{1,0:T(8,128)(2,1)S(1)} %get-tuple-element.98), channel_id=1, source_target_pairs={{0,1},{1,0},{2,3},{3,2},{4,5},{5,4},{6,7},{7,6},{8,9},{9,8},{10,11... | collective-permute-start | bytes 196616 | tf_op jit(solution)/shard_map/ppermute | solution.py:458
  102.4 2.7 %collective-permute-done.13.refs_9_.refs_4_ = bf16[1,128,1536]{2,1,0:T(8,128)(2,1)S(1)} collective-permute-done((bf16[1,128,1536]{2,1,0:T(8,128)(2,1)}, bf16[1,128,1536]{2,1,0:T(8,128)(2,1)S(1)}, u32[]{:S(2)}, u32[]{:S(2)}) %collective-permute-start.13) | collective-permute-done | bytes 393248 | tf_op jit(solution)/shard_map/ppermute | solution.py:445
  106.2 2.6 %collective-permute-start.18 = (bf16[32,1536]{1,0:T(8,128)(2,1)S(1)}, bf16[32,1536]{1,0:T(8,128)(2,1)S(1)}, u32[]{:S(2)}, u32[]{:S(2)}) collective-permute-start(bf16[32,1536]{1,0:T(8,128)(2,1)S(1)} %get-tuple-element.94), channel_id=1, source_target_pairs={{0,1},{1,0},{2,3},{3,2},{4,5},{5,4},{6,7},{7,6},{8,9},{9,8},{10,11... | collective-permute-start | bytes 294920 | tf_op jit(solution)/shard_map/ppermute | solution.py:458
  108.7 2.8 %collective-permute-start.19 = (bf16[32,1536]{1,0:T(8,128)(2,1)S(1)}, bf16[32,1536]{1,0:T(8,128)(2,1)S(1)}, u32[]{:S(2)}, u32[]{:S(2)}) collective-permute-start(bf16[32,1536]{1,0:T(8,128)(2,1)S(1)} %get-tuple-element.93), channel_id=1, source_target_pairs={{0,2},{1,3},{2,0},{3,1},{4,6},{5,7},{6,4},{7,5},{8,10},{9,11},{10,... | collective-permute-start | bytes 294920 | tf_op jit(solution)/shard_map/ppermute | solution.py:458
  111.6 3.7 %collective-permute-done.15.refs_1_ = bf16[32,1024]{1,0:T(8,128)(2,1)S(1)} collective-permute-done((bf16[32,1024]{1,0:T(8,128)(2,1)S(1)}, bf16[32,1024]{1,0:T(8,128)(2,1)S(1)}, u32[]{:S(2)}, u32[]{:S(2)}) %collective-permute-start.15) | collective-permute-done | bytes 65568 | tf_op jit(solution)/shard_map/ppermute | solution.py:458
  115.8 1.3 %collective-permute-start.17 = (bf16[32,1024]{1,0:T(8,128)(2,1)S(1)}, bf16[32,1024]{1,0:T(8,128)(2,1)S(1)}, u32[]{:S(2)}, u32[]{:S(2)}) collective-permute-start(bf16[32,1024]{1,0:T(8,128)(2,1)S(1)} %get-tuple-element.96), channel_id=1, source_target_pairs={{0,3},{1,2},{2,1},{3,0},{4,7},{5,6},{6,5},{7,4},{8,11},{9,10},{10,... | collective-permute-start | bytes 196616 | tf_op jit(solution)/shard_map/ppermute | solution.py:458
  117.1 2.2 %copy-done.3 = bf16[1024,2048]{1,0:T(8,128)(2,1)S(1)} copy-done((bf16[1024,2048]{1,0:T(8,128)(2,1)S(1)}, bf16[1024,2048]{1,0:T(8,128)(2,1)}, u32[]{:S(2)}) %copy-start.3) | copy-done | bytes 4194328
  119.3 2.4 %near.1.refs_2_ = f32[512,1024]{1,0:T(8,128)S(1)} custom-call(bf16[512,512]{1,0:T(8,128)(2,1)S(1)} %copy-done.18, bf16[512,1024]{1,0:T(8,128)(2,1)S(1)} %get-tuple-element.74.refs_5_.refs_2_.refs_1_, bf16[512,512]{1,0:T(8,128)(2,1)S(1)} %get-tuple-element.77.refs_2_.refs_6_, bf16[1024,2048]{1,0:T(8,128)(2,1)S(1)} %copy-done.3, ...), custom_call_target="tpu_custom_call" | custom-call | tf_op jit(solution)/shard_map/near/pallas_call | solution.py:35
  121.7 3.6 %tokens.1.refs_8_ = bf16[512,1024]{1,0:T(8,128)(2,1)} custom-call(bf16[512,1024]{1,0:T(8,128)(2,1)S(1)} %bitcast.28, bf16[512,1024]{1,0:T(8,128)(2,1)S(1)} %bitcast.33, f32[512,1024]{1,0:T(8,128)S(1)} %near.1.refs_2_, bf16[512,1024]{1,0:T(8,128)(2,1)} %collective-permute-done.14.refs_3_, bf16[1,128,1536]{2,1,0:T(8,128)(2,1)S(1)} %collective-permute-done.13.refs_9_.refs_4_), custom_call_target="tpu_custom_call" | custom-call | tf_op jit(solution)/shard_map/tokens/pallas_call | solution.py:35
  125.4 1.2 copy-done.4
  (99 shorter events, 18.0 us)
Async XLA Ops:
  0.6 27.8 %collective-permute-start.1 = (bf16[512,1024]{1,0:T(8,128)(2,1)}, bf16[512,1024]{1,0:T(8,128)(2,1)}, u32[]{:S(2)}, u32[]{:S(2)}) collective-permute-start(bf16[512,1024]{1,0:T(8,128)(2,1)} %bitcast.25), channel_id=1, source_target_pairs={{0,1},{1,2},{2,3},{4,5},{5,6},{6,7},{8,9},{9,10},{10,11},{12,13},{... | collective-permute-start | bytes 3145736 | tf_op jit(solution)/shard_map/ppermute | solution.py:26
  6.6 2.2 %copy-start = (bf16[1024,2048]{1,0:T(8,128)(2,1)S(1)}, bf16[1024,2048]{1,0:T(8,128)(2,1)}, u32[]{:S(2)}) copy-start(bf16[1024,2048]{1,0:T(8,128)(2,1)} %refs_6_.1) | copy-start | bytes 12582916
  10.0 4.8 %copy-start.1 = (bf16[1024,2048]{1,0:T(8,128)(2,1)S(1)}, bf16[1024,2048]{1,0:T(8,128)(2,1)}, u32[]{:S(2)}) copy-start(bf16[1024,2048]{1,0:T(8,128)(2,1)} %refs_6_.1) | copy-start | bytes 12582916
  12.2 3.5 %copy-start.26 = (bf16[512,512]{1,0:T(8,128)(2,1)}, bf16[512,512]{1,0:T(8,128)(2,1)S(1)}, u32[]{:S(2)}) copy-start(bf16[512,512]{1,0:T(8,128)(2,1)S(1)} %get-tuple-element.73.refs_11_) | copy-start | bytes 1572868
  12.2 3.6 %copy-start.28 = (bf16[512,512]{1,0:T(8,128)(2,1)}, bf16[512,512]{1,0:T(8,128)(2,1)S(1)}, u32[]{:S(2)}) copy-start(bf16[512,512]{1,0:T(8,128)(2,1)S(1)} %get-tuple-element.49.refs_4_) | copy-start | bytes 1572868
  12.2 19.5 %collective-permute-start = (bf16[512,512]{1,0:T(8,128)(2,1)}, bf16[512,512]{1,0:T(8,128)(2,1)}, u32[]{:S(2)}, u32[]{:S(2)}) collective-permute-start(bf16[512,512]{1,0:T(8,128)(2,1)} %get-tuple-element.48), channel_id=1, source_target_pairs={{1,0},{2,1},{3,2},{5,4},{6,5},{7,6},{9,8},{10,9},{11,10},{13,12},{... | collective-permute-start | bytes 1572872 | tf_op jit(solution)/shard_map/ppermute | solution.py:26
  13.5 39.7 %collective-permute-start.6 = (bf16[512,1024]{1,0:T(8,128)(2,1)}, bf16[512,1024]{1,0:T(8,128)(2,1)S(1)}, u32[]{:S(2)}, u32[]{:S(2)}) collective-permute-start(bf16[512,1024]{1,0:T(8,128)(2,1)} %get-tuple-element.70), channel_id=1, source_target_pairs={{1,0},{2,1},{3,2},{5,4},{6,5},{7,6},{9,8},{10,9},{11,10},{13,12},{... | collective-permute-start | bytes 3145736 | tf_op jit(solution)/shard_map/ppermute | solution.py:26
  16.6 1.8 %copy-start.21 = (bf16[512,512]{1,0:T(8,128)(2,1)}, bf16[512,512]{1,0:T(8,128)(2,1)S(1)}, u32[]{:S(2)}) copy-start(bf16[512,512]{1,0:T(8,128)(2,1)S(1)} %get-tuple-element.51.refs_3_) | copy-start | bytes 1572868
  16.6 4.3 %copy-start.25 = (s32[1,2048]{1,0:T(1,128)S(1)}, s32[1,2048]{1,0:T(1,128)}, u32[]{:S(2)}) copy-start(s32[1,2048]{1,0:T(1,128)} %refs_2_.20) | copy-start | bytes 24580
  16.6 5.7 %copy-start.10 = (bf16[1,512,1024]{2,1,0:T(8,128)(2,1)S(1)}, bf16[1,512,1024]{2,1,0:T(8,128)(2,1)}, u32[]{:S(2)}) copy-start(bf16[1,512,1024]{2,1,0:T(8,128)(2,1)} %param.9) | copy-start | bytes 3145732
  22.4 1.2 copy-start.14
  24.7 1.4 %copy-start.29 = (bf16[512,512]{1,0:T(8,128)(2,1)S(1)}, bf16[512,512]{1,0:T(8,128)(2,1)}, u32[]{:S(2)}) copy-start(bf16[512,512]{1,0:T(8,128)(2,1)} %copy-done.28) | copy-start | bytes 1572868
  24.7 1.5 %copy-start.31 = (bf16[512,512]{1,0:T(8,128)(2,1)S(1)}, bf16[512,512]{1,0:T(8,128)(2,1)}, u32[]{:S(2)}) copy-start(bf16[512,512]{1,0:T(8,128)(2,1)} %copy-done.30) | copy-start | bytes 1572868
  26.2 2.2 %copy-start.2 = (bf16[1024,2048]{1,0:T(8,128)(2,1)S(1)}, bf16[1024,2048]{1,0:T(8,128)(2,1)}, u32[]{:S(2)}) copy-start(bf16[1024,2048]{1,0:T(8,128)(2,1)} %refs_6_.1) | copy-start | bytes 12582916
  32.9 13.3 %collective-permute-start.3 = (bf16[256,512]{1,0:T(8,128)(2,1)S(1)}, bf16[256,512]{1,0:T(8,128)(2,1)S(1)}, u32[]{:S(2)}, u32[]{:S(2)}) collective-permute-start(bf16[256,512]{1,0:T(8,128)(2,1)S(1)} %forward.5.refs_7_), channel_id=1, source_target_pairs={{0,1},{1,2},{2,3},{4,5},{5,6},{6,7},{8,9},{9,10},{10,11},{12,13},{... | collective-permute-start | bytes 786440 | tf_op jit(solution)/shard_map/ppermute | solution.py:26
  40.6 5.6 %copy-start.20 = (bf16[512,512]{1,0:T(8,128)(2,1)S(1)}, bf16[512,512]{1,0:T(8,128)(2,1)}, u32[]{:S(2)}) copy-start(bf16[512,512]{1,0:T(8,128)(2,1)} %copy-done.19) | copy-start | bytes 1572868
  40.6 5.6 %copy-start.22 = (bf16[512,512]{1,0:T(8,128)(2,1)S(1)}, bf16[512,512]{1,0:T(8,128)(2,1)}, u32[]{:S(2)}) copy-start(bf16[512,512]{1,0:T(8,128)(2,1)} %copy-done.21) | copy-start | bytes 1572868
  40.6 9.4 %collective-permute-start.2 = (bf16[256,512]{1,0:T(8,128)(2,1)S(1)}, bf16[256,512]{1,0:T(8,128)(2,1)S(1)}, u32[]{:S(2)}, u32[]{:S(2)}) collective-permute-start(bf16[256,512]{1,0:T(8,128)(2,1)S(1)} %forward.6.refs_8_), channel_id=1, source_target_pairs={{0,1},{1,2},{2,3},{4,5},{5,6},{6,7},{8,9},{9,10},{10,11},{12,13},{... | collective-permute-start | bytes 786440 | tf_op jit(solution)/shard_map/ppermute | solution.py:26
  46.6 17.9 %collective-permute-start.4 = (bf16[256,512]{1,0:T(8,128)(2,1)S(1)}, bf16[256,512]{1,0:T(8,128)(2,1)S(1)}, u32[]{:S(2)}, u32[]{:S(2)}) collective-permute-start(bf16[256,512]{1,0:T(8,128)(2,1)S(1)} %get-tuple-element.59.refs_8_.refs_5_), channel_id=1, source_target_pairs={{1,0},{2,1},{3,2},{5,4},{6,5},{7,6},{9,8},{10,9},{11,10},{13,12},{... | collective-permute-start | bytes 786440 | tf_op jit(solution)/shard_map/ppermute | solution.py:26
  50.6 6.1 %copy-start.17 = (bf16[512,512]{1,0:T(8,128)(2,1)}, bf16[512,512]{1,0:T(8,128)(2,1)S(1)}, u32[]{:S(2)}) copy-start(bf16[512,512]{1,0:T(8,128)(2,1)S(1)} %get-tuple-element.69.refs_4_.refs_0_) | copy-start | bytes 1572868
  50.6 2.7 %copy-start.35 = (bf16[512,1024]{1,0:T(8,128)(2,1)S(1)}, bf16[512,1024]{1,0:T(8,128)(2,1)}, u32[]{:S(2)}) copy-start(bf16[512,1024]{1,0:T(8,128)(2,1)} %copy-done.34) | copy-start | bytes 3145732
  51.9 6.1 %collective-permute-start.7 = (bf16[4,128,1024]{2,1,0:T(8,128)(2,1)S(1)}, bf16[4,128,1024]{2,1,0:T(8,128)(2,1)S(1)}, u32[]{:S(2)}, u32[]{:S(2)}) collective-permute-start(bf16[4,128,1024]{2,1,0:T(8,128)(2,1)S(1)} %weights.4.refs_11_), channel_id=1, source_target_pairs={{0,4},{4,0},{8,12},{12,8},{16,20},{20,16},{24,28},{28,24},{1,5},{5... | collective-permute-start | bytes 3145736 | tf_op jit(solution)/shard_map/ppermute | solution.py:445
  52.0 12.6 %collective-permute-start.5 = (bf16[256,512]{1,0:T(8,128)(2,1)S(1)}, bf16[256,512]{1,0:T(8,128)(2,1)S(1)}, u32[]{:S(2)}, u32[]{:S(2)}) collective-permute-start(bf16[256,512]{1,0:T(8,128)(2,1)S(1)} %get-tuple-element.65), channel_id=1, source_target_pairs={{1,0},{2,1},{3,2},{5,4},{6,5},{7,6},{9,8},{10,9},{11,10},{13,12},{... | collective-permute-start | bytes 786440 | tf_op jit(solution)/shard_map/ppermute | solution.py:26
  53.3 3.4 %copy-start.8 = (bf16[512,1024]{1,0:T(8,128)(2,1)}, bf16[512,1024]{1,0:T(8,128)(2,1)S(1)}, u32[]{:S(2)}) copy-start(bf16[512,1024]{1,0:T(8,128)(2,1)S(1)} %collective-permute-done.6.refs_12_.refs_0_.refs_7_) | copy-start | bytes 3145732
  53.3 3.4 %copy-start.11 = (bf16[1,512,1024]{2,1,0:T(8,128)(2,1)S(1)}, bf16[1,512,1024]{2,1,0:T(8,128)(2,1)}, u32[]{:S(2)}) copy-start(bf16[1,512,1024]{2,1,0:T(8,128)(2,1)} %param.9) | copy-start | bytes 3145732
  58.0 1.8 %copy-start.27 = (bf16[512,512]{1,0:T(8,128)(2,1)S(1)}, bf16[512,512]{1,0:T(8,128)(2,1)}, u32[]{:S(2)}) copy-start(bf16[512,512]{1,0:T(8,128)(2,1)} %copy-done.26) | copy-start | bytes 1572868
  58.2 9.2 %collective-permute-start.8 = (bf16[2,128,1024]{2,1,0:T(8,128)(2,1)S(1)}, bf16[2,128,1024]{2,1,0:T(8,128)(2,1)S(1)}, u32[]{:S(2)}, u32[]{:S(2)}) collective-permute-start(bf16[2,128,1024]{2,1,0:T(8,128)(2,1)S(1)} %get-tuple-element.75.refs_12_), channel_id=1, source_target_pairs={{0,8},{4,20},{8,0},{12,28},{16,24},{20,4},{24,16},{28,12},{1,9},{5... | collective-permute-start | bytes 1572872 | tf_op jit(solution)/shard_map/ppermute | solution.py:445
  67.6 4.9 %copy-start.24 = (bf16[1,128,1024]{2,1,0:T(8,128)(2,1)}, bf16[1,128,1024]{2,1,0:T(8,128)(2,1)S(1)}, u32[]{:S(2)}) copy-start(bf16[1,128,1024]{2,1,0:T(8,128)(2,1)S(1)} %get-tuple-element.88) | copy-start | bytes 786436
  70.0 3.5 %collective-permute-start.9 = (bf16[4,128,1536]{2,1,0:T(8,128)(2,1)S(1)}, bf16[4,128,1536]{2,1,0:T(8,128)(2,1)S(1)}, u32[]{:S(2)}, u32[]{:S(2)}) collective-permute-start(bf16[4,128,1536]{2,1,0:T(8,128)(2,1)S(1)} %weights.6.refs_9_), channel_id=1, source_target_pairs={{0,4},{4,0},{8,12},{12,8},{16,20},{20,16},{24,28},{28,24},{1,5},{5... | collective-permute-start | bytes 4718600 | tf_op jit(solution)/shard_map/ppermute | solution.py:445
  73.9 18.7 %copy-start.6 = (bf16[1,512,1024]{2,1,0:T(8,128)(2,1)S(1)}, bf16[1,512,1024]{2,1,0:T(8,128)(2,1)}, u32[]{:S(2)}) copy-start(bf16[1,512,1024]{2,1,0:T(8,128)(2,1)} %param.5) | copy-start | bytes 3145732
  73.9 18.6 %copy-start.15 = (bf16[512,1024]{1,0:T(8,128)(2,1)S(1)}, bf16[512,1024]{1,0:T(8,128)(2,1)}, u32[]{:S(2)}) copy-start(bf16[512,1024]{1,0:T(8,128)(2,1)} %refs_1_.31) | copy-start | bytes 3145732
  73.9 20.3 %collective-permute-start.12 = (bf16[2,128,1536]{2,1,0:T(8,128)(2,1)S(1)}, bf16[2,128,1536]{2,1,0:T(8,128)(2,1)S(1)}, u32[]{:S(2)}, u32[]{:S(2)}) collective-permute-start(bf16[2,128,1536]{2,1,0:T(8,128)(2,1)S(1)} %get-tuple-element.85.refs_3_), channel_id=1, source_target_pairs={{0,8},{4,20},{8,0},{12,28},{16,24},{20,4},{24,16},{28,12},{1,9},{5... | collective-permute-start | bytes 2359304 | tf_op jit(solution)/shard_map/ppermute | solution.py:445
  75.4 17.1 %collective-permute-start.11 = (bf16[512,512]{1,0:T(8,128)(2,1)S(1)}, bf16[512,512]{1,0:T(8,128)(2,1)S(1)}, u32[]{:S(2)}, u32[]{:S(2)}) collective-permute-start(bf16[512,512]{1,0:T(8,128)(2,1)S(1)} %get-tuple-element.82.refs_2_.refs_8_), channel_id=1, source_target_pairs={{0,1},{1,2},{2,3},{4,5},{5,6},{6,7},{8,9},{9,10},{10,11},{12,13},{... | collective-permute-start | bytes 1572872 | tf_op jit(solution)/shard_map/ppermute | solution.py:26
  83.7 32.1 %collective-permute-start.14 = (bf16[512,1024]{1,0:T(8,128)(2,1)}, bf16[512,1024]{1,0:T(8,128)(2,1)}, u32[]{:S(2)}, u32[]{:S(2)}) collective-permute-start(bf16[512,1024]{1,0:T(8,128)(2,1)} %far.1.refs_3_), channel_id=1, source_target_pairs={{1,0},{2,1},{3,2},{5,4},{6,5},{7,6},{9,8},{10,9},{11,10},{13,12},{... | collective-permute-start | bytes 3145736 | tf_op jit(solution)/shard_map/ppermute | solution.py:26
  85.2 7.3 %collective-permute-start.10 = (bf16[1,128,1024]{2,1,0:T(8,128)(2,1)S(1)}, bf16[1,128,1024]{2,1,0:T(8,128)(2,1)S(1)}, u32[]{:S(2)}, u32[]{:S(2)}) collective-permute-start(bf16[1,128,1024]{2,1,0:T(8,128)(2,1)S(1)} %get-tuple-element.84.refs_9_), channel_id=1, source_target_pairs={{0,16},{4,12},{8,24},{12,4},{16,0},{20,28},{24,8},{28,20},{1,17},{... | collective-permute-start | bytes 786440 | tf_op jit(solution)/shard_map/ppermute | solution.py:445
  92.5 3.8 %copy-start.16 = (bf16[1,128,1024]{2,1,0:T(8,128)(2,1)}, bf16[1,128,1024]{2,1,0:T(8,128)(2,1)S(1)}, u32[]{:S(2)}) copy-start(bf16[1,128,1024]{2,1,0:T(8,128)(2,1)S(1)} %collective-permute-done.10.refs_4_) | copy-start | bytes 786436
  94.2 1.2 copy-start.7
  97.1 8.0 %collective-permute-start.13 = (bf16[1,128,1536]{2,1,0:T(8,128)(2,1)}, bf16[1,128,1536]{2,1,0:T(8,128)(2,1)S(1)}, u32[]{:S(2)}, u32[]{:S(2)}) collective-permute-start(bf16[1,128,1536]{2,1,0:T(8,128)(2,1)} %get-tuple-element.87.refs_8_), channel_id=1, source_target_pairs={{0,16},{4,12},{8,24},{12,4},{16,0},{20,28},{24,8},{28,20},{1,17},{... | collective-permute-start | bytes 1179656 | tf_op jit(solution)/shard_map/ppermute | solution.py:445
  98.7 18.5 %copy-start.18 = (bf16[512,512]{1,0:T(8,128)(2,1)S(1)}, bf16[512,512]{1,0:T(8,128)(2,1)}, u32[]{:S(2)}) copy-start(bf16[512,512]{1,0:T(8,128)(2,1)} %copy-done.17) | copy-start | bytes 1572868
  99.8 15.4 %collective-permute-start.15 = (bf16[32,1024]{1,0:T(8,128)(2,1)S(1)}, bf16[32,1024]{1,0:T(8,128)(2,1)S(1)}, u32[]{:S(2)}, u32[]{:S(2)}) collective-permute-start(bf16[32,1024]{1,0:T(8,128)(2,1)S(1)} %get-tuple-element.98), channel_id=1, source_target_pairs={{0,1},{1,0},{2,3},{3,2},{4,5},{5,4},{6,7},{7,6},{8,9},{9,8},{10,11... | collective-permute-start | bytes 196616 | tf_op jit(solution)/shard_map/ppermute | solution.py:458
  106.2 19.1 %collective-permute-start.18 = (bf16[32,1536]{1,0:T(8,128)(2,1)S(1)}, bf16[32,1536]{1,0:T(8,128)(2,1)S(1)}, u32[]{:S(2)}, u32[]{:S(2)}) collective-permute-start(bf16[32,1536]{1,0:T(8,128)(2,1)S(1)} %get-tuple-element.94), channel_id=1, source_target_pairs={{0,1},{1,0},{2,3},{3,2},{4,5},{5,4},{6,7},{7,6},{8,9},{9,8},{10,11... | collective-permute-start | bytes 294920 | tf_op jit(solution)/shard_map/ppermute | solution.py:458
  108.7 16.6 %collective-permute-start.19 = (bf16[32,1536]{1,0:T(8,128)(2,1)S(1)}, bf16[32,1536]{1,0:T(8,128)(2,1)S(1)}, u32[]{:S(2)}, u32[]{:S(2)}) collective-permute-start(bf16[32,1536]{1,0:T(8,128)(2,1)S(1)} %get-tuple-element.93), channel_id=1, source_target_pairs={{0,2},{1,3},{2,0},{3,1},{4,6},{5,7},{6,4},{7,5},{8,10},{9,11},{10,... | collective-permute-start | bytes 294920 | tf_op jit(solution)/shard_map/ppermute | solution.py:458
  111.6 13.8 %collective-permute-start.20 = (bf16[32,1536]{1,0:T(8,128)(2,1)S(1)}, bf16[32,1536]{1,0:T(8,128)(2,1)S(1)}, u32[]{:S(2)}, u32[]{:S(2)}) collective-permute-start(bf16[32,1536]{1,0:T(8,128)(2,1)S(1)} %get-tuple-element.92), channel_id=1, source_target_pairs={{0,3},{1,2},{2,1},{3,0},{4,7},{5,6},{6,5},{7,4},{8,11},{9,10},{10,... | collective-permute-start | bytes 294920 | tf_op jit(solution)/shard_map/ppermute | solution.py:458
  115.3 10.1 %collective-permute-start.16 = (bf16[32,1024]{1,0:T(8,128)(2,1)S(1)}, bf16[32,1024]{1,0:T(8,128)(2,1)S(1)}, u32[]{:S(2)}, u32[]{:S(2)}) collective-permute-start(bf16[32,1024]{1,0:T(8,128)(2,1)S(1)} %get-tuple-element.97), channel_id=1, source_target_pairs={{0,2},{1,3},{2,0},{3,1},{4,6},{5,7},{6,4},{7,5},{8,10},{9,11},{10,... | collective-permute-start | bytes 196616 | tf_op jit(solution)/shard_map/ppermute | solution.py:458
  115.8 9.5 %collective-permute-start.17 = (bf16[32,1024]{1,0:T(8,128)(2,1)S(1)}, bf16[32,1024]{1,0:T(8,128)(2,1)S(1)}, u32[]{:S(2)}, u32[]{:S(2)}) collective-permute-start(bf16[32,1024]{1,0:T(8,128)(2,1)S(1)} %get-tuple-element.96), channel_id=1, source_target_pairs={{0,3},{1,2},{2,1},{3,0},{4,7},{5,6},{6,5},{7,4},{8,11},{9,10},{10,... | collective-permute-start | bytes 196616 | tf_op jit(solution)/shard_map/ppermute | solution.py:458
  117.1 2.2 %copy-start.3 = (bf16[1024,2048]{1,0:T(8,128)(2,1)S(1)}, bf16[1024,2048]{1,0:T(8,128)(2,1)}, u32[]{:S(2)}) copy-start(bf16[1024,2048]{1,0:T(8,128)(2,1)} %refs_6_.1) | copy-start | bytes 12582916
  119.3 2.4 %copy-start.12 = (bf16[1,512,1024]{2,1,0:T(8,128)(2,1)S(1)}, bf16[1,512,1024]{2,1,0:T(8,128)(2,1)}, u32[]{:S(2)}) copy-start(bf16[1,512,1024]{2,1,0:T(8,128)(2,1)} %param.9) | copy-start | bytes 3145732
  125.3 1.2 copy-start.4
  (9 other events, 8.9 us)
where the time goes:
time: 128 us; the launch traced here: 127 us
  Pallas kernels  43.9 us (34%)
  starting transfers between devices  43.6 us (34%)
  waiting for transfers between devices  19.7 us (15%)
  local copies, waits for them, and re-layouts  16.7 us (13%)
  other arithmetic  2.38 us (2%)
    pallas_call x29, Pallas kernels, call(): pl.pallas_call(body, grid=(1,), out_shape=outs, in_specs=(specs or [VMEM]...  43.9 us
    ppermute x9, starting transfers between devices, shift(): return lax.ppermute(value, 'seq', pairs)  27.9 us
    unnamed x72, local copies, waits for them, and re-layouts  15.3 us
    ppermute x9, waiting for transfers between devices, shift(): return lax.ppermute(value, 'seq', pairs)  11.1 us
    ppermute x6, starting transfers between devices, over_seq(): lax.ppermute(chunk(me ^ r).astype(BF16), 'seq', [(i, i ^ r) for i in rang...  9.82 us
    ppermute x6, starting transfers between devices, swap_dp(): return lax.ppermute(value, 'dp', pairs)  5.9 us
    ppermute x6, waiting for transfers between devices, swap_dp(): return lax.ppermute(value, 'dp', pairs)  4.88 us
    ppermute x6, waiting for transfers between devices, over_seq(): lax.ppermute(chunk(me ^ r).astype(BF16), 'seq', [(i, i ^ r) for i in rang...  3.69 us
  transfers between devices with their start and end apart: 21, of which 8 were waited for; matrix products, arithmetic and copies ran while one was open for 3% of the time, Pallas kernels for 32%

commit v1 on v0

--- a/solution.py
+++ b/solution.py
@@ -26,7 +26,9 @@
     return lax.ppermute(value, "seq", pairs)
 
 
-def call(kernel, outs, args, specs=None, scratch=(), flops=0, nbytes=0, name=None, after=(), weight=8):
+def call(
+    kernel, outs, args, specs=None, scratch=(), flops=0, nbytes=0, name=None, after=(), weight=8, out_specs=None
+):
     first, last = len(args), len(args) + len(after)
 
     def body(*refs):
@@ -37,7 +39,7 @@
         grid=(1,),
         out_shape=outs,
         in_specs=(specs or [VMEM] * first) + [pl.BlockSpec(memory_space=pl.ANY)] * len(after),
-        out_specs=jax.tree.map(lambda _: VMEM, outs),
+        out_specs=out_specs or jax.tree.map(lambda _: VMEM, outs),
         scratch_shapes=scratch,
         compiler_params=pltpu.CompilerParams(vmem_limit_bytes=GRANT),
         cost_estimate=pl.CostEstimate(
@@ -333,7 +335,8 @@
     out_ref[...] = dot_nt(x_ref[...], w_ref[...]).astype(out_ref.dtype)
 
 
-def output_kernel(gated_ref, w_ref, tokens_ref, out_ref):
+def output_kernel(gated_ref, w_ref, tokens_ref, out_ref, flag_ref):
+    flag_ref[...] = jnp.zeros_like(flag_ref)
     out_ref[...] = (dot(gated_ref[...], w_ref[...]) + tokens_ref[...].astype(F32)).astype(BF16)
 
 
@@ -344,25 +347,64 @@
     ).astype(out_ref.dtype)
 
 
-def near_kernel(gu_ref, gvk_ref, gq_ref, wu_ref, wv_ref, wq_ref, wk_ref, *refs):
+def near_kernel(gu_ref, gvk_ref, gq_ref, wu_ref, wv_ref, wq_ref, wk_ref, out_ref):
     width = wv_ref.shape[1]
-    grad_q = gq_ref[...].astype(F32)
-    for far_ref in refs[:-1]:
-        grad_q = grad_q + far_ref[...].astype(F32)
-    refs[-1][...] = (
+    out_ref[...] = (
         dot_nt(gu_ref[...], wu_ref[...])
         + dot_nt(gvk_ref[:, :width], wv_ref[...])
-        + dot_nt(grad_q.astype(BF16), wq_ref[...])
+        + dot_nt(gq_ref[...], wq_ref[...])
         + dot_nt(gvk_ref[:, width:], wk_ref[...])
     )
 
 
-def tokens_kernel(tokens_ref, cotangent_ref, near_ref, *refs):
+def mid_kernel(count, near_ref, tokens_ref, cotangent_ref, *refs):
+    far_refs, refs = refs[:count], refs[count:]
+    if count:
+        w_ref, sum_ref, scaled_ref, inverse_ref, held_ref, sem = refs
+        width = held_ref.shape[1]
+        fetch = pltpu.make_async_copy(w_ref.at[:, 2 * width : 3 * width], held_ref, sem)
+        fetch.start()
+    else:
+        sum_ref, scaled_ref, inverse_ref = refs
+    scaled, inverse = centred(tokens_ref[...].astype(F32))
+    scaled_ref[...] = scaled.astype(BF16)
+    inverse_ref[...] = jnp.broadcast_to(inverse, inverse_ref.shape)
     grad = near_ref[...]
-    for far_ref in refs[:-1]:
-        grad = grad + far_ref[...].astype(F32)
-    scaled, inverse = centred(tokens_ref[...].astype(F32))
-    refs[-1][...] = (back(scaled, inverse, grad) + cotangent_ref[...].astype(F32)).astype(BF16)
+    if count:
+        fetch.wait()
+        for gq_ref in far_refs:
+            grad = grad + dot_nt(gq_ref[...], held_ref[...])
+    sum_ref[...] = back(scaled, inverse, grad) + cotangent_ref[...].astype(F32)
+
+
+def tokens_kernel(count, sum_ref, scaled_ref, inverse_ref, *refs):
+    far_refs, (out_ref, flag_ref, far, out, far_sem, out_sem) = refs[:count], refs[count:]
+    flag_ref[...] = jnp.zeros_like(flag_ref)
+    chunks = far_sem.shape[1]
+    step = out.shape[0] // chunks
+
+    def rows(c):
+        return pl.ds(c * step, step)
+
+    fetches = [
+        [pltpu.make_async_copy(ref.at[rows(c)], far.at[i, rows(c)], far_sem.at[i, c]) for i, ref in enumerate(far_refs)]
+        for c in range(chunks)
+    ]
+    puts = [pltpu.make_async_copy(out.at[rows(c)], out_ref.at[rows(c)], out_sem.at[c]) for c in range(chunks)]
+    for fetch in fetches:
+        for copy in fetch:
+            copy.start()
+    for c in range(chunks):
+        for copy in fetches[c]:
+            copy.wait()
+        grad = far[0, rows(c)].astype(F32)
+        for i in range(1, count):
+            grad = grad + far[i, rows(c)].astype(F32)
+        part = back(scaled_ref[rows(c), :].astype(F32), inverse_ref[rows(c), :1], grad)
+        out[rows(c)] = (sum_ref[rows(c), :] + part).astype(BF16)
+        puts[c].start()
+    for put in puts:
+        put.wait()
 
 
 def orders(dp):
@@ -445,20 +487,53 @@
     return lax.ppermute(value, "dp", pairs)
 
 
-def over_seq(mine, other):
-    n_seq, me = lax.axis_size("seq"), lax.axis_index("seq")
-    rows, width = mine.shape[1] // n_seq, mine.shape[2]
-
-    def chunk(index):
-        start = (0, index * rows, 0)
-        a = lax.dynamic_slice(mine, start, (1, rows, width))[0].astype(F32)
-        return a + lax.dynamic_slice(other, start, (1, rows, width))[0].astype(F32)
-
-    far = [
-        lax.ppermute(chunk(me ^ r).astype(BF16), "seq", [(i, i ^ r) for i in range(n_seq)])
-        for r in range(1, n_seq)
-    ]
-    return [chunk(me), *far]
+def first_share_kernel(count, place_ref, mine_ref, other_ref, keep_ref, send_ref, sum_ref):
+    rows = sum_ref.shape[0] // count
+    sum_ref[...] = mine_ref[0].astype(F32) + other_ref[0].astype(F32)
+
+    def block(r):
+        return sum_ref[pl.ds(pl.multiple_of((place_ref[1] ^ r) * rows, rows), rows), :]
+
+    keep_ref[...] = jnp.concatenate([block(r) for r in range(0, count, 2)], axis=0)
+    send_ref[...] = jnp.concatenate([block(r) for r in range(1, count, 2)], axis=0).astype(BF16)
+
+
+def next_share_kernel(count, mine_ref, other_ref, keep_ref, send_ref):
+    rows = mine_ref.shape[0] // count
+    total = mine_ref[...] + other_ref[...].astype(F32)
+    blocks = [total[r * rows : (r + 1) * rows] for r in range(count)]
+    keep_ref[...] = jnp.concatenate(blocks[::2], axis=0)
+    send_ref[...] = jnp.concatenate(blocks[1::2], axis=0).astype(BF16)
+
+
+def swap_seq(value, bit):
+    return lax.ppermute(value, "seq", [(i, i ^ bit) for i in range(lax.axis_size("seq"))])
+
+
+def first_share(place, mine, other, after=()):
+    rows, width = mine.shape[1], mine.shape[2]
+    keep, send = call(
+        functools.partial(first_share_kernel, lax.axis_size("seq")),
+        [like(rows // 2, width, F32), like(rows // 2, width, BF16)],
+        [place, mine, other],
+        [SMEM, VMEM, VMEM],
+        scratch=[pltpu.VMEM((rows, width), F32)],
+        name="share",
+        after=after,
+    )
+    return keep, swap_seq(send, 1)
+
+
+def next_share(count, mine, other, after=()):
+    rows, width = mine.shape
+    keep, send = call(
+        functools.partial(next_share_kernel, count),
+        [like(rows // 2, width, F32), like(rows // 2, width, BF16)],
+        [mine, other],
+        name="share",
+        after=after,
+    )
+    return keep, swap_seq(send, lax.axis_size("seq") // count)
 
 
 def total_kernel(*refs):
@@ -553,21 +628,15 @@
             functools.partial(gate_kernel, 0, 0), [like(n, width, BF16)] * 3, gate_args, name="gate"
         )
         grad_q, rest = None, (0, 1)
-    early = [[(upstream, gated)], [(normed, grad_u)]]
-    early_send = weight_half(place, early, 1)
-    early_other = swap_dp(early_send, 0)
     grad_q, grad_vk = backward(
         users, "own", query, (keys, keys_t), values, grad_attended, add_q=grad_q, slope_k=slope_vk,
-        after=[early_send] + ([next_normed] if down else []),
-    )
-    early_mine = weight_half(place, early, 0, after=[grad_vk])
-    early_send, early_mine = halve(early_mine, early_other)
-    early_other = swap_dp(early_send, 1)
+        after=[next_normed] if down else [],
+    )
     for by, (_, slope, far_values, far_keys) in enumerate(pieces, 1):
         grad_q, far_sums[by - 1] = backward(
             users, "near", query, far_keys, far_values, grad_attended, 0, by, add_q=grad_q,
             add_k=far_sums[by - 1], slope_q=slope_q if by == up else None,
-            slope_k=None if by <= down else slope, chunks=rest, after=[early_send],
+            slope_k=None if by <= down else slope, chunks=rest,
         )
     if down:
         next_slope, _ = project(next_normed, w_in, [2], False, after=[grad_q])
@@ -584,11 +653,7 @@
     late = [vk_pairs, q_pairs]
     phases = range(2, lax.axis_size("dp").bit_length() - 1)
     order = [next_q] if down else [grad_q]
-    for phase in phases:
-        early_send, early_mine = halve(early_mine, early_other, after=order)
-        early_other = swap_dp(early_send, phase)
-        order = [early_send]
-    late_send = weight_half(place, late, 1, after=order, weight=1)
+    late_send = weight_half(place, late, 1, weight=1)
     late_other = swap_dp(late_send, 0)
     late_mine = weight_half(place, late, 0, after=[late_send], weight=1)
     late_send, late_mine = halve(late_mine, late_other)
@@ -608,37 +673,70 @@
     order = far_parts
     far_parts = [shift(part, -by) for by, part in enumerate(far_parts, 1)]
     next_q = [shift(next_q, up)] if down else []
-    output = call(
-        output_kernel, like(n, d, BF16), [gated, w_out, tokens], flops=2 * n * d * width,
-        name="output", weight=0, after=[*order, early_other, *next_q],
-    )
-    early_sum = over_seq(early_mine, early_other)
-    order = [output]
+    early = [[(upstream, gated)], [(normed, grad_u)]]
+    early_send = weight_half(place, early, 1, after=order, weight=1)
+    early_other = swap_dp(early_send, 0)
+    early_mine = weight_half(place, early, 0, after=[early_send], weight=1)
+    early_send, early_mine = halve(early_mine, early_other)
+    early_other = swap_dp(early_send, 1)
+    order = [early_send]
+    near = call(
+        near_kernel,
+        like(n, d, F32),
+        [grad_u, grad_vk, grad_q] + [w_in] * 4,
+        [VMEM] * 3 + [columns(d, width, b) for b in range(4)],
+        flops=8 * n * d * width,
+        name="near", weight=1,
+        after=order,
+    )
+    output, written = call(
+        output_kernel, [like(n, d, BF16), like(8, 128, F32)], [gated, w_out, tokens], flops=2 * n * d * width,
+        name="output", weight=1, after=[near],
+    )
+    order = [written]
     for phase in phases:
         late_send, late_mine = halve(late_mine, late_other, after=order)
         late_other = swap_dp(late_send, phase)
-        order = [late_send]
-    late_sum = over_seq(late_mine, late_other)
-    near = call(
-        near_kernel,
-        like(n, d, F32),
-        [grad_u, grad_vk, grad_q] + [w_in] * 4 + next_q,
-        [VMEM] * 3 + [columns(d, width, b) for b in range(4)] + [VMEM] * len(next_q),
-        flops=8 * n * d * width,
-        name="near", weight=0,
-        after=[*order, late_other],
-    )
-    grad_tokens = call(
-        tokens_kernel, like(n, d, BF16), [tokens, upstream, near, *far_parts], name="tokens", weight=0,
-        after=[late_other],
-    )
+        early_send, early_mine = halve(early_mine, early_other, after=[late_send])
+        early_other = swap_dp(early_send, phase)
+        order = [early_send]
+    late_sum = first_share(place, late_mine, late_other, order)
+    early_sum = first_share(place, early_mine, early_other, late_sum[:1])
+    mid, scaled, inverse = call(
+        functools.partial(mid_kernel, len(next_q)),
+        [like(n, d, F32), like(n, d, BF16), like(n, 128, F32)],
+        [near, tokens, upstream, *next_q] + [w_in] * bool(next_q),
+        [VMEM] * (3 + len(next_q)) + [pl.BlockSpec(memory_space=pl.ANY)] * bool(next_q),
+        scratch=[pltpu.VMEM((d, width), BF16), pltpu.SemaphoreType.DMA] if next_q else [],
+        name="mid", weight=0,
+        after=early_sum[:1],
+    )
+    count = len(far_parts)
+    grad_tokens, written = call(
+        functools.partial(tokens_kernel, count),
+        [like(n, d, BF16), like(8, 128, F32)],
+        [mid, scaled, inverse, *far_parts],
+        [VMEM] * 3 + [pl.BlockSpec(memory_space=pl.ANY)] * count,
+        scratch=[
+            pltpu.VMEM((count, n, d), BF16), pltpu.VMEM((n, d), BF16),
+            pltpu.SemaphoreType.DMA((count, 4)), pltpu.SemaphoreType.DMA((4,)),
+        ],
+        name="tokens", weight=0,
+        after=early_sum[:1],
+        out_specs=[pl.BlockSpec(memory_space=pl.ANY), VMEM],
+    )
+    count = n_seq // 2
+    while count > 1:
+        early_sum = next_share(count, *early_sum, after=[written, late_sum[0]])
+        late_sum = next_share(count, *late_sum, after=early_sum[:1])
+        count //= 2
     rows = early_sum[0].shape[0]
     total_in, out_w = call(
         total_kernel,
         [like(rows, 4 * width, F32), like(rows, width, F32)],
         [*early_sum, *late_sum],
         name="total",
-        after=[grad_tokens],
+        after=[written],
     )
     return (output[None], grad_tokens[None], total_in, out_w.T)
 

time: 128 us -> 121 us (0.945)
  local copies, waits for them, and re-layouts: 16.7 us -> 11.2 us
  other arithmetic: 2.38 us -> 0.07 us
  waiting for transfers between devices: 19.7 us -> 21.2 us
    ppermute x9, waiting for transfers between devices: 11.1 us -> 5.38 us  [shift(): return lax.ppermute(value, 'seq', pairs)]
    unnamed x72 -> x50, local copies, waits for them, and re-layouts: 15.3 us -> 9.9 us
    ppermute x6 -> x4, waiting for transfers between devices: 3.69 us -> 8.91 us  [swap_seq(): lax.ppermute(value, 'seq', [(i, i ^ bit) for i in range(lax.axis_size('se...]
    convert_element_type x2 -> x0, other arithmetic: 2.3 us -> none  [over_seq(): chunk(me ^ r).astype(BF16)]
    ppermute x6, waiting for transfers between devices: 4.88 us -> 6.9 us  [swap_dp(): return lax.ppermute(value, 'dp', pairs)]
    pallas_call x29 -> x34, Pallas kernels: 43.9 us -> 43.9 us  [call(): pl.pallas_call(body, grid=(1,), out_shape=outs, in_specs=(specs or [VMEM]...]
    ppermute x6 -> x4, starting transfers between devices: 9.82 us -> 9.86 us  [swap_seq(): lax.ppermute(value, 'seq', [(i, i ^ bit) for i in range(lax.axis_size('se...]
  transfers between devices with their start and end apart: 21 -> 19, of which waited for: 8 -> 9; matrix products, arithmetic and copies ran while one was open for 3% -> 1% of each run, Pallas kernels for 32% -> 30%
where the time goes in v1:
time: 121 us
  Pallas kernels  43.9 us (36%)
  starting transfers between devices  43.6 us (36%)
  waiting for transfers between devices  21.2 us (18%)
  local copies, waits for them, and re-layouts  11.2 us (9%)
    pallas_call x34, Pallas kernels, call(): pl.pallas_call(body, grid=(1,), out_shape=outs, in_specs=(specs or [VMEM]...  43.9 us
    ppermute x9, starting transfers between devices, shift(): return lax.ppermute(value, 'seq', pairs)  28.3 us
    unnamed x50, local copies, waits for them, and re-layouts  9.9 us
    ppermute x4, starting transfers between devices, swap_seq(): lax.ppermute(value, 'seq', [(i, i ^ bit) for i in range(lax.axis_size('se...  9.86 us
    ppermute x4, waiting for transfers between devices, swap_seq(): lax.ppermute(value, 'seq', [(i, i ^ bit) for i in range(lax.axis_size('se...  8.91 us
    ppermute x6, waiting for transfers between devices, swap_dp(): return lax.ppermute(value, 'dp', pairs)  6.9 us
    ppermute x6, starting transfers between devices, swap_dp(): return lax.ppermute(value, 'dp', pairs)  5.52 us
    ppermute x9, waiting for transfers between devices, shift(): return lax.ppermute(value, 'seq', pairs)  5.38 us
  transfers between devices with their start and end apart: 19, of which 9 were waited for; matrix products, arithmetic and copies ran while one was open for 1% of the time, Pallas kernels for 30%

profile of v1, /device:TPU:0, one launch (start us, length us, event | category | flops | bytes accessed | tf_op | source)
XLA Modules:
  0.0 121.2 jit_solution(13847335352072911947)
XLA Ops:
  0.6 5.9 %collective-permute-start.1 = (bf16[512,1024]{1,0:T(8,128)(2,1)}, bf16[512,1024]{1,0:T(8,128)(2,1)}, u32[]{:S(2)}, u32[]{:S(2)}) collective-permute-start(bf16[512,1024]{1,0:T(8,128)(2,1)} %bitcast.12), channel_id=1, source_target_pairs={{0,1},{1,2},{2,3},{4,5},{5,6},{6,7},{8,9},{9,10},{10,11},{12,13},{... | collective-permute-start | bytes 3145736 | tf_op jit(solution)/shard_map/ppermute | solution.py:26
  6.6 2.2 %copy-done = bf16[1024,2048]{1,0:T(8,128)(2,1)S(1)} copy-done((bf16[1024,2048]{1,0:T(8,128)(2,1)S(1)}, bf16[1024,2048]{1,0:T(8,128)(2,1)}, u32[]{:S(2)}) %copy-start) | copy-done | bytes 4194328
  8.8 1.2 %copy-done.4 = bf16[1,512,1024]{2,1,0:T(8,128)(2,1)S(1)} copy-done((bf16[1,512,1024]{2,1,0:T(8,128)(2,1)S(1)}, bf16[1,512,1024]{2,1,0:T(8,128)(2,1)}, u32[]{:S(2)}) %copy-start.4) | copy-done | bytes 1048600
  10.0 2.3 %project.5 = (bf16[512,1024]{1,0:T(8,128)(2,1)S(1)}, bf16[512,512]{1,0:T(8,128)(2,1)S(1)}, bf16[512,512]{1,0:T(8,128)(2,1)S(1)}, bf16[512,1024]{1,0:T(8,128)(2,1)}, bf16[512,512]{1,0:T(8,128)(2,1)}) custom-call(bf16[512,1024]{1,0:T(8,128)(2,1)S(1)} %bitcast.13, bf16[1024,2048]{1,0:T(8,128)(2,1)S(1)} %copy-done), custom_call_target="tpu_custom_call" | custom-call | flops 4294967296 | bytes 2097152 | tf_op jit(solution)/shard_map/project/pallas_call | solution.py:37
  12.3 1.3 %collective-permute-start = (bf16[512,512]{1,0:T(8,128)(2,1)}, bf16[512,512]{1,0:T(8,128)(2,1)}, u32[]{:S(2)}, u32[]{:S(2)}) collective-permute-start(bf16[512,512]{1,0:T(8,128)(2,1)} %get-tuple-element.63), channel_id=1, source_target_pairs={{1,0},{2,1},{3,2},{5,4},{6,5},{7,6},{9,8},{10,9},{11,10},{13,12},{... | collective-permute-start | bytes 1572872 | tf_op jit(solution)/shard_map/ppermute | solution.py:26
  13.5 1.3 %collective-permute-start.4 = (bf16[512,1024]{1,0:T(8,128)(2,1)}, bf16[512,1024]{1,0:T(8,128)(2,1)S(1)}, u32[]{:S(2)}, u32[]{:S(2)}) collective-permute-start(bf16[512,1024]{1,0:T(8,128)(2,1)} %get-tuple-element.84), channel_id=1, source_target_pairs={{1,0},{2,1},{3,2},{5,4},{6,5},{7,6},{9,8},{10,9},{11,10},{13,12},{... | collective-permute-start | bytes 3145736 | tf_op jit(solution)/shard_map/ppermute | solution.py:26
  16.6 1.7 %project.7 = (bf16[512,1024]{1,0:T(8,128)(2,1)S(1)}, bf16[512,512]{1,0:T(8,128)(2,1)S(1)}, bf16[512,512]{1,0:T(8,128)(2,1)S(1)}) custom-call(bf16[512,1024]{1,0:T(8,128)(2,1)S(1)} %get-tuple-element.65.refs_0_.refs_1_.refs_5_.refs_3_, bf16[1024,2048]{1,0:T(8,128)(2,1)S(1)} %copy-done.1, bf16[1024,2048]{1,0:T(8,128)(2,1)S(1)} %copy-done.1, ...), custom_call_target="tpu_custom_call" | custom-call | flops 8589934592 | bytes 3145728 | tf_op jit(solution)/shard_map/project/pallas_call | solution.py:37
  20.0 1.0 copy-done.23
  21.0 1.3 %copy.11.refs_3_ = s32[2048,1]{1,0:T(8,128)} copy(s32[2048,1]{0,1:T(1,128)S(1)} %bitcast.16) | data formatting | bytes 16384 | tf_op jit(solution)/shard_map/reshape;squeeze | solution.py:564
  22.4 1.2 %copy-done.7 = bf16[512,1024]{1,0:T(8,128)(2,1)S(1)} copy-done((bf16[512,1024]{1,0:T(8,128)(2,1)S(1)}, bf16[512,1024]{1,0:T(8,128)(2,1)}, u32[]{:S(2)}) %copy-start.7) | copy-done | bytes 1048600
  23.6 1.0 copy-done.21
  26.2 2.2 %forward.4 = (f32[512,512]{1,0:T(8,128)S(1)}, bf16[512,512]{1,0:T(8,128)(2,1)S(1)}) custom-call(s32[2]{0:T(128)S(1)} %pad_add_fusion.refs_0_, s32[1,2048]{1,0:T(1,128)S(1)} %copy-done.13, s32[1,2048]{1,0:T(1,128)S(1)} %copy-done.13, s32[2048,1]{1,0:T(8,128)S(1)} %copy-done.6, bf16[512,512]{1,0:T(8,128)(2,1)S(1)} %copy-done.17, ...), custom_call_target="tpu_custom_call" | custom-call | flops 4294967296 | bytes 2621440 | tf_op jit(solution)/shard_map/forward/pallas_call | solution.py:37
  28.4 3.3 %project.8 = (bf16[512,1024]{1,0:T(8,128)(2,1)S(1)}, bf16[512,1024]{1,0:T(8,128)(2,1)S(1)}, bf16[512,512]{1,0:T(8,128)(2,1)S(1)}, bf16[512,512]{1,0:T(8,128)(2,1)S(1)}) custom-call(bf16[512,1024]{1,0:T(8,128)(2,1)} %collective-permute-done.1.refs_0_, bf16[1024,2048]{1,0:T(8,128)(2,1)S(1)} %copy-done.2, bf16[1024,2048]{1,0:T(8,128)(2,1)S(1)} %copy-done.2, ...), custom_call_target="tpu_custom_call" | custom-call | flops 8589934592 | bytes 3145728 | tf_op jit(solution)/shard_map/project/pallas_call | solution.py:37
  31.8 1.2 forward.5.refs_7_
  32.9 5.2 %collective-permute-start.3 = (bf16[256,512]{1,0:T(8,128)(2,1)S(1)}, bf16[256,512]{1,0:T(8,128)(2,1)S(1)}, u32[]{:S(2)}, u32[]{:S(2)}) collective-permute-start(bf16[256,512]{1,0:T(8,128)(2,1)S(1)} %forward.5.refs_7_), channel_id=1, source_target_pairs={{0,1},{1,2},{2,3},{4,5},{5,6},{6,7},{8,9},{9,10},{10,11},{12,13},{... | collective-permute-start | bytes 786440 | tf_op jit(solution)/shard_map/ppermute | solution.py:26
  38.1 1.2 forward.6.refs_8_
  39.3 5.4 %collective-permute-start.2 = (bf16[256,512]{1,0:T(8,128)(2,1)S(1)}, bf16[256,512]{1,0:T(8,128)(2,1)S(1)}, u32[]{:S(2)}, u32[]{:S(2)}) collective-permute-start(bf16[256,512]{1,0:T(8,128)(2,1)S(1)} %forward.6.refs_8_), channel_id=1, source_target_pairs={{0,1},{1,2},{2,3},{4,5},{5,6},{6,7},{8,9},{9,10},{10,11},{12,13},{... | collective-permute-start | bytes 786440 | tf_op jit(solution)/shard_map/ppermute | solution.py:26
  46.1 1.3 %collective-permute-start.5 = (bf16[256,512]{1,0:T(8,128)(2,1)S(1)}, bf16[256,512]{1,0:T(8,128)(2,1)S(1)}, u32[]{:S(2)}, u32[]{:S(2)}) collective-permute-start(bf16[256,512]{1,0:T(8,128)(2,1)S(1)} %get-tuple-element.74.refs_8_.refs_5_), channel_id=1, source_target_pairs={{1,0},{2,1},{3,2},{5,4},{6,5},{7,6},{9,8},{10,9},{11,10},{13,12},{... | collective-permute-start | bytes 786440 | tf_op jit(solution)/shard_map/ppermute | solution.py:26
  47.4 1.0 backward.4
  48.4 1.6 %collective-permute-done.2.refs_0_ = bf16[256,512]{1,0:T(8,128)(2,1)S(1)} collective-permute-done((bf16[256,512]{1,0:T(8,128)(2,1)S(1)}, bf16[256,512]{1,0:T(8,128)(2,1)S(1)}, u32[]{:S(2)}, u32[]{:S(2)}) %collective-permute-start.2) | collective-permute-done | bytes 262176 | tf_op jit(solution)/shard_map/ppermute | solution.py:26
  50.6 1.3 %collective-permute-start.6 = (bf16[256,512]{1,0:T(8,128)(2,1)S(1)}, bf16[256,512]{1,0:T(8,128)(2,1)S(1)}, u32[]{:S(2)}, u32[]{:S(2)}) collective-permute-start(bf16[256,512]{1,0:T(8,128)(2,1)S(1)} %get-tuple-element.90), channel_id=1, source_target_pairs={{1,0},{2,1},{3,2},{5,4},{6,5},{7,6},{9,8},{10,9},{11,10},{13,12},{... | collective-permute-start | bytes 786440 | tf_op jit(solution)/shard_map/ppermute | solution.py:26
  51.9 3.3 %backward.5 = (f32[512,512]{1,0:T(8,128)S(1)}, bf16[512,1024]{1,0:T(8,128)(2,1)S(1)}) custom-call(s32[2]{0:T(128)S(1)} %pad_add_fusion.refs_0_, s32[1,2048]{1,0:T(1,128)S(1)} %copy-done.13, s32[1,2048]{1,0:T(1,128)S(1)} %copy-done.13, s32[2048,1]{1,0:T(8,128)S(1)} %copy-done.6, bf16[512,512]{1,0:T(8,128)(2,1)S(1)} %copy-done.17, ...), custom_call_target="tpu_custom_call" | custom-call | flops 10737418240 | bytes 5242880 | tf_op jit(solution)/shard_map/backward/pallas_call | solution.py:37
  56.2 1.7 %project.9 = (bf16[512,512]{1,0:T(8,128)(2,1)S(1)}, bf16[512,512]{1,0:T(8,128)(2,1)}) custom-call(bf16[512,1024]{1,0:T(8,128)(2,1)S(1)} %collective-permute-done.4.refs_11_.refs_0_.refs_7_, bf16[1024,2048]{1,0:T(8,128)(2,1)S(1)} %copy-done.2, bf16[512,512]{1,0:T(8,128)(2,1)S(1)} %get-tuple-element.89.refs_2_.refs_6_), custom_call_target="tpu_custom_call" | custom-call | flops 4294967296 | bytes 2097152 | tf_op jit(solution)/shard_map/project/pallas_call | solution.py:37
  57.9 3.5 %collective-permute-done.6.refs_9_ = bf16[256,512]{1,0:T(8,128)(2,1)S(1)} collective-permute-done((bf16[256,512]{1,0:T(8,128)(2,1)S(1)}, bf16[256,512]{1,0:T(8,128)(2,1)S(1)}, u32[]{:S(2)}, u32[]{:S(2)}) %collective-permute-start.6) | collective-permute-done | bytes 262176 | tf_op jit(solution)/shard_map/ppermute | solution.py:26
  61.4 1.6 %backward.7 = (bf16[512,512]{1,0:T(8,128)(2,1)S(1)}, bf16[512,1024]{1,0:T(8,128)(2,1)S(1)}) custom-call(s32[2]{0:T(128)S(1)} %pad_add_fusion.refs_0_, s32[1,2048]{1,0:T(1,128)S(1)} %copy-done.13, s32[1,2048]{1,0:T(1,128)S(1)} %copy-done.13, s32[2048,1]{1,0:T(8,128)S(1)} %copy-done.6, bf16[512,512]{1,0:T(8,128)(2,1)} %collective-permute-done.refs_4_, ...), custom_call_target="tpu_custom_call" | custom-call | flops 10737418240 | bytes 5242880 | tf_op jit(solution)/shard_map/backward/pallas_call | solution.py:37
  63.1 2.4 %weights.4.refs_9_ = bf16[4,128,1536]{2,1,0:T(8,128)(2,1)S(1)} custom-call(s32[2]{0:T(128)S(1)} %pad_add_fusion.refs_0_, bf16[512,1024]{1,0:T(8,128)(2,1)S(1)} %get-tuple-element.65.refs_0_.refs_1_.refs_5_.refs_3_, bf16[512,1024]{1,0:T(8,128)(2,1)S(1)} %get-tuple-element.85.refs_2_.refs_1_, bf16[512,1024]{1,0:T(8,128)(2,1)S(1)} %get-tuple-element.95.refs_3_, ...), custom_call_target="tpu_custom_call" | custom-call | flops 1610612736 | bytes 1572864 | tf_op jit(solution)/shard_map/weights/pallas_call | solution.py:37
  65.6 2.4 %weights.5.refs_0_ = bf16[4,128,1536]{2,1,0:T(8,128)(2,1)S(1)} custom-call(s32[2]{0:T(128)S(1)} %pad_add_fusion.refs_0_, bf16[512,1024]{1,0:T(8,128)(2,1)S(1)} %get-tuple-element.65.refs_0_.refs_1_.refs_5_.refs_3_, bf16[512,1024]{1,0:T(8,128)(2,1)S(1)} %get-tuple-element.85.refs_2_.refs_1_, bf16[512,1024]{1,0:T(8,128)(2,1)S(1)} %get-tuple-element.95.refs_3_, ...), custom_call_target="tpu_custom_call" | custom-call | flops 1610612736 | bytes 1572864 | tf_op jit(solution)/shard_map/weights/pallas_call | solution.py:37
  68.0 1.0 collective-permute-done.7.refs_1_
  69.3 1.3 %far.1.refs_5_ = bf16[512,1024]{1,0:T(8,128)(2,1)S(1)} custom-call(bf16[512,1024]{1,0:T(8,128)(2,1)S(1)} %get-tuple-element.94.refs_4_.refs_0_, bf16[1024,2048]{1,0:T(8,128)(2,1)S(1)} %copy-done.2, bf16[1024,2048]{1,0:T(8,128)(2,1)S(1)} %copy-done.2, bf16[2,128,1536]{2,1,0:T(8,128)(2,1)S(1)} %get-tuple-element.97.refs_3_), custom_call_target="tpu_custom_call" | custom-call | flops 1073741824 | tf_op jit(solution)/shard_map/far/pallas_call | solution.py:37
  70.6 1.3 %weights.6.refs_5_ = bf16[4,128,1024]{2,1,0:T(8,128)(2,1)S(1)} custom-call(s32[2]{0:T(128)S(1)} %pad_add_fusion.refs_0_, bf16[512,1024]{1,0:T(8,128)(2,1)S(1)} %bitcast.9, bf16[512,512]{1,0:T(8,128)(2,1)S(1)} %get-tuple-element.79.refs_2_.refs_0_, bf16[512,1024]{1,0:T(8,128)(2,1)S(1)} %get-tuple-element.65.refs_0_.refs_1_.refs_5_.refs_3_, ...), custom_call_target="tpu_custom_call" | custom-call | flops 536870912 | bytes 1048576 | tf_op jit(solution)/shard_map/weights/pallas_call | solution.py:37
  72.1 1.5 %collective-permute-start.11 = (bf16[2,128,1536]{2,1,0:T(8,128)(2,1)S(1)}, bf16[2,128,1536]{2,1,0:T(8,128)(2,1)S(1)}, u32[]{:S(2)}, u32[]{:S(2)}) collective-permute-start(bf16[2,128,1536]{2,1,0:T(8,128)(2,1)S(1)} %get-tuple-element.97.refs_3_), channel_id=1, source_target_pairs={{0,8},{4,20},{8,0},{12,28},{16,24},{20,4},{24,16},{28,12},{1,9},{5... | collective-permute-start | bytes 2359304 | tf_op jit(solution)/shard_map/ppermute | solution.py:487
  73.6 1.3 %collective-permute-start.14 = (bf16[512,1024]{1,0:T(8,128)(2,1)S(1)}, bf16[512,1024]{1,0:T(8,128)(2,1)S(1)}, u32[]{:S(2)}, u32[]{:S(2)}) collective-permute-start(bf16[512,1024]{1,0:T(8,128)(2,1)S(1)} %far.1.refs_5_), channel_id=1, source_target_pairs={{1,0},{2,1},{3,2},{5,4},{6,5},{7,6},{9,8},{10,9},{11,10},{13,12},{... | collective-permute-start | bytes 3145736 | tf_op jit(solution)/shard_map/ppermute | solution.py:26
  74.9 1.3 %weights.7.refs_0_ = bf16[4,128,1024]{2,1,0:T(8,128)(2,1)S(1)} custom-call(s32[2]{0:T(128)S(1)} %pad_add_fusion.refs_0_, bf16[512,1024]{1,0:T(8,128)(2,1)S(1)} %bitcast.10, bf16[512,512]{1,0:T(8,128)(2,1)S(1)} %get-tuple-element.79.refs_2_.refs_0_, bf16[512,1024]{1,0:T(8,128)(2,1)S(1)} %get-tuple-element.65.refs_0_.refs_1_.refs_5_.refs_3_, ...), custom_call_target="tpu_custom_call" | custom-call | flops 536870912 | bytes 1048576 | tf_op jit(solution)/shard_map/weights/pallas_call | solution.py:37
  77.1 2.4 %near.1.refs_3_.refs_0_ = f32[512,1024]{1,0:T(8,128)S(1)} custom-call(bf16[512,512]{1,0:T(8,128)(2,1)S(1)} %get-tuple-element.80.refs_4_.refs_0_, bf16[512,1024]{1,0:T(8,128)(2,1)S(1)} %get-tuple-element.85.refs_2_.refs_1_, bf16[512,512]{1,0:T(8,128)(2,1)S(1)} %get-tuple-element.89.refs_2_.refs_6_, bf16[1024,2048]{1,0:T(8,128)(2,1)S(1)} %copy-done.2, ...), custom_call_target="tpu_custom_call" | custom-call | flops 2147483648 | tf_op jit(solution)/shard_map/near/pallas_call | solution.py:37
  79.5 1.7 %output.1 = (bf16[512,1024]{1,0:T(8,128)(2,1)}, f32[8,128]{1,0:T(8,128)S(1)}) custom-call(bf16[512,512]{1,0:T(8,128)(2,1)S(1)} %get-tuple-element.79.refs_2_.refs_0_, bf16[512,1024]{1,0:T(8,128)(2,1)S(1)} %copy-done.8, bf16[512,1024]{1,0:T(8,128)(2,1)S(1)} %bitcast.14, f32[512,1024]{1,0:T(8,128)S(1)} %near.1.refs_3_.refs_0_), custom_call_target="tpu_custom_call" | custom-call | flops 536870912 | tf_op jit(solution)/shard_map/output/pallas_call | solution.py:37
  81.2 2.9 %collective-permute-done.11.refs_1_ = bf16[2,128,1536]{2,1,0:T(8,128)(2,1)S(1)} collective-permute-done((bf16[2,128,1536]{2,1,0:T(8,128)(2,1)S(1)}, bf16[2,128,1536]{2,1,0:T(8,128)(2,1)S(1)}, u32[]{:S(2)}, u32[]{:S(2)}) %collective-permute-start.11) | collective-permute-done | bytes 786464 | tf_op jit(solution)/shard_map/ppermute | solution.py:487
  84.3 1.6 %collective-permute-start.13 = (bf16[1,128,1536]{2,1,0:T(8,128)(2,1)S(1)}, bf16[1,128,1536]{2,1,0:T(8,128)(2,1)S(1)}, u32[]{:S(2)}, u32[]{:S(2)}) collective-permute-start(bf16[1,128,1536]{2,1,0:T(8,128)(2,1)S(1)} %get-tuple-element.103.refs_2_), channel_id=1, source_target_pairs={{0,16},{4,12},{8,24},{12,4},{16,0},{20,28},{24,8},{28,20},{1,17},{... | collective-permute-start | bytes 1179656 | tf_op jit(solution)/shard_map/ppermute | solution.py:487
  85.9 5.3 %collective-permute-start.9 = (bf16[512,512]{1,0:T(8,128)(2,1)S(1)}, bf16[512,512]{1,0:T(8,128)(2,1)S(1)}, u32[]{:S(2)}, u32[]{:S(2)}) collective-permute-start(bf16[512,512]{1,0:T(8,128)(2,1)S(1)} %get-tuple-element.96.refs_8_), channel_id=1, source_target_pairs={{0,1},{1,2},{2,3},{4,5},{5,6},{6,7},{8,9},{9,10},{10,11},{12,13},{... | collective-permute-start | bytes 1572872 | tf_op jit(solution)/shard_map/ppermute | solution.py:26
  91.2 1.7 %collective-permute-done.10.refs_1_ = bf16[2,128,1024]{2,1,0:T(8,128)(2,1)S(1)} collective-permute-done((bf16[2,128,1024]{2,1,0:T(8,128)(2,1)S(1)}, bf16[2,128,1024]{2,1,0:T(8,128)(2,1)S(1)}, u32[]{:S(2)}, u32[]{:S(2)}) %collective-permute-start.10) | collective-permute-done | bytes 524320 | tf_op jit(solution)/shard_map/ppermute | solution.py:487
  93.0 1.6 %collective-permute-start.12 = (bf16[1,128,1024]{2,1,0:T(8,128)(2,1)S(1)}, bf16[1,128,1024]{2,1,0:T(8,128)(2,1)S(1)}, u32[]{:S(2)}, u32[]{:S(2)}) collective-permute-start(bf16[1,128,1024]{2,1,0:T(8,128)(2,1)S(1)} %get-tuple-element.105.refs_3_), channel_id=1, source_target_pairs={{0,16},{4,12},{8,24},{12,4},{16,0},{20,28},{24,8},{28,20},{1,17},{... | collective-permute-start | bytes 786440 | tf_op jit(solution)/shard_map/ppermute | solution.py:487
  95.3 2.9 %collective-permute-start.17 = (bf16[64,1536]{1,0:T(8,128)(2,1)S(1)}, bf16[64,1536]{1,0:T(8,128)(2,1)S(1)}, u32[]{:S(2)}, u32[]{:S(2)}) collective-permute-start(bf16[64,1536]{1,0:T(8,128)(2,1)S(1)} %get-tuple-element.117), channel_id=1, source_target_pairs={{0,1},{1,0},{2,3},{3,2},{4,5},{5,4},{6,7},{7,6},{8,9},{9,8},{10,11... | collective-permute-start | bytes 589832 | tf_op jit(solution)/shard_map/ppermute | solution.py:510
  98.2 1.2 %collective-permute-done.12.refs_2_ = bf16[1,128,1024]{2,1,0:T(8,128)(2,1)S(1)} collective-permute-done((bf16[1,128,1024]{2,1,0:T(8,128)(2,1)S(1)}, bf16[1,128,1024]{2,1,0:T(8,128)(2,1)S(1)}, u32[]{:S(2)}, u32[]{:S(2)}) %collective-permute-start.12) | collective-permute-done | bytes 262176 | tf_op jit(solution)/shard_map/ppermute | solution.py:487
  100.1 2.9 %collective-permute-start.15 = (bf16[64,1024]{1,0:T(8,128)(2,1)S(1)}, bf16[64,1024]{1,0:T(8,128)(2,1)S(1)}, u32[]{:S(2)}, u32[]{:S(2)}) collective-permute-start(bf16[64,1024]{1,0:T(8,128)(2,1)S(1)} %get-tuple-element.113), channel_id=1, source_target_pairs={{0,1},{1,0},{2,3},{3,2},{4,5},{5,4},{6,7},{7,6},{8,9},{9,8},{10,11... | collective-permute-start | bytes 393224 | tf_op jit(solution)/shard_map/ppermute | solution.py:510
  103.2 2.3 %mid.1 = (f32[512,1024]{1,0:T(8,128)S(1)}, bf16[512,1024]{1,0:T(8,128)(2,1)S(1)}, f32[512,128]{1,0:T(8,128)S(1)}) custom-call(f32[512,1024]{1,0:T(8,128)S(1)} %near.1.refs_3_.refs_0_, bf16[512,1024]{1,0:T(8,128)(2,1)S(1)} %bitcast.15, bf16[512,1024]{1,0:T(8,128)(2,1)S(1)} %bitcast.11, bf16[512,512]{1,0:T(8,128)(2,1)S(1)} %collective-permute-done.9.refs_3_, ...), custom_call_target="tpu_custom_call" | custom-call | tf_op jit(solution)/shard_map/mid/pallas_call | solution.py:37
  105.5 1.9 %tokens.1 = (bf16[512,1024]{1,0:T(8,128)(2,1)}, f32[8,128]{1,0:T(8,128)S(1)}) custom-call(f32[512,1024]{1,0:T(8,128)S(1)} %get-tuple-element.109.refs_0_, bf16[512,1024]{1,0:T(8,128)(2,1)S(1)} %get-tuple-element.110.refs_1_, f32[512,128]{1,0:T(8,128)S(1)} %get-tuple-element.111.refs_2_, bf16[512,1024]{1,0:T(8,128)(2,1)S(1)} %collective-permute-done.14.refs_3_, ...), custom_call_target="tpu_custom_call" | custom-call | tf_op jit(solution)/shard_map/tokens/pallas_call | solution.py:37
  107.4 1.6 %collective-permute-done.15.refs_1_ = bf16[64,1024]{1,0:T(8,128)(2,1)S(1)} collective-permute-done((bf16[64,1024]{1,0:T(8,128)(2,1)S(1)}, bf16[64,1024]{1,0:T(8,128)(2,1)S(1)}, u32[]{:S(2)}, u32[]{:S(2)}) %collective-permute-start.15) | collective-permute-done | bytes 131104 | tf_op jit(solution)/shard_map/ppermute | solution.py:510
  109.1 4.0 %collective-permute-start.18 = (bf16[32,1536]{1,0:T(8,128)(2,1)S(1)}, bf16[32,1536]{1,0:T(8,128)(2,1)S(1)}, u32[]{:S(2)}, u32[]{:S(2)}) collective-permute-start(bf16[32,1536]{1,0:T(8,128)(2,1)S(1)} %get-tuple-element.119), channel_id=1, source_target_pairs={{0,2},{1,3},{2,0},{3,1},{4,6},{5,7},{6,4},{7,5},{8,10},{9,11},{10,... | collective-permute-start | bytes 294920 | tf_op jit(solution)/shard_map/ppermute | solution.py:510
  113.2 7.3 %collective-permute-done.16.refs_1_ = bf16[32,1024]{1,0:T(8,128)(2,1)S(1)} collective-permute-done((bf16[32,1024]{1,0:T(8,128)(2,1)S(1)}, bf16[32,1024]{1,0:T(8,128)(2,1)S(1)}, u32[]{:S(2)}, u32[]{:S(2)}) %collective-permute-start.16) | collective-permute-done | bytes 65568 | tf_op jit(solution)/shard_map/ppermute | solution.py:510
  (76 shorter events, 12.0 us)
Async XLA Ops:
  0.6 27.8 %collective-permute-start.1 = (bf16[512,1024]{1,0:T(8,128)(2,1)}, bf16[512,1024]{1,0:T(8,128)(2,1)}, u32[]{:S(2)}, u32[]{:S(2)}) collective-permute-start(bf16[512,1024]{1,0:T(8,128)(2,1)} %bitcast.12), channel_id=1, source_target_pairs={{0,1},{1,2},{2,3},{4,5},{5,6},{6,7},{8,9},{9,10},{10,11},{12,13},{... | collective-permute-start | bytes 3145736 | tf_op jit(solution)/shard_map/ppermute | solution.py:26
  6.6 2.2 %copy-start = (bf16[1024,2048]{1,0:T(8,128)(2,1)S(1)}, bf16[1024,2048]{1,0:T(8,128)(2,1)}, u32[]{:S(2)}) copy-start(bf16[1024,2048]{1,0:T(8,128)(2,1)} %refs_4_.3) | copy-start | bytes 12582916
  8.8 1.2 %copy-start.4 = (bf16[1,512,1024]{2,1,0:T(8,128)(2,1)S(1)}, bf16[1,512,1024]{2,1,0:T(8,128)(2,1)}, u32[]{:S(2)}) copy-start(bf16[1,512,1024]{2,1,0:T(8,128)(2,1)} %param.5) | copy-start | bytes 3145732
  10.0 4.9 %copy-start.1 = (bf16[1024,2048]{1,0:T(8,128)(2,1)S(1)}, bf16[1024,2048]{1,0:T(8,128)(2,1)}, u32[]{:S(2)}) copy-start(bf16[1024,2048]{1,0:T(8,128)(2,1)} %refs_4_.3) | copy-start | bytes 12582916
  12.3 3.5 %copy-start.14 = (bf16[512,512]{1,0:T(8,128)(2,1)}, bf16[512,512]{1,0:T(8,128)(2,1)S(1)}, u32[]{:S(2)}) copy-start(bf16[512,512]{1,0:T(8,128)(2,1)S(1)} %get-tuple-element.88.refs_11_) | copy-start | bytes 1572868
  12.3 3.6 %copy-start.16 = (bf16[512,512]{1,0:T(8,128)(2,1)}, bf16[512,512]{1,0:T(8,128)(2,1)S(1)}, u32[]{:S(2)}) copy-start(bf16[512,512]{1,0:T(8,128)(2,1)S(1)} %get-tuple-element.64.refs_4_) | copy-start | bytes 1572868
  12.3 19.5 %collective-permute-start = (bf16[512,512]{1,0:T(8,128)(2,1)}, bf16[512,512]{1,0:T(8,128)(2,1)}, u32[]{:S(2)}, u32[]{:S(2)}) collective-permute-start(bf16[512,512]{1,0:T(8,128)(2,1)} %get-tuple-element.63), channel_id=1, source_target_pairs={{1,0},{2,1},{3,2},{5,4},{6,5},{7,6},{9,8},{10,9},{11,10},{13,12},{... | collective-permute-start | bytes 1572872 | tf_op jit(solution)/shard_map/ppermute | solution.py:26
  13.5 38.3 %collective-permute-start.4 = (bf16[512,1024]{1,0:T(8,128)(2,1)}, bf16[512,1024]{1,0:T(8,128)(2,1)S(1)}, u32[]{:S(2)}, u32[]{:S(2)}) collective-permute-start(bf16[512,1024]{1,0:T(8,128)(2,1)} %get-tuple-element.84), channel_id=1, source_target_pairs={{1,0},{2,1},{3,2},{5,4},{6,5},{7,6},{9,8},{10,9},{11,10},{13,12},{... | collective-permute-start | bytes 3145736 | tf_op jit(solution)/shard_map/ppermute | solution.py:26
  15.8 0.8 copy-start.9
  16.6 1.8 %copy-start.11 = (bf16[512,512]{1,0:T(8,128)(2,1)}, bf16[512,512]{1,0:T(8,128)(2,1)S(1)}, u32[]{:S(2)}) copy-start(bf16[512,512]{1,0:T(8,128)(2,1)S(1)} %get-tuple-element.66.refs_3_) | copy-start | bytes 1572868
  16.6 4.4 %copy-start.13 = (s32[1,2048]{1,0:T(1,128)S(1)}, s32[1,2048]{1,0:T(1,128)}, u32[]{:S(2)}) copy-start(s32[1,2048]{1,0:T(1,128)} %refs_2_.20) | copy-start | bytes 24580
  16.6 5.8 %copy-start.3 = (bf16[1,512,1024]{2,1,0:T(8,128)(2,1)S(1)}, bf16[1,512,1024]{2,1,0:T(8,128)(2,1)}, u32[]{:S(2)}) copy-start(bf16[1,512,1024]{2,1,0:T(8,128)(2,1)} %param.9) | copy-start | bytes 3145732
  18.4 0.8 copy-start.18
  19.2 0.8 copy-start.20
  20.0 1.0 copy-start.23
  22.4 1.2 %copy-start.7 = (bf16[512,1024]{1,0:T(8,128)(2,1)S(1)}, bf16[512,1024]{1,0:T(8,128)(2,1)}, u32[]{:S(2)}) copy-start(bf16[512,1024]{1,0:T(8,128)(2,1)} %refs_1_.31) | copy-start | bytes 3145732
  23.6 1.0 copy-start.21
  24.7 1.2 %copy-start.6 = (s32[2048,1]{1,0:T(8,128)S(1)}, s32[2048,1]{1,0:T(8,128)}, u32[]{:S(2)}) copy-start(s32[2048,1]{1,0:T(8,128)} %copy.11.refs_3_) | copy-start | bytes 24580
  24.7 1.4 %copy-start.17 = (bf16[512,512]{1,0:T(8,128)(2,1)S(1)}, bf16[512,512]{1,0:T(8,128)(2,1)}, u32[]{:S(2)}) copy-start(bf16[512,512]{1,0:T(8,128)(2,1)} %copy-done.16) | copy-start | bytes 1572868
  24.7 1.5 %copy-start.19 = (bf16[512,512]{1,0:T(8,128)(2,1)S(1)}, bf16[512,512]{1,0:T(8,128)(2,1)}, u32[]{:S(2)}) copy-start(bf16[512,512]{1,0:T(8,128)(2,1)} %copy-done.18) | copy-start | bytes 1572868
  26.2 2.2 %copy-start.2 = (bf16[1024,2048]{1,0:T(8,128)(2,1)S(1)}, bf16[1024,2048]{1,0:T(8,128)(2,1)}, u32[]{:S(2)}) copy-start(bf16[1024,2048]{1,0:T(8,128)(2,1)} %refs_4_.3) | copy-start | bytes 12582916
  32.9 12.7 %collective-permute-start.3 = (bf16[256,512]{1,0:T(8,128)(2,1)S(1)}, bf16[256,512]{1,0:T(8,128)(2,1)S(1)}, u32[]{:S(2)}, u32[]{:S(2)}) collective-permute-start(bf16[256,512]{1,0:T(8,128)(2,1)S(1)} %forward.5.refs_7_), channel_id=1, source_target_pairs={{0,1},{1,2},{2,3},{4,5},{5,6},{6,7},{8,9},{9,10},{10,11},{12,13},{... | collective-permute-start | bytes 786440 | tf_op jit(solution)/shard_map/ppermute | solution.py:26
  39.3 6.3 %copy-start.10 = (bf16[512,512]{1,0:T(8,128)(2,1)S(1)}, bf16[512,512]{1,0:T(8,128)(2,1)}, u32[]{:S(2)}) copy-start(bf16[512,512]{1,0:T(8,128)(2,1)} %copy-done.9) | copy-start | bytes 1572868
  39.3 6.3 %copy-start.12 = (bf16[512,512]{1,0:T(8,128)(2,1)S(1)}, bf16[512,512]{1,0:T(8,128)(2,1)}, u32[]{:S(2)}) copy-start(bf16[512,512]{1,0:T(8,128)(2,1)} %copy-done.11) | copy-start | bytes 1572868
  39.3 10.7 %collective-permute-start.2 = (bf16[256,512]{1,0:T(8,128)(2,1)S(1)}, bf16[256,512]{1,0:T(8,128)(2,1)S(1)}, u32[]{:S(2)}, u32[]{:S(2)}) collective-permute-start(bf16[256,512]{1,0:T(8,128)(2,1)S(1)} %forward.6.refs_8_), channel_id=1, source_target_pairs={{0,1},{1,2},{2,3},{4,5},{5,6},{6,7},{8,9},{9,10},{10,11},{12,13},{... | collective-permute-start | bytes 786440 | tf_op jit(solution)/shard_map/ppermute | solution.py:26
  46.1 15.3 %collective-permute-start.5 = (bf16[256,512]{1,0:T(8,128)(2,1)S(1)}, bf16[256,512]{1,0:T(8,128)(2,1)S(1)}, u32[]{:S(2)}, u32[]{:S(2)}) collective-permute-start(bf16[256,512]{1,0:T(8,128)(2,1)S(1)} %get-tuple-element.74.refs_8_.refs_5_), channel_id=1, source_target_pairs={{1,0},{2,1},{3,2},{5,4},{6,5},{7,6},{9,8},{10,9},{11,10},{13,12},{... | collective-permute-start | bytes 786440 | tf_op jit(solution)/shard_map/ppermute | solution.py:26
  50.1 1.8 %copy-start.22 = (bf16[512,512]{1,0:T(8,128)(2,1)S(1)}, bf16[512,512]{1,0:T(8,128)(2,1)}, u32[]{:S(2)}) copy-start(bf16[512,512]{1,0:T(8,128)(2,1)} %copy-done.20) | copy-start | bytes 1572868
  50.1 1.8 %copy-start.24 = (bf16[512,1024]{1,0:T(8,128)(2,1)S(1)}, bf16[512,1024]{1,0:T(8,128)(2,1)}, u32[]{:S(2)}) copy-start(bf16[512,1024]{1,0:T(8,128)(2,1)} %copy-done.23) | copy-start | bytes 3145732
  50.6 10.9 %collective-permute-start.6 = (bf16[256,512]{1,0:T(8,128)(2,1)S(1)}, bf16[256,512]{1,0:T(8,128)(2,1)S(1)}, u32[]{:S(2)}, u32[]{:S(2)}) collective-permute-start(bf16[256,512]{1,0:T(8,128)(2,1)S(1)} %get-tuple-element.90), channel_id=1, source_target_pairs={{1,0},{2,1},{3,2},{5,4},{6,5},{7,6},{9,8},{10,9},{11,10},{13,12},{... | collective-permute-start | bytes 786440 | tf_op jit(solution)/shard_map/ppermute | solution.py:26
  51.9 3.3 %copy-start.15 = (bf16[512,512]{1,0:T(8,128)(2,1)S(1)}, bf16[512,512]{1,0:T(8,128)(2,1)}, u32[]{:S(2)}) copy-start(bf16[512,512]{1,0:T(8,128)(2,1)} %copy-done.14) | copy-start | bytes 1572868
  65.5 3.5 %collective-permute-start.7 = (bf16[4,128,1536]{2,1,0:T(8,128)(2,1)S(1)}, bf16[4,128,1536]{2,1,0:T(8,128)(2,1)S(1)}, u32[]{:S(2)}, u32[]{:S(2)}) collective-permute-start(bf16[4,128,1536]{2,1,0:T(8,128)(2,1)S(1)} %weights.4.refs_9_), channel_id=1, source_target_pairs={{0,4},{4,0},{8,12},{12,8},{16,20},{20,16},{24,28},{28,24},{1,5},{5... | collective-permute-start | bytes 4718600 | tf_op jit(solution)/shard_map/ppermute | solution.py:487
  71.9 4.3 %collective-permute-start.8 = (bf16[4,128,1024]{2,1,0:T(8,128)(2,1)S(1)}, bf16[4,128,1024]{2,1,0:T(8,128)(2,1)S(1)}, u32[]{:S(2)}, u32[]{:S(2)}) collective-permute-start(bf16[4,128,1024]{2,1,0:T(8,128)(2,1)S(1)} %weights.6.refs_5_), channel_id=1, source_target_pairs={{0,4},{4,0},{8,12},{12,8},{16,20},{20,16},{24,28},{28,24},{1,5},{5... | collective-permute-start | bytes 3145736 | tf_op jit(solution)/shard_map/ppermute | solution.py:487
  72.1 12.0 %collective-permute-start.11 = (bf16[2,128,1536]{2,1,0:T(8,128)(2,1)S(1)}, bf16[2,128,1536]{2,1,0:T(8,128)(2,1)S(1)}, u32[]{:S(2)}, u32[]{:S(2)}) collective-permute-start(bf16[2,128,1536]{2,1,0:T(8,128)(2,1)S(1)} %get-tuple-element.97.refs_3_), channel_id=1, source_target_pairs={{0,8},{4,20},{8,0},{12,28},{16,24},{20,4},{24,16},{28,12},{1,9},{5... | collective-permute-start | bytes 2359304 | tf_op jit(solution)/shard_map/ppermute | solution.py:487
  73.6 31.9 %collective-permute-start.14 = (bf16[512,1024]{1,0:T(8,128)(2,1)S(1)}, bf16[512,1024]{1,0:T(8,128)(2,1)S(1)}, u32[]{:S(2)}, u32[]{:S(2)}) collective-permute-start(bf16[512,1024]{1,0:T(8,128)(2,1)S(1)} %far.1.refs_5_), channel_id=1, source_target_pairs={{1,0},{2,1},{3,2},{5,4},{6,5},{7,6},{9,8},{10,9},{11,10},{13,12},{... | collective-permute-start | bytes 3145736 | tf_op jit(solution)/shard_map/ppermute | solution.py:26
  76.5 3.0 %copy-start.5 = (bf16[1,512,1024]{2,1,0:T(8,128)(2,1)S(1)}, bf16[1,512,1024]{2,1,0:T(8,128)(2,1)}, u32[]{:S(2)}) copy-start(bf16[1,512,1024]{2,1,0:T(8,128)(2,1)} %param.5) | copy-start | bytes 3145732
  76.5 3.0 %copy-start.8 = (bf16[512,1024]{1,0:T(8,128)(2,1)S(1)}, bf16[512,1024]{1,0:T(8,128)(2,1)}, u32[]{:S(2)}) copy-start(bf16[512,1024]{1,0:T(8,128)(2,1)} %refs_1_.31) | copy-start | bytes 3145732
  76.5 16.4 %collective-permute-start.10 = (bf16[2,128,1024]{2,1,0:T(8,128)(2,1)S(1)}, bf16[2,128,1024]{2,1,0:T(8,128)(2,1)S(1)}, u32[]{:S(2)}, u32[]{:S(2)}) collective-permute-start(bf16[2,128,1024]{2,1,0:T(8,128)(2,1)S(1)} %get-tuple-element.98.refs_7_), channel_id=1, source_target_pairs={{0,8},{4,20},{8,0},{12,28},{16,24},{20,4},{24,16},{28,12},{1,9},{5... | collective-permute-start | bytes 1572872 | tf_op jit(solution)/shard_map/ppermute | solution.py:487
  84.3 10.3 %collective-permute-start.13 = (bf16[1,128,1536]{2,1,0:T(8,128)(2,1)S(1)}, bf16[1,128,1536]{2,1,0:T(8,128)(2,1)S(1)}, u32[]{:S(2)}, u32[]{:S(2)}) collective-permute-start(bf16[1,128,1536]{2,1,0:T(8,128)(2,1)S(1)} %get-tuple-element.103.refs_2_), channel_id=1, source_target_pairs={{0,16},{4,12},{8,24},{12,4},{16,0},{20,28},{24,8},{28,20},{1,17},{... | collective-permute-start | bytes 1179656 | tf_op jit(solution)/shard_map/ppermute | solution.py:487
  85.9 17.3 %collective-permute-start.9 = (bf16[512,512]{1,0:T(8,128)(2,1)S(1)}, bf16[512,512]{1,0:T(8,128)(2,1)S(1)}, u32[]{:S(2)}, u32[]{:S(2)}) collective-permute-start(bf16[512,512]{1,0:T(8,128)(2,1)S(1)} %get-tuple-element.96.refs_8_), channel_id=1, source_target_pairs={{0,1},{1,2},{2,3},{4,5},{5,6},{6,7},{8,9},{9,10},{10,11},{12,13},{... | collective-permute-start | bytes 1572872 | tf_op jit(solution)/shard_map/ppermute | solution.py:26
  93.0 6.4 %collective-permute-start.12 = (bf16[1,128,1024]{2,1,0:T(8,128)(2,1)S(1)}, bf16[1,128,1024]{2,1,0:T(8,128)(2,1)S(1)}, u32[]{:S(2)}, u32[]{:S(2)}) collective-permute-start(bf16[1,128,1024]{2,1,0:T(8,128)(2,1)S(1)} %get-tuple-element.105.refs_3_), channel_id=1, source_target_pairs={{0,16},{4,12},{8,24},{12,4},{16,0},{20,28},{24,8},{28,20},{1,17},{... | collective-permute-start | bytes 786440 | tf_op jit(solution)/shard_map/ppermute | solution.py:487
  95.3 13.7 %collective-permute-start.17 = (bf16[64,1536]{1,0:T(8,128)(2,1)S(1)}, bf16[64,1536]{1,0:T(8,128)(2,1)S(1)}, u32[]{:S(2)}, u32[]{:S(2)}) collective-permute-start(bf16[64,1536]{1,0:T(8,128)(2,1)S(1)} %get-tuple-element.117), channel_id=1, source_target_pairs={{0,1},{1,0},{2,3},{3,2},{4,5},{5,4},{6,7},{7,6},{8,9},{9,8},{10,11... | collective-permute-start | bytes 589832 | tf_op jit(solution)/shard_map/ppermute | solution.py:510
  100.1 8.9 %collective-permute-start.15 = (bf16[64,1024]{1,0:T(8,128)(2,1)S(1)}, bf16[64,1024]{1,0:T(8,128)(2,1)S(1)}, u32[]{:S(2)}, u32[]{:S(2)}) collective-permute-start(bf16[64,1024]{1,0:T(8,128)(2,1)S(1)} %get-tuple-element.113), channel_id=1, source_target_pairs={{0,1},{1,0},{2,3},{3,2},{4,5},{5,4},{6,7},{7,6},{8,9},{9,8},{10,11... | collective-permute-start | bytes 393224 | tf_op jit(solution)/shard_map/ppermute | solution.py:510
  109.1 11.4 %collective-permute-start.18 = (bf16[32,1536]{1,0:T(8,128)(2,1)S(1)}, bf16[32,1536]{1,0:T(8,128)(2,1)S(1)}, u32[]{:S(2)}, u32[]{:S(2)}) collective-permute-start(bf16[32,1536]{1,0:T(8,128)(2,1)S(1)} %get-tuple-element.119), channel_id=1, source_target_pairs={{0,2},{1,3},{2,0},{3,1},{4,6},{5,7},{6,4},{7,5},{8,10},{9,11},{10,... | collective-permute-start | bytes 294920 | tf_op jit(solution)/shard_map/ppermute | solution.py:510
  113.1 7.4 %collective-permute-start.16 = (bf16[32,1024]{1,0:T(8,128)(2,1)S(1)}, bf16[32,1024]{1,0:T(8,128)(2,1)S(1)}, u32[]{:S(2)}, u32[]{:S(2)}) collective-permute-start(bf16[32,1024]{1,0:T(8,128)(2,1)S(1)} %get-tuple-element.116), channel_id=1, source_target_pairs={{0,2},{1,3},{2,0},{3,1},{4,6},{5,7},{6,4},{7,5},{8,10},{9,11},{10,... | collective-permute-start | bytes 196616 | tf_op jit(solution)/shard_map/ppermute | solution.py:510

commit v2 on v1

--- a/solution.py
+++ b/solution.py
@@ -655,9 +655,6 @@
     order = [next_q] if down else [grad_q]
     late_send = weight_half(place, late, 1, weight=1)
     late_other = swap_dp(late_send, 0)
-    late_mine = weight_half(place, late, 0, after=[late_send], weight=1)
-    late_send, late_mine = halve(late_mine, late_other)
-    late_other = swap_dp(late_send, 1)
     far_parts = []
     for by, grad in enumerate(far_sums, 1):
         part = call(
@@ -670,8 +667,11 @@
             after=[late_send],
         )
         far_parts.append(part)
-    order = far_parts
+    late_mine = weight_half(place, late, 0, after=far_parts, weight=1)
     far_parts = [shift(part, -by) for by, part in enumerate(far_parts, 1)]
+    late_send, late_mine = halve(late_mine, late_other)
+    late_other = swap_dp(late_send, 1)
+    order = [late_send]
     next_q = [shift(next_q, up)] if down else []
     early = [[(upstream, gated)], [(normed, grad_u)]]
     early_send = weight_half(place, early, 1, after=order, weight=1)

time: 121 us -> 119 us (0.983)
  starting transfers between devices: 43.6 us -> 39.3 us
  waiting for transfers between devices: 21.2 us -> 23.1 us
    ppermute x6, waiting for transfers between devices: 6.9 us -> 9.77 us  [swap_dp(): return lax.ppermute(value, 'dp', pairs)]
    ppermute x9, starting transfers between devices: 28.3 us -> 25.7 us  [shift(): return lax.ppermute(value, 'seq', pairs)]
    ppermute x4, starting transfers between devices: 9.86 us -> 7.76 us  [swap_seq(): lax.ppermute(value, 'seq', [(i, i ^ bit) for i in range(lax.axis_size('se...]
    ppermute x4, waiting for transfers between devices: 8.91 us -> 7.51 us  [swap_seq(): lax.ppermute(value, 'seq', [(i, i ^ bit) for i in range(lax.axis_size('se...]
  transfers between devices with their start and end apart: 19 -> 19, of which waited for: 9 -> 7; matrix products, arithmetic and copies ran while one was open for 1% -> 1% of each run, Pallas kernels for 30% -> 32%
where the time goes in v2:
time: 119 us
  Pallas kernels  44.1 us (37%)
  starting transfers between devices  39.3 us (33%)
  waiting for transfers between devices  23.1 us (19%)
  local copies, waits for them, and re-layouts  11.2 us (9%)
    pallas_call x34, Pallas kernels, call(): pl.pallas_call(body, grid=(1,), out_shape=outs, in_specs=(specs or [VMEM]...  44.1 us
    ppermute x9, starting transfers between devices, shift(): return lax.ppermute(value, 'seq', pairs)  25.7 us
    unnamed x50, local copies, waits for them, and re-layouts  9.9 us
    ppermute x6, waiting for transfers between devices, swap_dp(): return lax.ppermute(value, 'dp', pairs)  9.77 us
    ppermute x4, starting transfers between devices, swap_seq(): lax.ppermute(value, 'seq', [(i, i ^ bit) for i in range(lax.axis_size('se...  7.76 us
    ppermute x4, waiting for transfers between devices, swap_seq(): lax.ppermute(value, 'seq', [(i, i ^ bit) for i in range(lax.axis_size('se...  7.51 us
    ppermute x6, starting transfers between devices, swap_dp(): return lax.ppermute(value, 'dp', pairs)  5.86 us
    ppermute x9, waiting for transfers between devices, shift(): return lax.ppermute(value, 'seq', pairs)  5.82 us
  transfers between devices with their start and end apart: 19, of which 7 were waited for; matrix products, arithmetic and copies ran while one was open for 1% of the time, Pallas kernels for 32%

profile of v2, /device:TPU:0, one launch (start us, length us, event | category | flops | bytes accessed | tf_op | source)
XLA Modules:
  0.0 118.9 jit_solution(9804085320308903357)
XLA Ops:
  0.6 5.9 %collective-permute-start.1 = (bf16[512,1024]{1,0:T(8,128)(2,1)}, bf16[512,1024]{1,0:T(8,128)(2,1)}, u32[]{:S(2)}, u32[]{:S(2)}) collective-permute-start(bf16[512,1024]{1,0:T(8,128)(2,1)} %bitcast.12), channel_id=1, source_target_pairs={{0,1},{1,2},{2,3},{4,5},{5,6},{6,7},{8,9},{9,10},{10,11},{12,13},{... | collective-permute-start | bytes 3145736 | tf_op jit(solution)/shard_map/ppermute | solution.py:26
  6.6 2.2 %copy-done = bf16[1024,2048]{1,0:T(8,128)(2,1)S(1)} copy-done((bf16[1024,2048]{1,0:T(8,128)(2,1)S(1)}, bf16[1024,2048]{1,0:T(8,128)(2,1)}, u32[]{:S(2)}) %copy-start) | copy-done | bytes 4194328
  8.8 1.2 %copy-done.4 = bf16[1,512,1024]{2,1,0:T(8,128)(2,1)S(1)} copy-done((bf16[1,512,1024]{2,1,0:T(8,128)(2,1)S(1)}, bf16[1,512,1024]{2,1,0:T(8,128)(2,1)}, u32[]{:S(2)}) %copy-start.4) | copy-done | bytes 1048600
  10.0 2.3 %project.5 = (bf16[512,1024]{1,0:T(8,128)(2,1)S(1)}, bf16[512,512]{1,0:T(8,128)(2,1)S(1)}, bf16[512,512]{1,0:T(8,128)(2,1)S(1)}, bf16[512,1024]{1,0:T(8,128)(2,1)}, bf16[512,512]{1,0:T(8,128)(2,1)}) custom-call(bf16[512,1024]{1,0:T(8,128)(2,1)S(1)} %bitcast.13, bf16[1024,2048]{1,0:T(8,128)(2,1)S(1)} %copy-done), custom_call_target="tpu_custom_call" | custom-call | flops 4294967296 | bytes 2097152 | tf_op jit(solution)/shard_map/project/pallas_call | solution.py:37
  12.3 1.3 %collective-permute-start = (bf16[512,512]{1,0:T(8,128)(2,1)}, bf16[512,512]{1,0:T(8,128)(2,1)}, u32[]{:S(2)}, u32[]{:S(2)}) collective-permute-start(bf16[512,512]{1,0:T(8,128)(2,1)} %get-tuple-element.63), channel_id=1, source_target_pairs={{1,0},{2,1},{3,2},{5,4},{6,5},{7,6},{9,8},{10,9},{11,10},{13,12},{... | collective-permute-start | bytes 1572872 | tf_op jit(solution)/shard_map/ppermute | solution.py:26
  13.5 1.3 %collective-permute-start.4 = (bf16[512,1024]{1,0:T(8,128)(2,1)}, bf16[512,1024]{1,0:T(8,128)(2,1)S(1)}, u32[]{:S(2)}, u32[]{:S(2)}) collective-permute-start(bf16[512,1024]{1,0:T(8,128)(2,1)} %get-tuple-element.84), channel_id=1, source_target_pairs={{1,0},{2,1},{3,2},{5,4},{6,5},{7,6},{9,8},{10,9},{11,10},{13,12},{... | collective-permute-start | bytes 3145736 | tf_op jit(solution)/shard_map/ppermute | solution.py:26
  14.9 0.9 project.6
  16.6 1.7 %project.7 = (bf16[512,1024]{1,0:T(8,128)(2,1)S(1)}, bf16[512,512]{1,0:T(8,128)(2,1)S(1)}, bf16[512,512]{1,0:T(8,128)(2,1)S(1)}) custom-call(bf16[512,1024]{1,0:T(8,128)(2,1)S(1)} %get-tuple-element.65.refs_0_.refs_1_.refs_5_.refs_3_, bf16[1024,2048]{1,0:T(8,128)(2,1)S(1)} %copy-done.1, bf16[1024,2048]{1,0:T(8,128)(2,1)S(1)} %copy-done.1, ...), custom_call_target="tpu_custom_call" | custom-call | flops 8589934592 | bytes 3145728 | tf_op jit(solution)/shard_map/project/pallas_call | solution.py:37
  20.0 1.0 copy-done.23
  21.0 1.3 %copy.11.refs_3_ = s32[2048,1]{1,0:T(8,128)} copy(s32[2048,1]{0,1:T(1,128)S(1)} %bitcast.16) | data formatting | bytes 16384 | tf_op jit(solution)/shard_map/reshape;squeeze | solution.py:564
  22.4 1.2 %copy-done.7 = bf16[512,1024]{1,0:T(8,128)(2,1)S(1)} copy-done((bf16[512,1024]{1,0:T(8,128)(2,1)S(1)}, bf16[512,1024]{1,0:T(8,128)(2,1)}, u32[]{:S(2)}) %copy-start.7) | copy-done | bytes 1048600
  23.6 1.0 copy-done.21
  26.2 2.2 %forward.4 = (f32[512,512]{1,0:T(8,128)S(1)}, bf16[512,512]{1,0:T(8,128)(2,1)S(1)}) custom-call(s32[2]{0:T(128)S(1)} %pad_add_fusion.refs_0_, s32[1,2048]{1,0:T(1,128)S(1)} %copy-done.13, s32[1,2048]{1,0:T(1,128)S(1)} %copy-done.13, s32[2048,1]{1,0:T(8,128)S(1)} %copy-done.6, bf16[512,512]{1,0:T(8,128)(2,1)S(1)} %copy-done.17, ...), custom_call_target="tpu_custom_call" | custom-call | flops 4294967296 | bytes 2621440 | tf_op jit(solution)/shard_map/forward/pallas_call | solution.py:37
  28.4 3.3 %project.8 = (bf16[512,1024]{1,0:T(8,128)(2,1)S(1)}, bf16[512,1024]{1,0:T(8,128)(2,1)S(1)}, bf16[512,512]{1,0:T(8,128)(2,1)S(1)}, bf16[512,512]{1,0:T(8,128)(2,1)S(1)}) custom-call(bf16[512,1024]{1,0:T(8,128)(2,1)} %collective-permute-done.1.refs_0_, bf16[1024,2048]{1,0:T(8,128)(2,1)S(1)} %copy-done.2, bf16[1024,2048]{1,0:T(8,128)(2,1)S(1)} %copy-done.2, ...), custom_call_target="tpu_custom_call" | custom-call | flops 8589934592 | bytes 3145728 | tf_op jit(solution)/shard_map/project/pallas_call | solution.py:37
  31.8 1.2 forward.5.refs_7_
  33.0 5.2 %collective-permute-start.3 = (bf16[256,512]{1,0:T(8,128)(2,1)S(1)}, bf16[256,512]{1,0:T(8,128)(2,1)S(1)}, u32[]{:S(2)}, u32[]{:S(2)}) collective-permute-start(bf16[256,512]{1,0:T(8,128)(2,1)S(1)} %forward.5.refs_7_), channel_id=1, source_target_pairs={{0,1},{1,2},{2,3},{4,5},{5,6},{6,7},{8,9},{9,10},{10,11},{12,13},{... | collective-permute-start | bytes 786440 | tf_op jit(solution)/shard_map/ppermute | solution.py:26
  38.1 1.2 forward.6.refs_8_
  39.3 4.7 %collective-permute-start.2 = (bf16[256,512]{1,0:T(8,128)(2,1)S(1)}, bf16[256,512]{1,0:T(8,128)(2,1)S(1)}, u32[]{:S(2)}, u32[]{:S(2)}) collective-permute-start(bf16[256,512]{1,0:T(8,128)(2,1)S(1)} %forward.6.refs_8_), channel_id=1, source_target_pairs={{0,1},{1,2},{2,3},{4,5},{5,6},{6,7},{8,9},{9,10},{10,11},{12,13},{... | collective-permute-start | bytes 786440 | tf_op jit(solution)/shard_map/ppermute | solution.py:26
  45.4 1.3 %collective-permute-start.5 = (bf16[256,512]{1,0:T(8,128)(2,1)S(1)}, bf16[256,512]{1,0:T(8,128)(2,1)S(1)}, u32[]{:S(2)}, u32[]{:S(2)}) collective-permute-start(bf16[256,512]{1,0:T(8,128)(2,1)S(1)} %get-tuple-element.74.refs_8_.refs_5_), channel_id=1, source_target_pairs={{1,0},{2,1},{3,2},{5,4},{6,5},{7,6},{9,8},{10,9},{11,10},{13,12},{... | collective-permute-start | bytes 786440 | tf_op jit(solution)/shard_map/ppermute | solution.py:26
  46.7 1.0 backward.4
  47.7 2.3 %collective-permute-done.2.refs_0_ = bf16[256,512]{1,0:T(8,128)(2,1)S(1)} collective-permute-done((bf16[256,512]{1,0:T(8,128)(2,1)S(1)}, bf16[256,512]{1,0:T(8,128)(2,1)S(1)}, u32[]{:S(2)}, u32[]{:S(2)}) %collective-permute-start.2) | collective-permute-done | bytes 262176 | tf_op jit(solution)/shard_map/ppermute | solution.py:26
  50.6 1.3 %collective-permute-start.6 = (bf16[256,512]{1,0:T(8,128)(2,1)S(1)}, bf16[256,512]{1,0:T(8,128)(2,1)S(1)}, u32[]{:S(2)}, u32[]{:S(2)}) collective-permute-start(bf16[256,512]{1,0:T(8,128)(2,1)S(1)} %get-tuple-element.91), channel_id=1, source_target_pairs={{1,0},{2,1},{3,2},{5,4},{6,5},{7,6},{9,8},{10,9},{11,10},{13,12},{... | collective-permute-start | bytes 786440 | tf_op jit(solution)/shard_map/ppermute | solution.py:26
  51.9 3.3 %backward.5 = (f32[512,512]{1,0:T(8,128)S(1)}, bf16[512,1024]{1,0:T(8,128)(2,1)S(1)}) custom-call(s32[2]{0:T(128)S(1)} %pad_add_fusion.refs_0_, s32[1,2048]{1,0:T(1,128)S(1)} %copy-done.13, s32[1,2048]{1,0:T(1,128)S(1)} %copy-done.13, s32[2048,1]{1,0:T(8,128)S(1)} %copy-done.6, bf16[512,512]{1,0:T(8,128)(2,1)S(1)} %copy-done.17, ...), custom_call_target="tpu_custom_call" | custom-call | flops 10737418240 | bytes 5242880 | tf_op jit(solution)/shard_map/backward/pallas_call | solution.py:37
  55.3 1.0 backward.6
  56.2 1.7 %project.9 = (bf16[512,512]{1,0:T(8,128)(2,1)S(1)}, bf16[512,512]{1,0:T(8,128)(2,1)}) custom-call(bf16[512,1024]{1,0:T(8,128)(2,1)S(1)} %collective-permute-done.4.refs_11_.refs_0_.refs_7_, bf16[1024,2048]{1,0:T(8,128)(2,1)S(1)} %copy-done.2, bf16[512,512]{1,0:T(8,128)(2,1)S(1)} %get-tuple-element.89.refs_2_.refs_6_), custom_call_target="tpu_custom_call" | custom-call | flops 4294967296 | bytes 2097152 | tf_op jit(solution)/shard_map/project/pallas_call | solution.py:37
  58.0 3.5 %collective-permute-done.6.refs_9_ = bf16[256,512]{1,0:T(8,128)(2,1)S(1)} collective-permute-done((bf16[256,512]{1,0:T(8,128)(2,1)S(1)}, bf16[256,512]{1,0:T(8,128)(2,1)S(1)}, u32[]{:S(2)}, u32[]{:S(2)}) %collective-permute-start.6) | collective-permute-done | bytes 262176 | tf_op jit(solution)/shard_map/ppermute | solution.py:26
  61.4 1.7 %backward.7 = (bf16[512,512]{1,0:T(8,128)(2,1)S(1)}, bf16[512,1024]{1,0:T(8,128)(2,1)S(1)}) custom-call(s32[2]{0:T(128)S(1)} %pad_add_fusion.refs_0_, s32[1,2048]{1,0:T(1,128)S(1)} %copy-done.13, s32[1,2048]{1,0:T(1,128)S(1)} %copy-done.13, s32[2048,1]{1,0:T(8,128)S(1)} %copy-done.6, bf16[512,512]{1,0:T(8,128)(2,1)} %collective-permute-done.refs_4_, ...), custom_call_target="tpu_custom_call" | custom-call | flops 10737418240 | bytes 5242880 | tf_op jit(solution)/shard_map/backward/pallas_call | solution.py:37
  63.1 2.4 %weights.4.refs_3_ = bf16[4,128,1536]{2,1,0:T(8,128)(2,1)S(1)} custom-call(s32[2]{0:T(128)S(1)} %pad_add_fusion.refs_0_, bf16[512,1024]{1,0:T(8,128)(2,1)S(1)} %get-tuple-element.65.refs_0_.refs_1_.refs_5_.refs_3_, bf16[512,1024]{1,0:T(8,128)(2,1)S(1)} %get-tuple-element.85.refs_2_.refs_1_, bf16[512,1024]{1,0:T(8,128)(2,1)S(1)} %get-tuple-element.90.refs_3_, ...), custom_call_target="tpu_custom_call" | custom-call | flops 1610612736 | bytes 1572864 | tf_op jit(solution)/shard_map/weights/pallas_call | solution.py:37
  65.6 1.3 %far.1.refs_9_ = bf16[512,1024]{1,0:T(8,128)(2,1)S(1)} custom-call(bf16[512,1024]{1,0:T(8,128)(2,1)S(1)} %get-tuple-element.95.refs_4_.refs_0_, bf16[1024,2048]{1,0:T(8,128)(2,1)S(1)} %copy-done.2, bf16[1024,2048]{1,0:T(8,128)(2,1)S(1)} %copy-done.2, bf16[4,128,1536]{2,1,0:T(8,128)(2,1)S(1)} %weights.4.refs_3_), custom_call_target="tpu_custom_call" | custom-call | flops 1073741824 | tf_op jit(solution)/shard_map/far/pallas_call | solution.py:37
  66.9 2.4 %weights.5.refs_0_ = bf16[4,128,1536]{2,1,0:T(8,128)(2,1)S(1)} custom-call(s32[2]{0:T(128)S(1)} %pad_add_fusion.refs_0_, bf16[512,1024]{1,0:T(8,128)(2,1)S(1)} %get-tuple-element.65.refs_0_.refs_1_.refs_5_.refs_3_, bf16[512,1024]{1,0:T(8,128)(2,1)S(1)} %get-tuple-element.85.refs_2_.refs_1_, bf16[512,1024]{1,0:T(8,128)(2,1)S(1)} %get-tuple-element.90.refs_3_, ...), custom_call_target="tpu_custom_call" | custom-call | flops 1610612736 | bytes 1572864 | tf_op jit(solution)/shard_map/weights/pallas_call | solution.py:37
  69.7 1.3 %weights.6.refs_5_ = bf16[4,128,1024]{2,1,0:T(8,128)(2,1)S(1)} custom-call(s32[2]{0:T(128)S(1)} %pad_add_fusion.refs_0_, bf16[512,1024]{1,0:T(8,128)(2,1)S(1)} %bitcast.9, bf16[512,512]{1,0:T(8,128)(2,1)S(1)} %get-tuple-element.79.refs_2_.refs_0_, bf16[512,1024]{1,0:T(8,128)(2,1)S(1)} %get-tuple-element.65.refs_0_.refs_1_.refs_5_.refs_3_, ...), custom_call_target="tpu_custom_call" | custom-call | flops 536870912 | bytes 1048576 | tf_op jit(solution)/shard_map/weights/pallas_call | solution.py:37
  71.6 1.5 %collective-permute-start.11 = (bf16[2,128,1536]{2,1,0:T(8,128)(2,1)S(1)}, bf16[2,128,1536]{2,1,0:T(8,128)(2,1)S(1)}, u32[]{:S(2)}, u32[]{:S(2)}) collective-permute-start(bf16[2,128,1536]{2,1,0:T(8,128)(2,1)S(1)} %get-tuple-element.97.refs_5_), channel_id=1, source_target_pairs={{0,8},{4,20},{8,0},{12,28},{16,24},{20,4},{24,16},{28,12},{1,9},{5... | collective-permute-start | bytes 2359304 | tf_op jit(solution)/shard_map/ppermute | solution.py:487
  73.0 1.3 %collective-permute-start.14 = (bf16[512,1024]{1,0:T(8,128)(2,1)S(1)}, bf16[512,1024]{1,0:T(8,128)(2,1)S(1)}, u32[]{:S(2)}, u32[]{:S(2)}) collective-permute-start(bf16[512,1024]{1,0:T(8,128)(2,1)S(1)} %far.1.refs_9_), channel_id=1, source_target_pairs={{1,0},{2,1},{3,2},{5,4},{6,5},{7,6},{9,8},{10,9},{11,10},{13,12},{... | collective-permute-start | bytes 3145736 | tf_op jit(solution)/shard_map/ppermute | solution.py:26
  74.3 1.3 %weights.7.refs_0_ = bf16[4,128,1024]{2,1,0:T(8,128)(2,1)S(1)} custom-call(s32[2]{0:T(128)S(1)} %pad_add_fusion.refs_0_, bf16[512,1024]{1,0:T(8,128)(2,1)S(1)} %bitcast.10, bf16[512,512]{1,0:T(8,128)(2,1)S(1)} %get-tuple-element.79.refs_2_.refs_0_, bf16[512,1024]{1,0:T(8,128)(2,1)S(1)} %get-tuple-element.65.refs_0_.refs_1_.refs_5_.refs_3_, ...), custom_call_target="tpu_custom_call" | custom-call | flops 536870912 | bytes 1048576 | tf_op jit(solution)/shard_map/weights/pallas_call | solution.py:37
  76.5 2.4 %near.1.refs_3_.refs_0_ = f32[512,1024]{1,0:T(8,128)S(1)} custom-call(bf16[512,512]{1,0:T(8,128)(2,1)S(1)} %get-tuple-element.80.refs_4_.refs_0_, bf16[512,1024]{1,0:T(8,128)(2,1)S(1)} %get-tuple-element.85.refs_2_.refs_1_, bf16[512,512]{1,0:T(8,128)(2,1)S(1)} %get-tuple-element.89.refs_2_.refs_6_, bf16[1024,2048]{1,0:T(8,128)(2,1)S(1)} %copy-done.2, ...), custom_call_target="tpu_custom_call" | custom-call | flops 2147483648 | tf_op jit(solution)/shard_map/near/pallas_call | solution.py:37
  78.9 1.7 %output.1 = (bf16[512,1024]{1,0:T(8,128)(2,1)}, f32[8,128]{1,0:T(8,128)S(1)}) custom-call(bf16[512,512]{1,0:T(8,128)(2,1)S(1)} %get-tuple-element.79.refs_2_.refs_0_, bf16[512,1024]{1,0:T(8,128)(2,1)S(1)} %copy-done.8, bf16[512,1024]{1,0:T(8,128)(2,1)S(1)} %bitcast.14, f32[512,1024]{1,0:T(8,128)S(1)} %near.1.refs_3_.refs_0_), custom_call_target="tpu_custom_call" | custom-call | flops 536870912 | tf_op jit(solution)/shard_map/output/pallas_call | solution.py:37
  80.6 2.9 %collective-permute-done.11.refs_1_ = bf16[2,128,1536]{2,1,0:T(8,128)(2,1)S(1)} collective-permute-done((bf16[2,128,1536]{2,1,0:T(8,128)(2,1)S(1)}, bf16[2,128,1536]{2,1,0:T(8,128)(2,1)S(1)}, u32[]{:S(2)}, u32[]{:S(2)}) %collective-permute-start.11) | collective-permute-done | bytes 786464 | tf_op jit(solution)/shard_map/ppermute | solution.py:487
  83.7 1.6 %collective-permute-start.13 = (bf16[1,128,1536]{2,1,0:T(8,128)(2,1)S(1)}, bf16[1,128,1536]{2,1,0:T(8,128)(2,1)S(1)}, u32[]{:S(2)}, u32[]{:S(2)}) collective-permute-start(bf16[1,128,1536]{2,1,0:T(8,128)(2,1)S(1)} %get-tuple-element.103.refs_2_), channel_id=1, source_target_pairs={{0,16},{4,12},{8,24},{12,4},{16,0},{20,28},{24,8},{28,20},{1,17},{... | collective-permute-start | bytes 1179656 | tf_op jit(solution)/shard_map/ppermute | solution.py:487
  85.3 3.4 %collective-permute-start.9 = (bf16[512,512]{1,0:T(8,128)(2,1)S(1)}, bf16[512,512]{1,0:T(8,128)(2,1)S(1)}, u32[]{:S(2)}, u32[]{:S(2)}) collective-permute-start(bf16[512,512]{1,0:T(8,128)(2,1)S(1)} %get-tuple-element.96.refs_8_), channel_id=1, source_target_pairs={{0,1},{1,2},{2,3},{4,5},{5,6},{6,7},{8,9},{9,10},{10,11},{12,13},{... | collective-permute-start | bytes 1572872 | tf_op jit(solution)/shard_map/ppermute | solution.py:26
  88.7 4.0 %collective-permute-done.10.refs_1_ = bf16[2,128,1024]{2,1,0:T(8,128)(2,1)S(1)} collective-permute-done((bf16[2,128,1024]{2,1,0:T(8,128)(2,1)S(1)}, bf16[2,128,1024]{2,1,0:T(8,128)(2,1)S(1)}, u32[]{:S(2)}, u32[]{:S(2)}) %collective-permute-start.10) | collective-permute-done | bytes 524320 | tf_op jit(solution)/shard_map/ppermute | solution.py:487
  92.8 1.6 %collective-permute-start.12 = (bf16[1,128,1024]{2,1,0:T(8,128)(2,1)S(1)}, bf16[1,128,1024]{2,1,0:T(8,128)(2,1)S(1)}, u32[]{:S(2)}, u32[]{:S(2)}) collective-permute-start(bf16[1,128,1024]{2,1,0:T(8,128)(2,1)S(1)} %get-tuple-element.105.refs_3_), channel_id=1, source_target_pairs={{0,16},{4,12},{8,24},{12,4},{16,0},{20,28},{24,8},{28,20},{1,17},{... | collective-permute-start | bytes 786440 | tf_op jit(solution)/shard_map/ppermute | solution.py:487
  95.1 1.3 %collective-permute-start.17 = (bf16[64,1536]{1,0:T(8,128)(2,1)S(1)}, bf16[64,1536]{1,0:T(8,128)(2,1)S(1)}, u32[]{:S(2)}, u32[]{:S(2)}) collective-permute-start(bf16[64,1536]{1,0:T(8,128)(2,1)S(1)} %get-tuple-element.117), channel_id=1, source_target_pairs={{0,1},{1,0},{2,3},{3,2},{4,5},{5,4},{6,7},{7,6},{8,9},{9,8},{10,11... | collective-permute-start | bytes 589832 | tf_op jit(solution)/shard_map/ppermute | solution.py:510
  96.3 2.9 %collective-permute-done.12.refs_2_ = bf16[1,128,1024]{2,1,0:T(8,128)(2,1)S(1)} collective-permute-done((bf16[1,128,1024]{2,1,0:T(8,128)(2,1)S(1)}, bf16[1,128,1024]{2,1,0:T(8,128)(2,1)S(1)}, u32[]{:S(2)}, u32[]{:S(2)}) %collective-permute-start.12) | collective-permute-done | bytes 262176 | tf_op jit(solution)/shard_map/ppermute | solution.py:487
  99.9 2.4 %collective-permute-start.15 = (bf16[64,1024]{1,0:T(8,128)(2,1)S(1)}, bf16[64,1024]{1,0:T(8,128)(2,1)S(1)}, u32[]{:S(2)}, u32[]{:S(2)}) collective-permute-start(bf16[64,1024]{1,0:T(8,128)(2,1)S(1)} %get-tuple-element.113), channel_id=1, source_target_pairs={{0,1},{1,0},{2,3},{3,2},{4,5},{5,4},{6,7},{7,6},{8,9},{9,8},{10,11... | collective-permute-start | bytes 393224 | tf_op jit(solution)/shard_map/ppermute | solution.py:510
  102.3 2.3 %mid.1 = (f32[512,1024]{1,0:T(8,128)S(1)}, bf16[512,1024]{1,0:T(8,128)(2,1)S(1)}, f32[512,128]{1,0:T(8,128)S(1)}) custom-call(f32[512,1024]{1,0:T(8,128)S(1)} %near.1.refs_3_.refs_0_, bf16[512,1024]{1,0:T(8,128)(2,1)S(1)} %bitcast.15, bf16[512,1024]{1,0:T(8,128)(2,1)S(1)} %bitcast.11, bf16[512,512]{1,0:T(8,128)(2,1)S(1)} %collective-permute-done.9.refs_3_, ...), custom_call_target="tpu_custom_call" | custom-call | tf_op jit(solution)/shard_map/mid/pallas_call | solution.py:37
  104.6 1.9 %tokens.1 = (bf16[512,1024]{1,0:T(8,128)(2,1)}, f32[8,128]{1,0:T(8,128)S(1)}) custom-call(f32[512,1024]{1,0:T(8,128)S(1)} %get-tuple-element.109.refs_0_, bf16[512,1024]{1,0:T(8,128)(2,1)S(1)} %get-tuple-element.110.refs_1_, f32[512,128]{1,0:T(8,128)S(1)} %get-tuple-element.111.refs_2_, bf16[512,1024]{1,0:T(8,128)(2,1)S(1)} %collective-permute-done.14.refs_3_, ...), custom_call_target="tpu_custom_call" | custom-call | tf_op jit(solution)/shard_map/tokens/pallas_call | solution.py:37
  107.0 4.0 %collective-permute-start.18 = (bf16[32,1536]{1,0:T(8,128)(2,1)S(1)}, bf16[32,1536]{1,0:T(8,128)(2,1)S(1)}, u32[]{:S(2)}, u32[]{:S(2)}) collective-permute-start(bf16[32,1536]{1,0:T(8,128)(2,1)S(1)} %get-tuple-element.119), channel_id=1, source_target_pairs={{0,2},{1,3},{2,0},{3,1},{4,6},{5,7},{6,4},{7,5},{8,10},{9,11},{10,... | collective-permute-start | bytes 294920 | tf_op jit(solution)/shard_map/ppermute | solution.py:510
  111.1 7.1 %collective-permute-done.16.refs_1_ = bf16[32,1024]{1,0:T(8,128)(2,1)S(1)} collective-permute-done((bf16[32,1024]{1,0:T(8,128)(2,1)S(1)}, bf16[32,1024]{1,0:T(8,128)(2,1)S(1)}, u32[]{:S(2)}, u32[]{:S(2)}) %collective-permute-start.16) | collective-permute-done | bytes 65568 | tf_op jit(solution)/shard_map/ppermute | solution.py:510
  (76 shorter events, 10.7 us)
Async XLA Ops:
  0.6 27.8 %collective-permute-start.1 = (bf16[512,1024]{1,0:T(8,128)(2,1)}, bf16[512,1024]{1,0:T(8,128)(2,1)}, u32[]{:S(2)}, u32[]{:S(2)}) collective-permute-start(bf16[512,1024]{1,0:T(8,128)(2,1)} %bitcast.12), channel_id=1, source_target_pairs={{0,1},{1,2},{2,3},{4,5},{5,6},{6,7},{8,9},{9,10},{10,11},{12,13},{... | collective-permute-start | bytes 3145736 | tf_op jit(solution)/shard_map/ppermute | solution.py:26
  6.6 2.2 %copy-start = (bf16[1024,2048]{1,0:T(8,128)(2,1)S(1)}, bf16[1024,2048]{1,0:T(8,128)(2,1)}, u32[]{:S(2)}) copy-start(bf16[1024,2048]{1,0:T(8,128)(2,1)} %refs_4_.3) | copy-start | bytes 12582916
  8.8 1.2 %copy-start.4 = (bf16[1,512,1024]{2,1,0:T(8,128)(2,1)S(1)}, bf16[1,512,1024]{2,1,0:T(8,128)(2,1)}, u32[]{:S(2)}) copy-start(bf16[1,512,1024]{2,1,0:T(8,128)(2,1)} %param.5) | copy-start | bytes 3145732
  10.0 4.9 %copy-start.1 = (bf16[1024,2048]{1,0:T(8,128)(2,1)S(1)}, bf16[1024,2048]{1,0:T(8,128)(2,1)}, u32[]{:S(2)}) copy-start(bf16[1024,2048]{1,0:T(8,128)(2,1)} %refs_4_.3) | copy-start | bytes 12582916
  12.3 3.5 %copy-start.14 = (bf16[512,512]{1,0:T(8,128)(2,1)}, bf16[512,512]{1,0:T(8,128)(2,1)S(1)}, u32[]{:S(2)}) copy-start(bf16[512,512]{1,0:T(8,128)(2,1)S(1)} %get-tuple-element.88.refs_11_) | copy-start | bytes 1572868
  12.3 3.6 %copy-start.16 = (bf16[512,512]{1,0:T(8,128)(2,1)}, bf16[512,512]{1,0:T(8,128)(2,1)S(1)}, u32[]{:S(2)}) copy-start(bf16[512,512]{1,0:T(8,128)(2,1)S(1)} %get-tuple-element.64.refs_4_) | copy-start | bytes 1572868
  12.3 19.5 %collective-permute-start = (bf16[512,512]{1,0:T(8,128)(2,1)}, bf16[512,512]{1,0:T(8,128)(2,1)}, u32[]{:S(2)}, u32[]{:S(2)}) collective-permute-start(bf16[512,512]{1,0:T(8,128)(2,1)} %get-tuple-element.63), channel_id=1, source_target_pairs={{1,0},{2,1},{3,2},{5,4},{6,5},{7,6},{9,8},{10,9},{11,10},{13,12},{... | collective-permute-start | bytes 1572872 | tf_op jit(solution)/shard_map/ppermute | solution.py:26
  13.5 38.3 %collective-permute-start.4 = (bf16[512,1024]{1,0:T(8,128)(2,1)}, bf16[512,1024]{1,0:T(8,128)(2,1)S(1)}, u32[]{:S(2)}, u32[]{:S(2)}) collective-permute-start(bf16[512,1024]{1,0:T(8,128)(2,1)} %get-tuple-element.84), channel_id=1, source_target_pairs={{1,0},{2,1},{3,2},{5,4},{6,5},{7,6},{9,8},{10,9},{11,10},{13,12},{... | collective-permute-start | bytes 3145736 | tf_op jit(solution)/shard_map/ppermute | solution.py:26
  15.8 0.8 copy-start.9
  16.6 1.8 %copy-start.11 = (bf16[512,512]{1,0:T(8,128)(2,1)}, bf16[512,512]{1,0:T(8,128)(2,1)S(1)}, u32[]{:S(2)}) copy-start(bf16[512,512]{1,0:T(8,128)(2,1)S(1)} %get-tuple-element.66.refs_3_) | copy-start | bytes 1572868
  16.6 4.4 %copy-start.13 = (s32[1,2048]{1,0:T(1,128)S(1)}, s32[1,2048]{1,0:T(1,128)}, u32[]{:S(2)}) copy-start(s32[1,2048]{1,0:T(1,128)} %refs_2_.20) | copy-start | bytes 24580
  16.6 5.8 %copy-start.3 = (bf16[1,512,1024]{2,1,0:T(8,128)(2,1)S(1)}, bf16[1,512,1024]{2,1,0:T(8,128)(2,1)}, u32[]{:S(2)}) copy-start(bf16[1,512,1024]{2,1,0:T(8,128)(2,1)} %param.9) | copy-start | bytes 3145732
  18.4 0.8 copy-start.18
  19.2 0.8 copy-start.20
  20.0 1.0 copy-start.23
  22.4 1.2 %copy-start.7 = (bf16[512,1024]{1,0:T(8,128)(2,1)S(1)}, bf16[512,1024]{1,0:T(8,128)(2,1)}, u32[]{:S(2)}) copy-start(bf16[512,1024]{1,0:T(8,128)(2,1)} %refs_1_.31) | copy-start | bytes 3145732
  23.6 1.0 copy-start.21
  24.7 1.2 %copy-start.6 = (s32[2048,1]{1,0:T(8,128)S(1)}, s32[2048,1]{1,0:T(8,128)}, u32[]{:S(2)}) copy-start(s32[2048,1]{1,0:T(8,128)} %copy.11.refs_3_) | copy-start | bytes 24580
  24.7 1.4 %copy-start.17 = (bf16[512,512]{1,0:T(8,128)(2,1)S(1)}, bf16[512,512]{1,0:T(8,128)(2,1)}, u32[]{:S(2)}) copy-start(bf16[512,512]{1,0:T(8,128)(2,1)} %copy-done.16) | copy-start | bytes 1572868
  24.7 1.5 %copy-start.19 = (bf16[512,512]{1,0:T(8,128)(2,1)S(1)}, bf16[512,512]{1,0:T(8,128)(2,1)}, u32[]{:S(2)}) copy-start(bf16[512,512]{1,0:T(8,128)(2,1)} %copy-done.18) | copy-start | bytes 1572868
  26.2 2.2 %copy-start.2 = (bf16[1024,2048]{1,0:T(8,128)(2,1)S(1)}, bf16[1024,2048]{1,0:T(8,128)(2,1)}, u32[]{:S(2)}) copy-start(bf16[1024,2048]{1,0:T(8,128)(2,1)} %refs_4_.3) | copy-start | bytes 12582916
  33.0 12.0 %collective-permute-start.3 = (bf16[256,512]{1,0:T(8,128)(2,1)S(1)}, bf16[256,512]{1,0:T(8,128)(2,1)S(1)}, u32[]{:S(2)}, u32[]{:S(2)}) collective-permute-start(bf16[256,512]{1,0:T(8,128)(2,1)S(1)} %forward.5.refs_7_), channel_id=1, source_target_pairs={{0,1},{1,2},{2,3},{4,5},{5,6},{6,7},{8,9},{9,10},{10,11},{12,13},{... | collective-permute-start | bytes 786440 | tf_op jit(solution)/shard_map/ppermute | solution.py:26
  39.3 5.6 %copy-start.10 = (bf16[512,512]{1,0:T(8,128)(2,1)S(1)}, bf16[512,512]{1,0:T(8,128)(2,1)}, u32[]{:S(2)}) copy-start(bf16[512,512]{1,0:T(8,128)(2,1)} %copy-done.9) | copy-start | bytes 1572868
  39.3 5.6 %copy-start.12 = (bf16[512,512]{1,0:T(8,128)(2,1)S(1)}, bf16[512,512]{1,0:T(8,128)(2,1)}, u32[]{:S(2)}) copy-start(bf16[512,512]{1,0:T(8,128)(2,1)} %copy-done.11) | copy-start | bytes 1572868
  39.3 10.7 %collective-permute-start.2 = (bf16[256,512]{1,0:T(8,128)(2,1)S(1)}, bf16[256,512]{1,0:T(8,128)(2,1)S(1)}, u32[]{:S(2)}, u32[]{:S(2)}) collective-permute-start(bf16[256,512]{1,0:T(8,128)(2,1)S(1)} %forward.6.refs_8_), channel_id=1, source_target_pairs={{0,1},{1,2},{2,3},{4,5},{5,6},{6,7},{8,9},{9,10},{10,11},{12,13},{... | collective-permute-start | bytes 786440 | tf_op jit(solution)/shard_map/ppermute | solution.py:26
  45.4 16.0 %collective-permute-start.5 = (bf16[256,512]{1,0:T(8,128)(2,1)S(1)}, bf16[256,512]{1,0:T(8,128)(2,1)S(1)}, u32[]{:S(2)}, u32[]{:S(2)}) collective-permute-start(bf16[256,512]{1,0:T(8,128)(2,1)S(1)} %get-tuple-element.74.refs_8_.refs_5_), channel_id=1, source_target_pairs={{1,0},{2,1},{3,2},{5,4},{6,5},{7,6},{9,8},{10,9},{11,10},{13,12},{... | collective-permute-start | bytes 786440 | tf_op jit(solution)/shard_map/ppermute | solution.py:26
  50.1 1.8 %copy-start.22 = (bf16[512,512]{1,0:T(8,128)(2,1)S(1)}, bf16[512,512]{1,0:T(8,128)(2,1)}, u32[]{:S(2)}) copy-start(bf16[512,512]{1,0:T(8,128)(2,1)} %copy-done.20) | copy-start | bytes 1572868
  50.1 1.8 %copy-start.24 = (bf16[512,1024]{1,0:T(8,128)(2,1)S(1)}, bf16[512,1024]{1,0:T(8,128)(2,1)}, u32[]{:S(2)}) copy-start(bf16[512,1024]{1,0:T(8,128)(2,1)} %copy-done.23) | copy-start | bytes 3145732
  50.6 10.9 %collective-permute-start.6 = (bf16[256,512]{1,0:T(8,128)(2,1)S(1)}, bf16[256,512]{1,0:T(8,128)(2,1)S(1)}, u32[]{:S(2)}, u32[]{:S(2)}) collective-permute-start(bf16[256,512]{1,0:T(8,128)(2,1)S(1)} %get-tuple-element.91), channel_id=1, source_target_pairs={{1,0},{2,1},{3,2},{5,4},{6,5},{7,6},{9,8},{10,9},{11,10},{13,12},{... | collective-permute-start | bytes 786440 | tf_op jit(solution)/shard_map/ppermute | solution.py:26
  51.9 3.3 %copy-start.15 = (bf16[512,512]{1,0:T(8,128)(2,1)S(1)}, bf16[512,512]{1,0:T(8,128)(2,1)}, u32[]{:S(2)}) copy-start(bf16[512,512]{1,0:T(8,128)(2,1)} %copy-done.14) | copy-start | bytes 1572868
  65.5 3.8 %collective-permute-start.7 = (bf16[4,128,1536]{2,1,0:T(8,128)(2,1)S(1)}, bf16[4,128,1536]{2,1,0:T(8,128)(2,1)S(1)}, u32[]{:S(2)}, u32[]{:S(2)}) collective-permute-start(bf16[4,128,1536]{2,1,0:T(8,128)(2,1)S(1)} %weights.4.refs_3_), channel_id=1, source_target_pairs={{0,4},{4,0},{8,12},{12,8},{16,20},{20,16},{24,28},{28,24},{1,5},{5... | collective-permute-start | bytes 4718600 | tf_op jit(solution)/shard_map/ppermute | solution.py:487
  71.0 4.6 %collective-permute-start.8 = (bf16[4,128,1024]{2,1,0:T(8,128)(2,1)S(1)}, bf16[4,128,1024]{2,1,0:T(8,128)(2,1)S(1)}, u32[]{:S(2)}, u32[]{:S(2)}) collective-permute-start(bf16[4,128,1024]{2,1,0:T(8,128)(2,1)S(1)} %weights.6.refs_5_), channel_id=1, source_target_pairs={{0,4},{4,0},{8,12},{12,8},{16,20},{20,16},{24,28},{28,24},{1,5},{5... | collective-permute-start | bytes 3145736 | tf_op jit(solution)/shard_map/ppermute | solution.py:487
  71.6 12.0 %collective-permute-start.11 = (bf16[2,128,1536]{2,1,0:T(8,128)(2,1)S(1)}, bf16[2,128,1536]{2,1,0:T(8,128)(2,1)S(1)}, u32[]{:S(2)}, u32[]{:S(2)}) collective-permute-start(bf16[2,128,1536]{2,1,0:T(8,128)(2,1)S(1)} %get-tuple-element.97.refs_5_), channel_id=1, source_target_pairs={{0,8},{4,20},{8,0},{12,28},{16,24},{20,4},{24,16},{28,12},{1,9},{5... | collective-permute-start | bytes 2359304 | tf_op jit(solution)/shard_map/ppermute | solution.py:487
  73.0 31.5 %collective-permute-start.14 = (bf16[512,1024]{1,0:T(8,128)(2,1)S(1)}, bf16[512,1024]{1,0:T(8,128)(2,1)S(1)}, u32[]{:S(2)}, u32[]{:S(2)}) collective-permute-start(bf16[512,1024]{1,0:T(8,128)(2,1)S(1)} %far.1.refs_9_), channel_id=1, source_target_pairs={{1,0},{2,1},{3,2},{5,4},{6,5},{7,6},{9,8},{10,9},{11,10},{13,12},{... | collective-permute-start | bytes 3145736 | tf_op jit(solution)/shard_map/ppermute | solution.py:26
  75.9 3.0 %copy-start.5 = (bf16[1,512,1024]{2,1,0:T(8,128)(2,1)S(1)}, bf16[1,512,1024]{2,1,0:T(8,128)(2,1)}, u32[]{:S(2)}) copy-start(bf16[1,512,1024]{2,1,0:T(8,128)(2,1)} %param.5) | copy-start | bytes 3145732
  75.9 3.0 %copy-start.8 = (bf16[512,1024]{1,0:T(8,128)(2,1)S(1)}, bf16[512,1024]{1,0:T(8,128)(2,1)}, u32[]{:S(2)}) copy-start(bf16[512,1024]{1,0:T(8,128)(2,1)} %refs_1_.31) | copy-start | bytes 3145732
  75.9 16.7 %collective-permute-start.10 = (bf16[2,128,1024]{2,1,0:T(8,128)(2,1)S(1)}, bf16[2,128,1024]{2,1,0:T(8,128)(2,1)S(1)}, u32[]{:S(2)}, u32[]{:S(2)}) collective-permute-start(bf16[2,128,1024]{2,1,0:T(8,128)(2,1)S(1)} %get-tuple-element.98.refs_7_), channel_id=1, source_target_pairs={{0,8},{4,20},{8,0},{12,28},{16,24},{20,4},{24,16},{28,12},{1,9},{5... | collective-permute-start | bytes 1572872 | tf_op jit(solution)/shard_map/ppermute | solution.py:487
  83.7 10.6 %collective-permute-start.13 = (bf16[1,128,1536]{2,1,0:T(8,128)(2,1)S(1)}, bf16[1,128,1536]{2,1,0:T(8,128)(2,1)S(1)}, u32[]{:S(2)}, u32[]{:S(2)}) collective-permute-start(bf16[1,128,1536]{2,1,0:T(8,128)(2,1)S(1)} %get-tuple-element.103.refs_2_), channel_id=1, source_target_pairs={{0,16},{4,12},{8,24},{12,4},{16,0},{20,28},{24,8},{28,20},{1,17},{... | collective-permute-start | bytes 1179656 | tf_op jit(solution)/shard_map/ppermute | solution.py:487
  85.3 17.0 %collective-permute-start.9 = (bf16[512,512]{1,0:T(8,128)(2,1)S(1)}, bf16[512,512]{1,0:T(8,128)(2,1)S(1)}, u32[]{:S(2)}, u32[]{:S(2)}) collective-permute-start(bf16[512,512]{1,0:T(8,128)(2,1)S(1)} %get-tuple-element.96.refs_8_), channel_id=1, source_target_pairs={{0,1},{1,2},{2,3},{4,5},{5,6},{6,7},{8,9},{9,10},{10,11},{12,13},{... | collective-permute-start | bytes 1572872 | tf_op jit(solution)/shard_map/ppermute | solution.py:26
  92.8 6.4 %collective-permute-start.12 = (bf16[1,128,1024]{2,1,0:T(8,128)(2,1)S(1)}, bf16[1,128,1024]{2,1,0:T(8,128)(2,1)S(1)}, u32[]{:S(2)}, u32[]{:S(2)}) collective-permute-start(bf16[1,128,1024]{2,1,0:T(8,128)(2,1)S(1)} %get-tuple-element.105.refs_3_), channel_id=1, source_target_pairs={{0,16},{4,12},{8,24},{12,4},{16,0},{20,28},{24,8},{28,20},{1,17},{... | collective-permute-start | bytes 786440 | tf_op jit(solution)/shard_map/ppermute | solution.py:487
  95.1 11.9 %collective-permute-start.17 = (bf16[64,1536]{1,0:T(8,128)(2,1)S(1)}, bf16[64,1536]{1,0:T(8,128)(2,1)S(1)}, u32[]{:S(2)}, u32[]{:S(2)}) collective-permute-start(bf16[64,1536]{1,0:T(8,128)(2,1)S(1)} %get-tuple-element.117), channel_id=1, source_target_pairs={{0,1},{1,0},{2,3},{3,2},{4,5},{5,4},{6,7},{7,6},{8,9},{9,8},{10,11... | collective-permute-start | bytes 589832 | tf_op jit(solution)/shard_map/ppermute | solution.py:510
  99.9 7.1 %collective-permute-start.15 = (bf16[64,1024]{1,0:T(8,128)(2,1)S(1)}, bf16[64,1024]{1,0:T(8,128)(2,1)S(1)}, u32[]{:S(2)}, u32[]{:S(2)}) collective-permute-start(bf16[64,1024]{1,0:T(8,128)(2,1)S(1)} %get-tuple-element.113), channel_id=1, source_target_pairs={{0,1},{1,0},{2,3},{3,2},{4,5},{5,4},{6,7},{7,6},{8,9},{9,8},{10,11... | collective-permute-start | bytes 393224 | tf_op jit(solution)/shard_map/ppermute | solution.py:510
  107.0 11.1 %collective-permute-start.18 = (bf16[32,1536]{1,0:T(8,128)(2,1)S(1)}, bf16[32,1536]{1,0:T(8,128)(2,1)S(1)}, u32[]{:S(2)}, u32[]{:S(2)}) collective-permute-start(bf16[32,1536]{1,0:T(8,128)(2,1)S(1)} %get-tuple-element.119), channel_id=1, source_target_pairs={{0,2},{1,3},{2,0},{3,1},{4,6},{5,7},{6,4},{7,5},{8,10},{9,11},{10,... | collective-permute-start | bytes 294920 | tf_op jit(solution)/shard_map/ppermute | solution.py:510
  111.0 7.1 %collective-permute-start.16 = (bf16[32,1024]{1,0:T(8,128)(2,1)S(1)}, bf16[32,1024]{1,0:T(8,128)(2,1)S(1)}, u32[]{:S(2)}, u32[]{:S(2)}) collective-permute-start(bf16[32,1024]{1,0:T(8,128)(2,1)S(1)} %get-tuple-element.116), channel_id=1, source_target_pairs={{0,2},{1,3},{2,0},{3,1},{4,6},{5,7},{6,4},{7,5},{8,10},{9,11},{10,... | collective-permute-start | bytes 196616 | tf_op jit(solution)/shard_map/ppermute | solution.py:510

commit v3 on v2

--- a/solution.py
+++ b/solution.py
@@ -697,7 +697,9 @@
     for phase in phases:
         late_send, late_mine = halve(late_mine, late_other, after=order)
         late_other = swap_dp(late_send, phase)
-        early_send, early_mine = halve(early_mine, early_other, after=[late_send])
+        early_send, early_mine = halve(
+            early_mine, early_other, after=[late_send, *next_q]
+        )
         early_other = swap_dp(early_send, phase)
         order = [early_send]
     late_sum = first_share(place, late_mine, late_other, order)

time: 119 us -> 119 us (level)
  waiting for transfers between devices: 23.1 us -> 17.6 us
  starting transfers between devices: 39.3 us -> 44.3 us
    ppermute x6, waiting for transfers between devices: 9.77 us -> 2.95 us  [swap_dp(): return lax.ppermute(value, 'dp', pairs)]
    ppermute x4, starting transfers between devices: 7.76 us -> 12 us  [swap_seq(): lax.ppermute(value, 'seq', [(i, i ^ bit) for i in range(lax.axis_size('se...]
    ppermute x9, waiting for transfers between devices: 5.82 us -> 8.83 us  [shift(): return lax.ppermute(value, 'seq', pairs)]
    ppermute x4, waiting for transfers between devices: 7.51 us -> 5.8 us  [swap_seq(): lax.ppermute(value, 'seq', [(i, i ^ bit) for i in range(lax.axis_size('se...]
  transfers between devices with their start and end apart: 19 -> 19, of which waited for: 7 -> 6; matrix products, arithmetic and copies ran while one was open for 1% -> 1% of each run, Pallas kernels for 32% -> 32%
where the time goes in v3:
time: 119 us
  starting transfers between devices  44.3 us (37%)
  Pallas kernels  44.3 us (37%)
  waiting for transfers between devices  17.6 us (15%)
  local copies, waits for them, and re-layouts  11.2 us (9%)
    pallas_call x34, Pallas kernels, call(): pl.pallas_call(body, grid=(1,), out_shape=outs, in_specs=(specs or [VMEM]...  44.3 us
    ppermute x9, starting transfers between devices, shift(): return lax.ppermute(value, 'seq', pairs)  26.5 us
    ppermute x4, starting transfers between devices, swap_seq(): lax.ppermute(value, 'seq', [(i, i ^ bit) for i in range(lax.axis_size('se...  12 us
    unnamed x50, local copies, waits for them, and re-layouts  9.9 us
    ppermute x9, waiting for transfers between devices, shift(): return lax.ppermute(value, 'seq', pairs)  8.83 us
    ppermute x6, starting transfers between devices, swap_dp(): return lax.ppermute(value, 'dp', pairs)  5.84 us
    ppermute x4, waiting for transfers between devices, swap_seq(): lax.ppermute(value, 'seq', [(i, i ^ bit) for i in range(lax.axis_size('se...  5.8 us
    ppermute x6, waiting for transfers between devices, swap_dp(): return lax.ppermute(value, 'dp', pairs)  2.95 us
  transfers between devices with their start and end apart: 19, of which 6 were waited for; matrix products, arithmetic and copies ran while one was open for 1% of the time, Pallas kernels for 32%

profile of v3, /device:TPU:0, one launch (start us, length us, event | category | flops | bytes accessed | tf_op | source)
XLA Modules:
  0.0 118.6 jit_solution(1645456453711546290)
XLA Ops:
  0.6 5.9 %collective-permute-start.1 = (bf16[512,1024]{1,0:T(8,128)(2,1)}, bf16[512,1024]{1,0:T(8,128)(2,1)}, u32[]{:S(2)}, u32[]{:S(2)}) collective-permute-start(bf16[512,1024]{1,0:T(8,128)(2,1)} %bitcast.12), channel_id=1, source_target_pairs={{0,1},{1,2},{2,3},{4,5},{5,6},{6,7},{8,9},{9,10},{10,11},{12,13},{... | collective-permute-start | bytes 3145736 | tf_op jit(solution)/shard_map/ppermute | solution.py:26
  6.6 2.2 %copy-done = bf16[1024,2048]{1,0:T(8,128)(2,1)S(1)} copy-done((bf16[1024,2048]{1,0:T(8,128)(2,1)S(1)}, bf16[1024,2048]{1,0:T(8,128)(2,1)}, u32[]{:S(2)}) %copy-start) | copy-done | bytes 4194328
  8.8 1.2 %copy-done.4 = bf16[1,512,1024]{2,1,0:T(8,128)(2,1)S(1)} copy-done((bf16[1,512,1024]{2,1,0:T(8,128)(2,1)S(1)}, bf16[1,512,1024]{2,1,0:T(8,128)(2,1)}, u32[]{:S(2)}) %copy-start.4) | copy-done | bytes 1048600
  10.0 2.3 %project.5 = (bf16[512,1024]{1,0:T(8,128)(2,1)S(1)}, bf16[512,512]{1,0:T(8,128)(2,1)S(1)}, bf16[512,512]{1,0:T(8,128)(2,1)S(1)}, bf16[512,1024]{1,0:T(8,128)(2,1)}, bf16[512,512]{1,0:T(8,128)(2,1)}) custom-call(bf16[512,1024]{1,0:T(8,128)(2,1)S(1)} %bitcast.13, bf16[1024,2048]{1,0:T(8,128)(2,1)S(1)} %copy-done), custom_call_target="tpu_custom_call" | custom-call | flops 4294967296 | bytes 2097152 | tf_op jit(solution)/shard_map/project/pallas_call | solution.py:37
  12.3 1.3 %collective-permute-start = (bf16[512,512]{1,0:T(8,128)(2,1)}, bf16[512,512]{1,0:T(8,128)(2,1)}, u32[]{:S(2)}, u32[]{:S(2)}) collective-permute-start(bf16[512,512]{1,0:T(8,128)(2,1)} %get-tuple-element.63), channel_id=1, source_target_pairs={{1,0},{2,1},{3,2},{5,4},{6,5},{7,6},{9,8},{10,9},{11,10},{13,12},{... | collective-permute-start | bytes 1572872 | tf_op jit(solution)/shard_map/ppermute | solution.py:26
  13.5 1.3 %collective-permute-start.4 = (bf16[512,1024]{1,0:T(8,128)(2,1)}, bf16[512,1024]{1,0:T(8,128)(2,1)S(1)}, u32[]{:S(2)}, u32[]{:S(2)}) collective-permute-start(bf16[512,1024]{1,0:T(8,128)(2,1)} %get-tuple-element.84), channel_id=1, source_target_pairs={{1,0},{2,1},{3,2},{5,4},{6,5},{7,6},{9,8},{10,9},{11,10},{13,12},{... | collective-permute-start | bytes 3145736 | tf_op jit(solution)/shard_map/ppermute | solution.py:26
  14.9 0.9 project.6
  16.6 1.7 %project.7 = (bf16[512,1024]{1,0:T(8,128)(2,1)S(1)}, bf16[512,512]{1,0:T(8,128)(2,1)S(1)}, bf16[512,512]{1,0:T(8,128)(2,1)S(1)}) custom-call(bf16[512,1024]{1,0:T(8,128)(2,1)S(1)} %get-tuple-element.65.refs_0_.refs_1_.refs_5_.refs_3_, bf16[1024,2048]{1,0:T(8,128)(2,1)S(1)} %copy-done.1, bf16[1024,2048]{1,0:T(8,128)(2,1)S(1)} %copy-done.1, ...), custom_call_target="tpu_custom_call" | custom-call | flops 8589934592 | bytes 3145728 | tf_op jit(solution)/shard_map/project/pallas_call | solution.py:37
  20.0 1.0 copy-done.23
  21.0 1.3 %copy.11.refs_3_ = s32[2048,1]{1,0:T(8,128)} copy(s32[2048,1]{0,1:T(1,128)S(1)} %bitcast.16) | data formatting | bytes 16384 | tf_op jit(solution)/shard_map/reshape;squeeze | solution.py:564
  22.4 1.2 %copy-done.7 = bf16[512,1024]{1,0:T(8,128)(2,1)S(1)} copy-done((bf16[512,1024]{1,0:T(8,128)(2,1)S(1)}, bf16[512,1024]{1,0:T(8,128)(2,1)}, u32[]{:S(2)}) %copy-start.7) | copy-done | bytes 1048600
  23.6 1.0 copy-done.21
  26.2 2.2 %forward.4 = (f32[512,512]{1,0:T(8,128)S(1)}, bf16[512,512]{1,0:T(8,128)(2,1)S(1)}) custom-call(s32[2]{0:T(128)S(1)} %pad_add_fusion.refs_0_, s32[1,2048]{1,0:T(1,128)S(1)} %copy-done.13, s32[1,2048]{1,0:T(1,128)S(1)} %copy-done.13, s32[2048,1]{1,0:T(8,128)S(1)} %copy-done.6, bf16[512,512]{1,0:T(8,128)(2,1)S(1)} %copy-done.17, ...), custom_call_target="tpu_custom_call" | custom-call | flops 4294967296 | bytes 2621440 | tf_op jit(solution)/shard_map/forward/pallas_call | solution.py:37
  28.4 3.3 %project.8 = (bf16[512,1024]{1,0:T(8,128)(2,1)S(1)}, bf16[512,1024]{1,0:T(8,128)(2,1)S(1)}, bf16[512,512]{1,0:T(8,128)(2,1)S(1)}, bf16[512,512]{1,0:T(8,128)(2,1)S(1)}) custom-call(bf16[512,1024]{1,0:T(8,128)(2,1)} %collective-permute-done.1.refs_0_, bf16[1024,2048]{1,0:T(8,128)(2,1)S(1)} %copy-done.2, bf16[1024,2048]{1,0:T(8,128)(2,1)S(1)} %copy-done.2, ...), custom_call_target="tpu_custom_call" | custom-call | flops 8589934592 | bytes 3145728 | tf_op jit(solution)/shard_map/project/pallas_call | solution.py:37
  31.8 1.2 forward.5.refs_7_
  33.0 5.2 %collective-permute-start.3 = (bf16[256,512]{1,0:T(8,128)(2,1)S(1)}, bf16[256,512]{1,0:T(8,128)(2,1)S(1)}, u32[]{:S(2)}, u32[]{:S(2)}) collective-permute-start(bf16[256,512]{1,0:T(8,128)(2,1)S(1)} %forward.5.refs_7_), channel_id=1, source_target_pairs={{0,1},{1,2},{2,3},{4,5},{5,6},{6,7},{8,9},{9,10},{10,11},{12,13},{... | collective-permute-start | bytes 786440 | tf_op jit(solution)/shard_map/ppermute | solution.py:26
  38.1 1.2 forward.6.refs_8_
  39.3 4.0 %collective-permute-start.2 = (bf16[256,512]{1,0:T(8,128)(2,1)S(1)}, bf16[256,512]{1,0:T(8,128)(2,1)S(1)}, u32[]{:S(2)}, u32[]{:S(2)}) collective-permute-start(bf16[256,512]{1,0:T(8,128)(2,1)S(1)} %forward.6.refs_8_), channel_id=1, source_target_pairs={{0,1},{1,2},{2,3},{4,5},{5,6},{6,7},{8,9},{9,10},{10,11},{12,13},{... | collective-permute-start | bytes 786440 | tf_op jit(solution)/shard_map/ppermute | solution.py:26
  44.7 1.3 %collective-permute-start.5 = (bf16[256,512]{1,0:T(8,128)(2,1)S(1)}, bf16[256,512]{1,0:T(8,128)(2,1)S(1)}, u32[]{:S(2)}, u32[]{:S(2)}) collective-permute-start(bf16[256,512]{1,0:T(8,128)(2,1)S(1)} %get-tuple-element.74.refs_8_.refs_5_), channel_id=1, source_target_pairs={{1,0},{2,1},{3,2},{5,4},{6,5},{7,6},{9,8},{10,9},{11,10},{13,12},{... | collective-permute-start | bytes 786440 | tf_op jit(solution)/shard_map/ppermute | solution.py:26
  46.0 1.0 backward.4
  47.1 1.7 %collective-permute-done.2.refs_0_ = bf16[256,512]{1,0:T(8,128)(2,1)S(1)} collective-permute-done((bf16[256,512]{1,0:T(8,128)(2,1)S(1)}, bf16[256,512]{1,0:T(8,128)(2,1)S(1)}, u32[]{:S(2)}, u32[]{:S(2)}) %collective-permute-start.2) | collective-permute-done | bytes 262176 | tf_op jit(solution)/shard_map/ppermute | solution.py:26
  49.2 1.3 %collective-permute-start.6 = (bf16[256,512]{1,0:T(8,128)(2,1)S(1)}, bf16[256,512]{1,0:T(8,128)(2,1)S(1)}, u32[]{:S(2)}, u32[]{:S(2)}) collective-permute-start(bf16[256,512]{1,0:T(8,128)(2,1)S(1)} %get-tuple-element.91), channel_id=1, source_target_pairs={{1,0},{2,1},{3,2},{5,4},{6,5},{7,6},{9,8},{10,9},{11,10},{13,12},{... | collective-permute-start | bytes 786440 | tf_op jit(solution)/shard_map/ppermute | solution.py:26
  50.5 1.1 collective-permute-done.4.refs_11_.refs_0_.refs_7_
  51.7 3.3 %backward.5 = (f32[512,512]{1,0:T(8,128)S(1)}, bf16[512,1024]{1,0:T(8,128)(2,1)S(1)}) custom-call(s32[2]{0:T(128)S(1)} %pad_add_fusion.refs_0_, s32[1,2048]{1,0:T(1,128)S(1)} %copy-done.13, s32[1,2048]{1,0:T(1,128)S(1)} %copy-done.13, s32[2048,1]{1,0:T(8,128)S(1)} %copy-done.6, bf16[512,512]{1,0:T(8,128)(2,1)S(1)} %copy-done.17, ...), custom_call_target="tpu_custom_call" | custom-call | flops 10737418240 | bytes 5242880 | tf_op jit(solution)/shard_map/backward/pallas_call | solution.py:37
  55.0 1.2 backward.6
  56.2 1.7 %project.9 = (bf16[512,512]{1,0:T(8,128)(2,1)S(1)}, bf16[512,512]{1,0:T(8,128)(2,1)}) custom-call(bf16[512,1024]{1,0:T(8,128)(2,1)S(1)} %collective-permute-done.4.refs_11_.refs_0_.refs_7_, bf16[1024,2048]{1,0:T(8,128)(2,1)S(1)} %copy-done.2, bf16[512,512]{1,0:T(8,128)(2,1)S(1)} %get-tuple-element.89.refs_2_.refs_6_), custom_call_target="tpu_custom_call" | custom-call | flops 4294967296 | bytes 2097152 | tf_op jit(solution)/shard_map/project/pallas_call | solution.py:37
  57.9 3.5 %collective-permute-done.6.refs_9_ = bf16[256,512]{1,0:T(8,128)(2,1)S(1)} collective-permute-done((bf16[256,512]{1,0:T(8,128)(2,1)S(1)}, bf16[256,512]{1,0:T(8,128)(2,1)S(1)}, u32[]{:S(2)}, u32[]{:S(2)}) %collective-permute-start.6) | collective-permute-done | bytes 262176 | tf_op jit(solution)/shard_map/ppermute | solution.py:26
  61.4 1.7 %backward.7 = (bf16[512,512]{1,0:T(8,128)(2,1)S(1)}, bf16[512,1024]{1,0:T(8,128)(2,1)S(1)}) custom-call(s32[2]{0:T(128)S(1)} %pad_add_fusion.refs_0_, s32[1,2048]{1,0:T(1,128)S(1)} %copy-done.13, s32[1,2048]{1,0:T(1,128)S(1)} %copy-done.13, s32[2048,1]{1,0:T(8,128)S(1)} %copy-done.6, bf16[512,512]{1,0:T(8,128)(2,1)} %collective-permute-done.refs_4_, ...), custom_call_target="tpu_custom_call" | custom-call | flops 10737418240 | bytes 5242880 | tf_op jit(solution)/shard_map/backward/pallas_call | solution.py:37
  63.1 2.4 %weights.4.refs_3_ = bf16[4,128,1536]{2,1,0:T(8,128)(2,1)S(1)} custom-call(s32[2]{0:T(128)S(1)} %pad_add_fusion.refs_0_, bf16[512,1024]{1,0:T(8,128)(2,1)S(1)} %get-tuple-element.65.refs_0_.refs_1_.refs_5_.refs_3_, bf16[512,1024]{1,0:T(8,128)(2,1)S(1)} %get-tuple-element.85.refs_2_.refs_1_, bf16[512,1024]{1,0:T(8,128)(2,1)S(1)} %get-tuple-element.90.refs_3_, ...), custom_call_target="tpu_custom_call" | custom-call | flops 1610612736 | bytes 1572864 | tf_op jit(solution)/shard_map/weights/pallas_call | solution.py:37
  65.6 1.3 %far.1.refs_9_ = bf16[512,1024]{1,0:T(8,128)(2,1)S(1)} custom-call(bf16[512,1024]{1,0:T(8,128)(2,1)S(1)} %get-tuple-element.95.refs_4_.refs_0_, bf16[1024,2048]{1,0:T(8,128)(2,1)S(1)} %copy-done.2, bf16[1024,2048]{1,0:T(8,128)(2,1)S(1)} %copy-done.2, bf16[4,128,1536]{2,1,0:T(8,128)(2,1)S(1)} %weights.4.refs_3_), custom_call_target="tpu_custom_call" | custom-call | flops 1073741824 | tf_op jit(solution)/shard_map/far/pallas_call | solution.py:37
  66.9 2.4 %weights.5.refs_0_ = bf16[4,128,1536]{2,1,0:T(8,128)(2,1)S(1)} custom-call(s32[2]{0:T(128)S(1)} %pad_add_fusion.refs_0_, bf16[512,1024]{1,0:T(8,128)(2,1)S(1)} %get-tuple-element.65.refs_0_.refs_1_.refs_5_.refs_3_, bf16[512,1024]{1,0:T(8,128)(2,1)S(1)} %get-tuple-element.85.refs_2_.refs_1_, bf16[512,1024]{1,0:T(8,128)(2,1)S(1)} %get-tuple-element.90.refs_3_, ...), custom_call_target="tpu_custom_call" | custom-call | flops 1610612736 | bytes 1572864 | tf_op jit(solution)/shard_map/weights/pallas_call | solution.py:37
  69.7 1.3 %weights.6.refs_5_ = bf16[4,128,1024]{2,1,0:T(8,128)(2,1)S(1)} custom-call(s32[2]{0:T(128)S(1)} %pad_add_fusion.refs_0_, bf16[512,1024]{1,0:T(8,128)(2,1)S(1)} %bitcast.9, bf16[512,512]{1,0:T(8,128)(2,1)S(1)} %get-tuple-element.79.refs_2_.refs_0_, bf16[512,1024]{1,0:T(8,128)(2,1)S(1)} %get-tuple-element.65.refs_0_.refs_1_.refs_5_.refs_3_, ...), custom_call_target="tpu_custom_call" | custom-call | flops 536870912 | bytes 1048576 | tf_op jit(solution)/shard_map/weights/pallas_call | solution.py:37
  71.6 1.5 %collective-permute-start.11 = (bf16[2,128,1536]{2,1,0:T(8,128)(2,1)S(1)}, bf16[2,128,1536]{2,1,0:T(8,128)(2,1)S(1)}, u32[]{:S(2)}, u32[]{:S(2)}) collective-permute-start(bf16[2,128,1536]{2,1,0:T(8,128)(2,1)S(1)} %get-tuple-element.97.refs_5_), channel_id=1, source_target_pairs={{0,8},{4,20},{8,0},{12,28},{16,24},{20,4},{24,16},{28,12},{1,9},{5... | collective-permute-start | bytes 2359304 | tf_op jit(solution)/shard_map/ppermute | solution.py:487
  73.0 1.3 %collective-permute-start.14 = (bf16[512,1024]{1,0:T(8,128)(2,1)S(1)}, bf16[512,1024]{1,0:T(8,128)(2,1)S(1)}, u32[]{:S(2)}, u32[]{:S(2)}) collective-permute-start(bf16[512,1024]{1,0:T(8,128)(2,1)S(1)} %far.1.refs_9_), channel_id=1, source_target_pairs={{1,0},{2,1},{3,2},{5,4},{6,5},{7,6},{9,8},{10,9},{11,10},{13,12},{... | collective-permute-start | bytes 3145736 | tf_op jit(solution)/shard_map/ppermute | solution.py:26
  74.3 4.8 %collective-permute-start.9 = (bf16[512,512]{1,0:T(8,128)(2,1)S(1)}, bf16[512,512]{1,0:T(8,128)(2,1)S(1)}, u32[]{:S(2)}, u32[]{:S(2)}) collective-permute-start(bf16[512,512]{1,0:T(8,128)(2,1)S(1)} %get-tuple-element.96.refs_8_), channel_id=1, source_target_pairs={{0,1},{1,2},{2,3},{4,5},{5,6},{6,7},{8,9},{9,10},{10,11},{12,13},{... | collective-permute-start | bytes 1572872 | tf_op jit(solution)/shard_map/ppermute | solution.py:26
  79.2 1.3 %weights.7.refs_0_ = bf16[4,128,1024]{2,1,0:T(8,128)(2,1)S(1)} custom-call(s32[2]{0:T(128)S(1)} %pad_add_fusion.refs_0_, bf16[512,1024]{1,0:T(8,128)(2,1)S(1)} %bitcast.10, bf16[512,512]{1,0:T(8,128)(2,1)S(1)} %get-tuple-element.79.refs_2_.refs_0_, bf16[512,1024]{1,0:T(8,128)(2,1)S(1)} %get-tuple-element.65.refs_0_.refs_1_.refs_5_.refs_3_, ...), custom_call_target="tpu_custom_call" | custom-call | flops 536870912 | bytes 1048576 | tf_op jit(solution)/shard_map/weights/pallas_call | solution.py:37
  81.4 2.4 %near.1.refs_3_.refs_0_ = f32[512,1024]{1,0:T(8,128)S(1)} custom-call(bf16[512,512]{1,0:T(8,128)(2,1)S(1)} %get-tuple-element.80.refs_4_.refs_0_, bf16[512,1024]{1,0:T(8,128)(2,1)S(1)} %get-tuple-element.85.refs_2_.refs_1_, bf16[512,512]{1,0:T(8,128)(2,1)S(1)} %get-tuple-element.89.refs_2_.refs_6_, bf16[1024,2048]{1,0:T(8,128)(2,1)S(1)} %copy-done.2, ...), custom_call_target="tpu_custom_call" | custom-call | flops 2147483648 | tf_op jit(solution)/shard_map/near/pallas_call | solution.py:37
  83.8 1.7 %output.1 = (bf16[512,1024]{1,0:T(8,128)(2,1)}, f32[8,128]{1,0:T(8,128)S(1)}) custom-call(bf16[512,512]{1,0:T(8,128)(2,1)S(1)} %get-tuple-element.79.refs_2_.refs_0_, bf16[512,1024]{1,0:T(8,128)(2,1)S(1)} %copy-done.8, bf16[512,1024]{1,0:T(8,128)(2,1)S(1)} %bitcast.14, f32[512,1024]{1,0:T(8,128)S(1)} %near.1.refs_3_.refs_0_), custom_call_target="tpu_custom_call" | custom-call | flops 536870912 | tf_op jit(solution)/shard_map/output/pallas_call | solution.py:37
  85.7 1.6 %collective-permute-start.13 = (bf16[1,128,1536]{2,1,0:T(8,128)(2,1)S(1)}, bf16[1,128,1536]{2,1,0:T(8,128)(2,1)S(1)}, u32[]{:S(2)}, u32[]{:S(2)}) collective-permute-start(bf16[1,128,1536]{2,1,0:T(8,128)(2,1)S(1)} %get-tuple-element.103.refs_2_), channel_id=1, source_target_pairs={{0,16},{4,12},{8,24},{12,4},{16,0},{20,28},{24,8},{28,20},{1,17},{... | collective-permute-start | bytes 1179656 | tf_op jit(solution)/shard_map/ppermute | solution.py:487
  87.2 2.5 %collective-permute-done.9.refs_3_ = bf16[512,512]{1,0:T(8,128)(2,1)S(1)} collective-permute-done((bf16[512,512]{1,0:T(8,128)(2,1)S(1)}, bf16[512,512]{1,0:T(8,128)(2,1)S(1)}, u32[]{:S(2)}, u32[]{:S(2)}) %collective-permute-start.9) | collective-permute-done | bytes 524320 | tf_op jit(solution)/shard_map/ppermute | solution.py:26
  89.8 2.9 %collective-permute-done.10.refs_1_ = bf16[2,128,1024]{2,1,0:T(8,128)(2,1)S(1)} collective-permute-done((bf16[2,128,1024]{2,1,0:T(8,128)(2,1)S(1)}, bf16[2,128,1024]{2,1,0:T(8,128)(2,1)S(1)}, u32[]{:S(2)}, u32[]{:S(2)}) %collective-permute-start.10) | collective-permute-done | bytes 524320 | tf_op jit(solution)/shard_map/ppermute | solution.py:487
  92.8 1.6 %collective-permute-start.12 = (bf16[1,128,1024]{2,1,0:T(8,128)(2,1)S(1)}, bf16[1,128,1024]{2,1,0:T(8,128)(2,1)S(1)}, u32[]{:S(2)}, u32[]{:S(2)}) collective-permute-start(bf16[1,128,1024]{2,1,0:T(8,128)(2,1)S(1)} %get-tuple-element.105.refs_3_), channel_id=1, source_target_pairs={{0,16},{4,12},{8,24},{12,4},{16,0},{20,28},{24,8},{28,20},{1,17},{... | collective-permute-start | bytes 786440 | tf_op jit(solution)/shard_map/ppermute | solution.py:487
  95.1 5.0 %collective-permute-start.17 = (bf16[64,1536]{1,0:T(8,128)(2,1)S(1)}, bf16[64,1536]{1,0:T(8,128)(2,1)S(1)}, u32[]{:S(2)}, u32[]{:S(2)}) collective-permute-start(bf16[64,1536]{1,0:T(8,128)(2,1)S(1)} %get-tuple-element.117), channel_id=1, source_target_pairs={{0,1},{1,0},{2,3},{3,2},{4,5},{5,4},{6,7},{7,6},{8,9},{9,8},{10,11... | collective-permute-start | bytes 589832 | tf_op jit(solution)/shard_map/ppermute | solution.py:510
  100.7 3.6 %collective-permute-start.15 = (bf16[64,1024]{1,0:T(8,128)(2,1)S(1)}, bf16[64,1024]{1,0:T(8,128)(2,1)S(1)}, u32[]{:S(2)}, u32[]{:S(2)}) collective-permute-start(bf16[64,1024]{1,0:T(8,128)(2,1)S(1)} %get-tuple-element.113), channel_id=1, source_target_pairs={{0,1},{1,0},{2,3},{3,2},{4,5},{5,4},{6,7},{7,6},{8,9},{9,8},{10,11... | collective-permute-start | bytes 393224 | tf_op jit(solution)/shard_map/ppermute | solution.py:510
  104.4 2.3 %mid.1 = (f32[512,1024]{1,0:T(8,128)S(1)}, bf16[512,1024]{1,0:T(8,128)(2,1)S(1)}, f32[512,128]{1,0:T(8,128)S(1)}) custom-call(f32[512,1024]{1,0:T(8,128)S(1)} %near.1.refs_3_.refs_0_, bf16[512,1024]{1,0:T(8,128)(2,1)S(1)} %bitcast.15, bf16[512,1024]{1,0:T(8,128)(2,1)S(1)} %bitcast.11, bf16[512,512]{1,0:T(8,128)(2,1)S(1)} %collective-permute-done.9.refs_3_, ...), custom_call_target="tpu_custom_call" | custom-call | tf_op jit(solution)/shard_map/mid/pallas_call | solution.py:37
  106.7 1.9 %tokens.1 = (bf16[512,1024]{1,0:T(8,128)(2,1)}, f32[8,128]{1,0:T(8,128)S(1)}) custom-call(f32[512,1024]{1,0:T(8,128)S(1)} %get-tuple-element.109.refs_0_, bf16[512,1024]{1,0:T(8,128)(2,1)S(1)} %get-tuple-element.110.refs_1_, f32[512,128]{1,0:T(8,128)S(1)} %get-tuple-element.111.refs_2_, bf16[512,1024]{1,0:T(8,128)(2,1)S(1)} %collective-permute-done.14.refs_3_, ...), custom_call_target="tpu_custom_call" | custom-call | tf_op jit(solution)/shard_map/tokens/pallas_call | solution.py:37
  108.6 3.3 %collective-permute-start.18 = (bf16[32,1536]{1,0:T(8,128)(2,1)S(1)}, bf16[32,1536]{1,0:T(8,128)(2,1)S(1)}, u32[]{:S(2)}, u32[]{:S(2)}) collective-permute-start(bf16[32,1536]{1,0:T(8,128)(2,1)S(1)} %get-tuple-element.119), channel_id=1, source_target_pairs={{0,2},{1,3},{2,0},{3,1},{4,6},{5,7},{6,4},{7,5},{8,10},{9,11},{10,... | collective-permute-start | bytes 294920 | tf_op jit(solution)/shard_map/ppermute | solution.py:510
  112.1 5.8 %collective-permute-done.16.refs_1_ = bf16[32,1024]{1,0:T(8,128)(2,1)S(1)} collective-permute-done((bf16[32,1024]{1,0:T(8,128)(2,1)S(1)}, bf16[32,1024]{1,0:T(8,128)(2,1)S(1)}, u32[]{:S(2)}, u32[]{:S(2)}) %collective-permute-start.16) | collective-permute-done | bytes 65568 | tf_op jit(solution)/shard_map/ppermute | solution.py:510
  (76 shorter events, 10.3 us)
Async XLA Ops:
  0.6 27.8 %collective-permute-start.1 = (bf16[512,1024]{1,0:T(8,128)(2,1)}, bf16[512,1024]{1,0:T(8,128)(2,1)}, u32[]{:S(2)}, u32[]{:S(2)}) collective-permute-start(bf16[512,1024]{1,0:T(8,128)(2,1)} %bitcast.12), channel_id=1, source_target_pairs={{0,1},{1,2},{2,3},{4,5},{5,6},{6,7},{8,9},{9,10},{10,11},{12,13},{... | collective-permute-start | bytes 3145736 | tf_op jit(solution)/shard_map/ppermute | solution.py:26
  6.6 2.2 %copy-start = (bf16[1024,2048]{1,0:T(8,128)(2,1)S(1)}, bf16[1024,2048]{1,0:T(8,128)(2,1)}, u32[]{:S(2)}) copy-start(bf16[1024,2048]{1,0:T(8,128)(2,1)} %refs_4_.3) | copy-start | bytes 12582916
  8.8 1.2 %copy-start.4 = (bf16[1,512,1024]{2,1,0:T(8,128)(2,1)S(1)}, bf16[1,512,1024]{2,1,0:T(8,128)(2,1)}, u32[]{:S(2)}) copy-start(bf16[1,512,1024]{2,1,0:T(8,128)(2,1)} %param.5) | copy-start | bytes 3145732
  10.0 4.9 %copy-start.1 = (bf16[1024,2048]{1,0:T(8,128)(2,1)S(1)}, bf16[1024,2048]{1,0:T(8,128)(2,1)}, u32[]{:S(2)}) copy-start(bf16[1024,2048]{1,0:T(8,128)(2,1)} %refs_4_.3) | copy-start | bytes 12582916
  12.3 3.5 %copy-start.14 = (bf16[512,512]{1,0:T(8,128)(2,1)}, bf16[512,512]{1,0:T(8,128)(2,1)S(1)}, u32[]{:S(2)}) copy-start(bf16[512,512]{1,0:T(8,128)(2,1)S(1)} %get-tuple-element.88.refs_11_) | copy-start | bytes 1572868
  12.3 3.6 %copy-start.16 = (bf16[512,512]{1,0:T(8,128)(2,1)}, bf16[512,512]{1,0:T(8,128)(2,1)S(1)}, u32[]{:S(2)}) copy-start(bf16[512,512]{1,0:T(8,128)(2,1)S(1)} %get-tuple-element.64.refs_4_) | copy-start | bytes 1572868
  12.3 19.5 %collective-permute-start = (bf16[512,512]{1,0:T(8,128)(2,1)}, bf16[512,512]{1,0:T(8,128)(2,1)}, u32[]{:S(2)}, u32[]{:S(2)}) collective-permute-start(bf16[512,512]{1,0:T(8,128)(2,1)} %get-tuple-element.63), channel_id=1, source_target_pairs={{1,0},{2,1},{3,2},{5,4},{6,5},{7,6},{9,8},{10,9},{11,10},{13,12},{... | collective-permute-start | bytes 1572872 | tf_op jit(solution)/shard_map/ppermute | solution.py:26
  13.5 38.1 %collective-permute-start.4 = (bf16[512,1024]{1,0:T(8,128)(2,1)}, bf16[512,1024]{1,0:T(8,128)(2,1)S(1)}, u32[]{:S(2)}, u32[]{:S(2)}) collective-permute-start(bf16[512,1024]{1,0:T(8,128)(2,1)} %get-tuple-element.84), channel_id=1, source_target_pairs={{1,0},{2,1},{3,2},{5,4},{6,5},{7,6},{9,8},{10,9},{11,10},{13,12},{... | collective-permute-start | bytes 3145736 | tf_op jit(solution)/shard_map/ppermute | solution.py:26
  15.8 0.8 copy-start.9
  16.6 1.8 %copy-start.11 = (bf16[512,512]{1,0:T(8,128)(2,1)}, bf16[512,512]{1,0:T(8,128)(2,1)S(1)}, u32[]{:S(2)}) copy-start(bf16[512,512]{1,0:T(8,128)(2,1)S(1)} %get-tuple-element.66.refs_3_) | copy-start | bytes 1572868
  16.6 4.4 %copy-start.13 = (s32[1,2048]{1,0:T(1,128)S(1)}, s32[1,2048]{1,0:T(1,128)}, u32[]{:S(2)}) copy-start(s32[1,2048]{1,0:T(1,128)} %refs_2_.20) | copy-start | bytes 24580
  16.6 5.8 %copy-start.3 = (bf16[1,512,1024]{2,1,0:T(8,128)(2,1)S(1)}, bf16[1,512,1024]{2,1,0:T(8,128)(2,1)}, u32[]{:S(2)}) copy-start(bf16[1,512,1024]{2,1,0:T(8,128)(2,1)} %param.9) | copy-start | bytes 3145732
  18.4 0.8 copy-start.18
  19.2 0.8 copy-start.20
  20.0 1.0 copy-start.23
  22.4 1.2 %copy-start.7 = (bf16[512,1024]{1,0:T(8,128)(2,1)S(1)}, bf16[512,1024]{1,0:T(8,128)(2,1)}, u32[]{:S(2)}) copy-start(bf16[512,1024]{1,0:T(8,128)(2,1)} %refs_1_.31) | copy-start | bytes 3145732
  23.6 1.0 copy-start.21
  24.7 1.2 %copy-start.6 = (s32[2048,1]{1,0:T(8,128)S(1)}, s32[2048,1]{1,0:T(8,128)}, u32[]{:S(2)}) copy-start(s32[2048,1]{1,0:T(8,128)} %copy.11.refs_3_) | copy-start | bytes 24580
  24.7 1.4 %copy-start.17 = (bf16[512,512]{1,0:T(8,128)(2,1)S(1)}, bf16[512,512]{1,0:T(8,128)(2,1)}, u32[]{:S(2)}) copy-start(bf16[512,512]{1,0:T(8,128)(2,1)} %copy-done.16) | copy-start | bytes 1572868
  24.7 1.5 %copy-start.19 = (bf16[512,512]{1,0:T(8,128)(2,1)S(1)}, bf16[512,512]{1,0:T(8,128)(2,1)}, u32[]{:S(2)}) copy-start(bf16[512,512]{1,0:T(8,128)(2,1)} %copy-done.18) | copy-start | bytes 1572868
  26.2 2.2 %copy-start.2 = (bf16[1024,2048]{1,0:T(8,128)(2,1)S(1)}, bf16[1024,2048]{1,0:T(8,128)(2,1)}, u32[]{:S(2)}) copy-start(bf16[1024,2048]{1,0:T(8,128)(2,1)} %refs_4_.3) | copy-start | bytes 12582916
  33.0 11.3 %collective-permute-start.3 = (bf16[256,512]{1,0:T(8,128)(2,1)S(1)}, bf16[256,512]{1,0:T(8,128)(2,1)S(1)}, u32[]{:S(2)}, u32[]{:S(2)}) collective-permute-start(bf16[256,512]{1,0:T(8,128)(2,1)S(1)} %forward.5.refs_7_), channel_id=1, source_target_pairs={{0,1},{1,2},{2,3},{4,5},{5,6},{6,7},{8,9},{9,10},{10,11},{12,13},{... | collective-permute-start | bytes 786440 | tf_op jit(solution)/shard_map/ppermute | solution.py:26
  39.3 5.0 %copy-start.10 = (bf16[512,512]{1,0:T(8,128)(2,1)S(1)}, bf16[512,512]{1,0:T(8,128)(2,1)}, u32[]{:S(2)}) copy-start(bf16[512,512]{1,0:T(8,128)(2,1)} %copy-done.9) | copy-start | bytes 1572868
  39.3 5.0 %copy-start.12 = (bf16[512,512]{1,0:T(8,128)(2,1)S(1)}, bf16[512,512]{1,0:T(8,128)(2,1)}, u32[]{:S(2)}) copy-start(bf16[512,512]{1,0:T(8,128)(2,1)} %copy-done.11) | copy-start | bytes 1572868
  39.3 9.4 %collective-permute-start.2 = (bf16[256,512]{1,0:T(8,128)(2,1)S(1)}, bf16[256,512]{1,0:T(8,128)(2,1)S(1)}, u32[]{:S(2)}, u32[]{:S(2)}) collective-permute-start(bf16[256,512]{1,0:T(8,128)(2,1)S(1)} %forward.6.refs_8_), channel_id=1, source_target_pairs={{0,1},{1,2},{2,3},{4,5},{5,6},{6,7},{8,9},{9,10},{10,11},{12,13},{... | collective-permute-start | bytes 786440 | tf_op jit(solution)/shard_map/ppermute | solution.py:26
  44.7 16.7 %collective-permute-start.5 = (bf16[256,512]{1,0:T(8,128)(2,1)S(1)}, bf16[256,512]{1,0:T(8,128)(2,1)S(1)}, u32[]{:S(2)}, u32[]{:S(2)}) collective-permute-start(bf16[256,512]{1,0:T(8,128)(2,1)S(1)} %get-tuple-element.74.refs_8_.refs_5_), channel_id=1, source_target_pairs={{1,0},{2,1},{3,2},{5,4},{6,5},{7,6},{9,8},{10,9},{11,10},{13,12},{... | collective-permute-start | bytes 786440 | tf_op jit(solution)/shard_map/ppermute | solution.py:26
  48.7 2.9 %copy-start.22 = (bf16[512,512]{1,0:T(8,128)(2,1)S(1)}, bf16[512,512]{1,0:T(8,128)(2,1)}, u32[]{:S(2)}) copy-start(bf16[512,512]{1,0:T(8,128)(2,1)} %copy-done.20) | copy-start | bytes 1572868
  48.7 2.9 %copy-start.24 = (bf16[512,1024]{1,0:T(8,128)(2,1)S(1)}, bf16[512,1024]{1,0:T(8,128)(2,1)}, u32[]{:S(2)}) copy-start(bf16[512,1024]{1,0:T(8,128)(2,1)} %copy-done.23) | copy-start | bytes 3145732
  49.2 12.2 %collective-permute-start.6 = (bf16[256,512]{1,0:T(8,128)(2,1)S(1)}, bf16[256,512]{1,0:T(8,128)(2,1)S(1)}, u32[]{:S(2)}, u32[]{:S(2)}) collective-permute-start(bf16[256,512]{1,0:T(8,128)(2,1)S(1)} %get-tuple-element.91), channel_id=1, source_target_pairs={{1,0},{2,1},{3,2},{5,4},{6,5},{7,6},{9,8},{10,9},{11,10},{13,12},{... | collective-permute-start | bytes 786440 | tf_op jit(solution)/shard_map/ppermute | solution.py:26
  51.7 3.3 %copy-start.15 = (bf16[512,512]{1,0:T(8,128)(2,1)S(1)}, bf16[512,512]{1,0:T(8,128)(2,1)}, u32[]{:S(2)}) copy-start(bf16[512,512]{1,0:T(8,128)(2,1)} %copy-done.14) | copy-start | bytes 1572868
  65.5 3.8 %collective-permute-start.7 = (bf16[4,128,1536]{2,1,0:T(8,128)(2,1)S(1)}, bf16[4,128,1536]{2,1,0:T(8,128)(2,1)S(1)}, u32[]{:S(2)}, u32[]{:S(2)}) collective-permute-start(bf16[4,128,1536]{2,1,0:T(8,128)(2,1)S(1)} %weights.4.refs_3_), channel_id=1, source_target_pairs={{0,4},{4,0},{8,12},{12,8},{16,20},{20,16},{24,28},{28,24},{1,5},{5... | collective-permute-start | bytes 4718600 | tf_op jit(solution)/shard_map/ppermute | solution.py:487
  71.0 9.5 %collective-permute-start.8 = (bf16[4,128,1024]{2,1,0:T(8,128)(2,1)S(1)}, bf16[4,128,1024]{2,1,0:T(8,128)(2,1)S(1)}, u32[]{:S(2)}, u32[]{:S(2)}) collective-permute-start(bf16[4,128,1024]{2,1,0:T(8,128)(2,1)S(1)} %weights.6.refs_5_), channel_id=1, source_target_pairs={{0,4},{4,0},{8,12},{12,8},{16,20},{20,16},{24,28},{28,24},{1,5},{5... | collective-permute-start | bytes 3145736 | tf_op jit(solution)/shard_map/ppermute | solution.py:487
  71.6 13.9 %collective-permute-start.11 = (bf16[2,128,1536]{2,1,0:T(8,128)(2,1)S(1)}, bf16[2,128,1536]{2,1,0:T(8,128)(2,1)S(1)}, u32[]{:S(2)}, u32[]{:S(2)}) collective-permute-start(bf16[2,128,1536]{2,1,0:T(8,128)(2,1)S(1)} %get-tuple-element.97.refs_5_), channel_id=1, source_target_pairs={{0,8},{4,20},{8,0},{12,28},{16,24},{20,4},{24,16},{28,12},{1,9},{5... | collective-permute-start | bytes 2359304 | tf_op jit(solution)/shard_map/ppermute | solution.py:487
  73.0 33.6 %collective-permute-start.14 = (bf16[512,1024]{1,0:T(8,128)(2,1)S(1)}, bf16[512,1024]{1,0:T(8,128)(2,1)S(1)}, u32[]{:S(2)}, u32[]{:S(2)}) collective-permute-start(bf16[512,1024]{1,0:T(8,128)(2,1)S(1)} %far.1.refs_9_), channel_id=1, source_target_pairs={{1,0},{2,1},{3,2},{5,4},{6,5},{7,6},{9,8},{10,9},{11,10},{13,12},{... | collective-permute-start | bytes 3145736 | tf_op jit(solution)/shard_map/ppermute | solution.py:26
  74.3 15.4 %collective-permute-start.9 = (bf16[512,512]{1,0:T(8,128)(2,1)S(1)}, bf16[512,512]{1,0:T(8,128)(2,1)S(1)}, u32[]{:S(2)}, u32[]{:S(2)}) collective-permute-start(bf16[512,512]{1,0:T(8,128)(2,1)S(1)} %get-tuple-element.96.refs_8_), channel_id=1, source_target_pairs={{0,1},{1,2},{2,3},{4,5},{5,6},{6,7},{8,9},{9,10},{10,11},{12,13},{... | collective-permute-start | bytes 1572872 | tf_op jit(solution)/shard_map/ppermute | solution.py:26
  80.8 3.0 %copy-start.5 = (bf16[1,512,1024]{2,1,0:T(8,128)(2,1)S(1)}, bf16[1,512,1024]{2,1,0:T(8,128)(2,1)}, u32[]{:S(2)}) copy-start(bf16[1,512,1024]{2,1,0:T(8,128)(2,1)} %param.5) | copy-start | bytes 3145732
  80.8 3.0 %copy-start.8 = (bf16[512,1024]{1,0:T(8,128)(2,1)S(1)}, bf16[512,1024]{1,0:T(8,128)(2,1)}, u32[]{:S(2)}) copy-start(bf16[512,1024]{1,0:T(8,128)(2,1)} %refs_1_.31) | copy-start | bytes 3145732
  80.8 11.9 %collective-permute-start.10 = (bf16[2,128,1024]{2,1,0:T(8,128)(2,1)S(1)}, bf16[2,128,1024]{2,1,0:T(8,128)(2,1)S(1)}, u32[]{:S(2)}, u32[]{:S(2)}) collective-permute-start(bf16[2,128,1024]{2,1,0:T(8,128)(2,1)S(1)} %get-tuple-element.98.refs_7_), channel_id=1, source_target_pairs={{0,8},{4,20},{8,0},{12,28},{16,24},{20,4},{24,16},{28,12},{1,9},{5... | collective-permute-start | bytes 1572872 | tf_op jit(solution)/shard_map/ppermute | solution.py:487
  85.7 8.7 %collective-permute-start.13 = (bf16[1,128,1536]{2,1,0:T(8,128)(2,1)S(1)}, bf16[1,128,1536]{2,1,0:T(8,128)(2,1)S(1)}, u32[]{:S(2)}, u32[]{:S(2)}) collective-permute-start(bf16[1,128,1536]{2,1,0:T(8,128)(2,1)S(1)} %get-tuple-element.103.refs_2_), channel_id=1, source_target_pairs={{0,16},{4,12},{8,24},{12,4},{16,0},{20,28},{24,8},{28,20},{1,17},{... | collective-permute-start | bytes 1179656 | tf_op jit(solution)/shard_map/ppermute | solution.py:487
  92.8 7.3 %collective-permute-start.12 = (bf16[1,128,1024]{2,1,0:T(8,128)(2,1)S(1)}, bf16[1,128,1024]{2,1,0:T(8,128)(2,1)S(1)}, u32[]{:S(2)}, u32[]{:S(2)}) collective-permute-start(bf16[1,128,1024]{2,1,0:T(8,128)(2,1)S(1)} %get-tuple-element.105.refs_3_), channel_id=1, source_target_pairs={{0,16},{4,12},{8,24},{12,4},{16,0},{20,28},{24,8},{28,20},{1,17},{... | collective-permute-start | bytes 786440 | tf_op jit(solution)/shard_map/ppermute | solution.py:487
  95.1 13.5 %collective-permute-start.17 = (bf16[64,1536]{1,0:T(8,128)(2,1)S(1)}, bf16[64,1536]{1,0:T(8,128)(2,1)S(1)}, u32[]{:S(2)}, u32[]{:S(2)}) collective-permute-start(bf16[64,1536]{1,0:T(8,128)(2,1)S(1)} %get-tuple-element.117), channel_id=1, source_target_pairs={{0,1},{1,0},{2,3},{3,2},{4,5},{5,4},{6,7},{7,6},{8,9},{9,8},{10,11... | collective-permute-start | bytes 589832 | tf_op jit(solution)/shard_map/ppermute | solution.py:510
  100.7 7.8 %collective-permute-start.15 = (bf16[64,1024]{1,0:T(8,128)(2,1)S(1)}, bf16[64,1024]{1,0:T(8,128)(2,1)S(1)}, u32[]{:S(2)}, u32[]{:S(2)}) collective-permute-start(bf16[64,1024]{1,0:T(8,128)(2,1)S(1)} %get-tuple-element.113), channel_id=1, source_target_pairs={{0,1},{1,0},{2,3},{3,2},{4,5},{5,4},{6,7},{7,6},{8,9},{9,8},{10,11... | collective-permute-start | bytes 393224 | tf_op jit(solution)/shard_map/ppermute | solution.py:510
  108.6 9.2 %collective-permute-start.18 = (bf16[32,1536]{1,0:T(8,128)(2,1)S(1)}, bf16[32,1536]{1,0:T(8,128)(2,1)S(1)}, u32[]{:S(2)}, u32[]{:S(2)}) collective-permute-start(bf16[32,1536]{1,0:T(8,128)(2,1)S(1)} %get-tuple-element.119), channel_id=1, source_target_pairs={{0,2},{1,3},{2,0},{3,1},{4,6},{5,7},{6,4},{7,5},{8,10},{9,11},{10,... | collective-permute-start | bytes 294920 | tf_op jit(solution)/shard_map/ppermute | solution.py:510
  112.0 5.9 %collective-permute-start.16 = (bf16[32,1024]{1,0:T(8,128)(2,1)S(1)}, bf16[32,1024]{1,0:T(8,128)(2,1)S(1)}, u32[]{:S(2)}, u32[]{:S(2)}) collective-permute-start(bf16[32,1024]{1,0:T(8,128)(2,1)S(1)} %get-tuple-element.116), channel_id=1, source_target_pairs={{0,2},{1,3},{2,0},{3,1},{4,6},{5,7},{6,4},{7,5},{8,10},{9,11},{10,... | collective-permute-start | bytes 196616 | tf_op jit(solution)/shard_map/ppermute | solution.py:510
